TPU v7x, 32 devices: a whole 2x2x4 slice. The times are simulated.
32 devices in a mesh: ka: 2 (over y), pb: 4 (over z), row: 4 (over x, core).
Axes of the slice: x: 2, y: 2, z: 4, core: 2. Of those that a mesh axis runs over, the one named last changes fastest.
Arguments:
- coupling: bfloat16 [16, 64, 20736], P('pb', ('ka', 'row')), may hold values from -1 to 1
- rotation: bfloat16 [16, 36, 36], P('pb'), may hold values from -1 to 1
- freq: float32 [16, 36], P('pb'), may hold values from 0.02 to 0.3
- eigvec: bfloat16 [256, 24, 24], P(('ka', 'row')), may hold values from -1.25 to 1.25
- energies: float32 [256, 24], P(('ka', 'row')), may hold values from -1.5 to 1.5
- window: int32 [256], P(('ka', 'row')), may hold values from 12 to 24
- kq_index: int32 [16, 256], P('pb'), may hold values from 0 to 255, as said below
- kpoints: float32 [256, 3], replicated, may hold values from 0 to 1
- lattice: int32 [64, 3], replicated, may hold values from -3 to 3
Outputs:
- electron: float32 [256, 24], P(('ka', 'row'))
- phonon: float32 [16, 36], P('pb')
Inputs may be any that keep to these rules, and one draw needn't show every extreme that they name: The k-points form a shifted grid of 256 points, (256 // 64) x 8 x 8, listed in an order drawn from the seed; each q-point is a vector of that grid without the shift. kq_index[q, k] is the index of the k-point equal to kpoints[k] plus the q-point's vector modulo 1, so each row of kq_index is a permutation of 0 to 255.
All inputs are finite; a program needn't handle non-finite values.
Results may differ from a plain program's by a relative error of at most 0.00089.
Values may be sent and summed in bfloat16 or wider, within the bound.
No kernel may reach another device: no remote copies, remote signals or barrier semaphores. Data moves between devices by JAX's collectives and lax.ppermute only.
A program may use at most 128 MiB of HBM per device.

v0:
```python
import math

import jax
import jax.numpy as jnp
from jax import lax
from jax.sharding import PartitionSpec as P

SIGMA = 0.1
THERMAL_ENERGY_KT = 0.2


def phase_table(lattice, kpoint_rows):
    rvec = lattice.astype(jnp.float32)
    argument = (
        rvec[:, 0:1] * kpoint_rows[:, 0][None, :]
        + rvec[:, 1:2] * kpoint_rows[:, 1][None, :]
        + rvec[:, 2:3] * kpoint_rows[:, 2][None, :]
    )
    return jnp.cos(2.0 * math.pi * argument).astype(jnp.bfloat16)


def block_terms(
    coup_rows, phase_cols, rot_rows, freq_rows, eig_k, eig_kq, level_k, level_kq, lim_k, lim_kq
):
    q_block = coup_rows.shape[0]
    k_block = phase_cols.shape[1]
    columns = q_block * k_block
    n_modes = rot_rows.shape[1]
    n_bands = eig_k.shape[0]
    norm = 1.0 / (math.sqrt(2.0 * math.pi) * SIGMA)
    bloch = jnp.einsum(
        "qrf,rk->fqk", coup_rows, phase_cols, preferred_element_type=jnp.float32
    ).astype(jnp.bfloat16)
    bloch = bloch.reshape(n_modes, n_bands, n_bands, columns)
    rot_cols = jnp.repeat(jnp.transpose(rot_rows, (1, 2, 0)), k_block, axis=2)
    modal = jnp.einsum(
        "amnc,abc->bmnc", bloch, rot_cols, preferred_element_type=jnp.float32
    ).astype(jnp.bfloat16)
    eig_k_cols = jnp.tile(eig_k, (1, 1, q_block))
    right = jnp.einsum(
        "bmjc,jnc->bmnc", modal, eig_k_cols, preferred_element_type=jnp.float32
    ).astype(jnp.bfloat16)
    coupled = jnp.einsum("imc,binc->bmnc", eig_kq, right, preferred_element_type=jnp.float32)
    level_k_cols = jnp.tile(level_k, (1, q_block))
    lim_k_cols = jnp.tile(lim_k, (q_block,))
    freq_cols = jnp.repeat(freq_rows.T, k_block, axis=1)
    diff = level_kq[None, :, None, :] - level_k_cols[None, None, :, :] - freq_cols[:, None, None, :]
    delta = jnp.exp(-(diff * diff) / (2.0 * SIGMA * SIGMA)) * norm
    bands = jnp.arange(n_bands).astype(jnp.float32)
    mask_m = (bands[:, None] < lim_kq[None, :]).astype(jnp.float32)
    mask_n = (bands[:, None] < lim_k_cols[None, :]).astype(jnp.float32)
    strength = coupled * coupled * delta * mask_m[None, :, None, :] * mask_n[None, None, :, :]
    filling_initial = jax.nn.sigmoid(-level_k_cols / THERMAL_ENERGY_KT)
    filling_final = jax.nn.sigmoid(-level_kq / THERMAL_ENERGY_KT)
    elec = jnp.sum(strength, axis=(0, 1)).reshape(n_bands, q_block, k_block).sum(axis=1)
    phon = jnp.sum(
        strength * (filling_initial[None, None, :, :] - filling_final[None, :, None, :]),
        axis=(1, 2),
    )
    phon = phon.reshape(n_modes, q_block, k_block).sum(axis=2)
    return (elec, phon)


def on_device(coupling, rotation, freq, eigvec, energies, window, kq_index, kpoints, lattice):
    n_ka = lax.axis_size("ka")
    n_row = lax.axis_size("row")
    n_pb = lax.axis_size("pb")
    k_dev = eigvec.shape[0]
    q_dev = rotation.shape[0]
    n_bands = eigvec.shape[1]
    n_modes = rotation.shape[1]
    total_k = k_dev * n_ka * n_row
    total_q = q_dev * n_pb
    eigen_grid = lax.all_gather(eigvec, ("ka", "row"), axis=0, tiled=True)
    level_all, limit_all = (
        lax.all_gather(energies, ("ka", "row"), axis=0, tiled=True),
        lax.all_gather(window.astype(jnp.float32), ("ka", "row"), axis=0, tiled=True),
    )
    eig_cols = jnp.transpose(eigen_grid, (1, 2, 0))
    level_cols = level_all.T
    ka_pos = lax.axis_index("ka")
    row_pos = lax.axis_index("row")
    coup_part = lax.all_to_all(coupling, "row", split_axis=0, concat_axis=1, tiled=True)
    coup_full = lax.all_gather(coup_part, "ka", axis=1, tiled=True)
    q_count = q_dev // n_row
    q_start = row_pos * q_count
    k_count = k_dev * n_row
    k_start = ka_pos * k_count
    rot_mine = lax.dynamic_slice_in_dim(rotation, q_start, q_count, 0)
    freq_mine = lax.dynamic_slice_in_dim(freq, q_start, q_count, 0)
    kq_mine = lax.dynamic_slice(kq_index, (q_start, k_start), (q_count, k_count))
    kp_mine = lax.dynamic_slice(kpoints, (k_start, jnp.int32(0)), (k_count, 3))
    eig_mine = lax.dynamic_slice_in_dim(eig_cols, k_start, k_count, 2)
    lev_mine = lax.dynamic_slice_in_dim(level_cols, k_start, k_count, 1)
    lim_mine = lax.dynamic_slice_in_dim(limit_all, k_start, k_count, 0)
    phase_all = phase_table(lattice, kp_mine)
    k_block = min(k_count, 128)
    elec_cols = [None] * (k_count // k_block)
    index = kq_mine.reshape(-1)
    eig_kq = jnp.take(eig_cols, index, axis=2)
    level_kq = jnp.take(level_cols, index, axis=1)
    lim_kq = jnp.take(limit_all, index, axis=0)
    elec, phon = block_terms(
        coup_full,
        phase_all,
        rot_mine,
        freq_mine,
        eig_mine,
        eig_kq,
        lev_mine,
        level_kq,
        lim_mine,
        lim_kq,
    )
    elec_cols[0] = elec
    elec_local = elec_cols[0].T * (1.0 / (total_q * n_modes * n_bands))
    phon_local = phon.T * (1.0 / (total_k * n_bands))
    elec_mine = lax.psum_scatter(elec_local, "row", scatter_dimension=0, tiled=True)
    phon_part = lax.psum(phon_local, "ka")
    phonon = lax.all_gather(phon_part, "row", axis=0, tiled=True)
    electron = lax.psum(elec_mine, "pb")
    return (electron, phonon)


def solution(mesh):
    return jax.shard_map(
        on_device,
        mesh=mesh,
        in_specs=(
            P("pb", ("ka", "row"), None),
            P("pb", None, None),
            P("pb", None),
            P(("ka", "row"), None, None),
            P(("ka", "row"), None),
            P(("ka", "row")),
            P("pb", None),
            P(),
            P(),
        ),
        out_specs=(P(("ka", "row"), None), P("pb", None)),
        check_vma=False,
    )
```

profile of v0, /device:TPU:0, one launch (start us, length us, event | category | flops | bytes accessed | tf_op | source)
XLA Modules:
  0.0 252.0 jit_solution(9701617613651377182)
XLA Ops:
  7.2 4.2 %all-to-all-start = ((bf16[4,8,20736]{2,1,0:T(8,128)(2,1)}), bf16[4,8,20736]{2,1,0:T(8,128)(2,1)S(1)}, u32[]{:S(2)}, u32[]{:S(2)}) async-start(bf16[4,8,20736]{2,1,0:T(8,128)(2,1)} %param.9), calls=%async_computation | async-start | bytes 2654208 | tf_op jit(solution)/shard_map/all_to_all | solution.py:83
  11.4 1.2 dynamic-slice.8
  13.3 15.6 %all-to-all-done = bf16[4,8,20736]{2,1,0:T(8,128)(2,1)S(1)} async-done(((bf16[4,8,20736]{2,1,0:T(8,128)(2,1)}), bf16[4,8,20736]{2,1,0:T(8,128)(2,1)S(1)}, u32[]{:S(2)}, u32[]{:S(2)}) %all-to-all-start) | async-done | bytes 1327136 | tf_op jit(solution)/shard_map/all_to_all | solution.py:83
  28.9 1.1 copy-done.1
  30.0 0.8 convert_dynamic-update-slice_fusion
  31.4 13.5 %all-reduce = f32[256]{0:T(256)S(1)} all-reduce(f32[256]{0:T(256)S(1)} %convert_dynamic-update-slice_fusion), channel_id=1, replica_groups=mesh['ka'=2,'pb'=4,'row'=4] {'ka','row'}, use_global_device_ids=true, to_apply=%add | all-reduce | flops 256 | bytes 2048
  45.1 0.8 compare_and_fusion
  45.8 1.3 gather_fusion.2
  47.5 8.5 %all-gather = f32[8,32,24]{1,2,0:T(8,128)S(1)} all-gather(f32[1,32,24]{1,2,0:T(8,128)} %bitcast.103), channel_id=1, replica_groups=mesh['ka'=2,'pb'=4,'row'=4] {'ka','row'}, dimensions={0}, use_global_device_ids=true | all-gather | bytes 27648 | tf_op jit(solution)/shard_map/all_gather | solution.py:76
  57.3 1.1 copy.27
  58.4 19.6 %all_gather.15 = bf16[256,24,24]{2,1,0:T(8,128)(2,1)S(1)} all-gather(bf16[32,24,24]{2,1,0:T(8,128)(2,1)S(1)} %copy.27), channel_id=1, replica_groups=mesh['ka'=2,'pb'=4,'row'=4] {'ka','row'}, dimensions={0}, use_global_device_ids=true | all-gather | bytes 331776 | tf_op jit(solution)/shard_map/all_gather | solution.py:74
  78.0 1.6 gather_fusion
  80.0 0.7 fusion.30
  81.4 1.9 broadcast_subtract_fusion
  83.2 5.8 %fusion.2 = bf16[20736,1,128]{0,2,1:T(8,128)(2,1)} fusion(bf16[1,64,20736]{2,1,0:T(8,128)(2,1)} %all-gather.4.cloned.1.call-done, f32[128]{0:T(128)S(1)} %get-tuple-element.14, f32[64]{0:T(128)S(1)} %get-tuple-element.11, f32[128]{0:T(128)S(1)} %get-tuple-element.15, f32[64]{0:T(128)S(1)} %get-tuple-element.12, f32[128]{0:T(128)S(1)} %get-tuple-element.13, ...), kind=kOutput, calls=%fused_computation.8 | convolution fusion | flops 342450176 | bytes 7964928 | tf_op jit(solution)/shard_map/qrf,rk->fqk/dot_general | solution.py:31
  89.1 8.0 %copy.30 = bf16[20736,1,128]{2,0,1:T(8,128)(2,1)} copy(bf16[20736,1,128]{0,2,1:T(8,128)(2,1)} %fusion.2) | data formatting | bytes 10616832 | tf_op jit(solution)/shard_map/convert_element_type | solution.py:33
  97.1 29.6 %copy.31 = bf16[36,24,24,128]{0,2,1,3:T(8,128)(2,1)} copy(bf16[36,24,24,128]{3,2,1,0:T(8,128)(2,1)} %bitcast.98) | data formatting | bytes 10616832 | tf_op jit(solution)/shard_map/reshape | solution.py:34
  126.7 17.8 %convert_bitcast_fusion = bf16[36,24,24,128]{0,2,1,3:T(8,128)(2,1)} fusion(bf16[36,24,24,128]{0,2,1,3:T(8,128)(2,1)} %copy.31, bf16[128,24,24]{1,2,0:T(8,128)(2,1)S(1)} %copy.51, bf16[36,36]{1,0:T(8,128)(2,1)S(1)} %bitcast.102), kind=kOutput, calls=%fused_computation.13 | convolution fusion | flops 323813376 | bytes 10766880 | tf_op jit(solution)/shard_map/bmjc,jnc->bmnc/dot_general | solution.py:40
  144.5 59.8 %multiply_reduce_fusion = (f32[36]{0:T(128)S(1)}, f32[24,128]{0,1:T(8,128)S(1)}) fusion(f32[24,24,128]{0,1,2:T(8,128)S(1)} %get-tuple-element.18, f32[24,128]{0,1:T(8,128)S(1)} %copy.40, f32[24,128]{0,1:T(8,128)S(1)} %copy.39, f32[36]{0:T(128)S(1)} %fusion.30, f32[24,24,128]{0,1,2:T(8,128)} %get-tuple-element.19, bf16[128,24,24]{2,1,0:T(8,128)(2,1)} %gather_fusion, ...), kind=kOutput, calls=%fused_computation.6 | convolution fusion | flops 159323104 | bytes 6082976 | tf_op jit(solution)/shard_map/imc,binc->bmnc/dot_general | solution.py:43
  204.9 4.9 %psum.15 = f32[1,36]{1,0:T(1,128)S(1)} all-reduce(f32[1,36]{1,0:T(1,128)S(1)} %multiply_bitcast_fusion.1), channel_id=1, replica_groups=mesh['ka'=2,'pb'=4,'row'=4] {'ka'}, use_global_device_ids=true, to_apply=%region_4.5 | all-reduce | flops 36 | bytes 288 | tf_op jit(solution)/shard_map/psum | solution.py:119
  209.9 5.0 %all-gather.1 = f32[4,1,36]{2,1,0:T(1,128)S(1)} all-gather(f32[1,1,36]{2,1,0:T(1,128)S(1)} %bitcast.105), channel_id=1, replica_groups=mesh['ka'=2,'pb'=4,'row'=4] {'row'}, dimensions={0}, use_global_device_ids=true | all-gather | bytes 720 | tf_op jit(solution)/shard_map/all_gather | solution.py:120
  214.9 9.6 %reduce-scatter.4.cloned.1.call-done = f32[32,24]{1,0:T(8,128)} async-done(((f32[128,24]{1,0:T(8,128)}), f32[32,24]{1,0:T(8,128)}) %reduce-scatter.4.cloned.1.call-update) | async-done | bytes 3088
  224.5 0.8 copy.50
  225.3 19.3 %psum.14 = f32[32,24]{0,1:T(8,128)} all-reduce(f32[32,24]{0,1:T(8,128)S(1)} %copy.50), channel_id=1, replica_groups=mesh['ka'=2,'pb'=4,'row'=4] {'pb'}, use_global_device_ids=true, to_apply=%region_2.3 | all-reduce | flops 768 | bytes 6144 | tf_op jit(solution)/shard_map/psum | solution.py:121
  (39 shorter events, 4.9 us)
Async XLA Ops:
  7.2 40.0 %copy-start = (bf16[4,36,36]{2,0,1:T(4,128)(2,1)S(1)}, bf16[4,36,36]{2,0,1:T(4,128)(2,1)}, u32[]{:S(2)}) copy-start(bf16[4,36,36]{2,0,1:T(4,128)(2,1)} %param.10) | copy-start | bytes 31108
  7.2 21.7 %all-to-all-start = ((bf16[4,8,20736]{2,1,0:T(8,128)(2,1)}), bf16[4,8,20736]{2,1,0:T(8,128)(2,1)S(1)}, u32[]{:S(2)}, u32[]{:S(2)}) async-start(bf16[4,8,20736]{2,1,0:T(8,128)(2,1)} %param.9), calls=%async_computation | async-start | bytes 2654208 | tf_op jit(solution)/shard_map/all_to_all | solution.py:83
  11.4 71.8 %all-gather.4.cloned.1.call-start = ((), (), s32[]{:S(2)}) async-start(), calls=%async_computation.2 | async-start | bytes 3981312 | tf_op jit(solution)/shard_map/all_gather | solution.py:84
  28.8 1.1 copy-start.1
  29.9 194.6 %reduce-scatter.4.cloned.1.call-start = ((), (), s32[]{:S(2)}) async-start(), calls=%async_computation.3 | async-start | bytes 81920
Sparse Core Ops, SparseCore 0:
  30.1 46.4 all-gather.3
  205.0 19.4 reduce-scatter.3
where the time goes:
time: 253 us; the launch traced here: 252 us
  matrix products  83.4 us (33%)
  blocking collectives  70.8 us (28%)
  local copies, waits for them, and re-layouts  48.6 us (19%)
  waiting for transfers between devices  25.2 us (10%)
  between operations  14.8 us (6%)
  other arithmetic  4.82 us (2%)
  starting transfers between devices  4.26 us (2%)
    dot_general x1, matrix products, block_terms(): jnp.einsum('imc,binc->bmnc', eig_kq, right, preferred_element_type=jnp.fl...  59.8 us
    reshape x1, local copies, waits for them, and re-layouts, block_terms(): bloch = bloch.reshape(n_modes, n_bands, n_bands, columns)  29.6 us
    all_gather x1, blocking collectives, on_device(): eigen_grid = lax.all_gather(eigvec, ('ka', 'row'), axis=0, tiled=True)  19.6 us
    psum x1, blocking collectives, on_device(): electron = lax.psum(elec_mine, 'pb')  19.3 us
    dot_general x1, matrix products, block_terms(): jnp.einsum('bmjc,jnc->bmnc', modal, eig_k_cols, preferred_element_type=jn...  17.8 us
    all_to_all x1, waiting for transfers between devices, on_device(): lax.all_to_all(coupling, 'row', split_axis=0, concat_axis=1, tiled=True)  15.6 us
    unnamed x1, blocking collectives  13.5 us
    unnamed x3, waiting for transfers between devices  9.64 us
  transfers between devices with their start and end apart: 3, of which 2 were waited for; matrix products, arithmetic and copies ran while one was open for 5% of the time, Pallas kernels for 0%

commit v1 on v0

v1 whole, which is shorter than its diff:
```python
import functools
import math

import jax
import jax.numpy as jnp
from jax import lax
from jax.experimental import pallas as pl
from jax.experimental.pallas import tpu as pltpu
from jax.sharding import PartitionSpec as P

SIGMA = 0.1
THERMAL_ENERGY_KT = 0.2
VMEM = pltpu.CompilerParams(vmem_limit_bytes=56 * 1024 * 1024)
F32 = jnp.float32
BF16 = jnp.bfloat16


def phase_table(lattice, kpoint_rows):
    rvec = lattice.astype(jnp.float32)
    argument = (
        rvec[:, 0:1] * kpoint_rows[:, 0][None, :]
        + rvec[:, 1:2] * kpoint_rows[:, 1][None, :]
        + rvec[:, 2:3] * kpoint_rows[:, 2][None, :]
    )
    return jnp.cos(2.0 * math.pi * argument).astype(jnp.bfloat16)


def iota(shape, dim):
    return lax.broadcasted_iota(jnp.int32, shape, dim)


def rotate_kernel(n_modes, n_bands, v_parts, coup_ref, rot_ref, out_ref):
    r = coup_ref.shape[1]
    pair = n_bands * n_bands
    rows = n_modes * r
    x = coup_ref[0].astype(F32)
    x = jnp.concatenate([x[:, c * pair : (c + 1) * pair] for c in range(n_modes)], axis=0).astype(BF16)
    rot = rot_ref[0]
    spread_v = (iota((rows, n_modes), 0) // r == iota((rows, n_modes), 1)).astype(BF16)
    spread_c = (iota((n_modes, rows), 1) // r == iota((n_modes, rows), 0)).astype(BF16)
    half = lax.dot_general(spread_v, rot, (((1,), (1,)), ((), ())), preferred_element_type=F32)
    full = jnp.dot(half.astype(BF16), spread_c, preferred_element_type=F32)
    same = iota((rows, rows), 0) % r == iota((rows, rows), 1) % r
    big = jnp.where(same, full, 0.0).astype(BF16)
    y = jnp.dot(big, x, preferred_element_type=F32)
    v_count = n_modes // v_parts
    for part in range(v_parts):
        for i in range(0, n_bands, 2):
            both = []
            for ii in (i, i + 1):
                both.append(
                    jnp.concatenate(
                        [
                            y[v * r : (v + 1) * r, ii * n_bands : (ii + 1) * n_bands]
                            for v in range(part * v_count, (part + 1) * v_count)
                        ],
                        axis=1,
                    )
                )
            out_ref[part, 0, i * r : (i + 2) * r, :] = jnp.concatenate(both, axis=0).astype(BF16)


def rotate(coupling, rotation, n_bands, v_parts):
    q, r, width = coupling.shape
    n_modes = rotation.shape[1]
    cols = n_modes // v_parts * n_bands
    return pl.pallas_call(
        functools.partial(rotate_kernel, n_modes, n_bands, v_parts),
        grid=(q,),
        in_specs=[
            pl.BlockSpec((1, r, width), lambda a: (a, 0, 0)),
            pl.BlockSpec((1, n_modes, n_modes), lambda a: (a, 0, 0)),
        ],
        out_specs=pl.BlockSpec((v_parts, 1, n_bands * r, cols), lambda a: (0, a, 0, 0)),
        out_shape=jax.ShapeDtypeStruct((v_parts, q, n_bands * r, cols), BF16),
        compiler_params=VMEM,
        name="rotate_modes",
    )(coupling, rotation)


def main_kernel(
    n_bands, n_v, r, group,
    freq_ref, a_ref, eig_ref, en_ref, lim_ref, idx_ref, phase_ref,
    el_out, ph_out,
    a_scr, v_scr, u_scr, ek_scr, ep_scr, lk_scr, lp_scr, w_scr, t_scr, el_scr, ph_scr,
):
    m = pl.program_id(0)
    n_src = a_ref.shape[0]
    depth = n_bands * r
    k_all = eig_ref.shape[0]
    k_loc = idx_ref.shape[1]
    high = lax.Precision.HIGHEST
    tn = (((0,), (0,)), ((), ()))

    @pl.when(m == 0)
    def _():
        for s in range(n_src):
            a_scr[:, s * depth : (s + 1) * depth] = a_ref[s].astype(F32).T.astype(BF16)
        at = iota((k_all, k_loc), 0)
        own = at == idx_ref[0:1, :]
        far = at == idx_ref[1:2, :]
        own_b, far_b = own.astype(BF16), far.astype(BF16)
        own_f, far_f = own.astype(F32), far.astype(F32)
        u_scr[...] = lax.dot_general(eig_ref[...], own_b, tn, preferred_element_type=F32).reshape(
            n_bands, n_bands, k_loc
        )
        v_scr[...] = lax.dot_general(eig_ref[...], far_b, tn, preferred_element_type=F32).reshape(
            n_bands, n_bands, k_loc
        )
        en = en_ref[...]
        ek_scr[...] = lax.dot_general(en, own_f, tn, precision=high, preferred_element_type=F32)
        ep_scr[...] = lax.dot_general(en, far_f, tn, precision=high, preferred_element_type=F32)
        lim = lim_ref[...]
        lk_scr[...] = jnp.dot(lim, own_f, precision=high, preferred_element_type=F32)
        lp_scr[...] = jnp.dot(lim, far_f, precision=high, preferred_element_type=F32)
        el_scr[...] = jnp.zeros_like(el_scr)
        ph_scr[...] = jnp.zeros_like(ph_scr)

    ph = phase_ref[...].astype(F32)
    for i in range(0, n_bands, 2):
        v0 = v_scr[i, pl.ds(m, 1), :]
        v1 = v_scr[i + 1, pl.ds(m, 1), :]
        for s in range(n_src):
            p = ph[s * r : (s + 1) * r, :]
            w_scr[s * depth + i * r : s * depth + (i + 2) * r, :] = jnp.concatenate(
                [p * v0, p * v1], axis=0
            ).astype(BF16)
    t_scr[...] = jnp.dot(a_scr[...], w_scr[...], preferred_element_type=F32)

    norm = 1.0 / (math.sqrt(2.0 * math.pi) * SIGMA)
    ep = ep_scr[pl.ds(m, 1), :]
    ek = ek_scr[...]
    base = ep - ek
    mask_m = jnp.where(m.astype(F32) < lp_scr[0:1, :], norm, 0.0)
    mask = jnp.where(iota((n_bands, k_loc), 0).astype(F32) < lk_scr[0:1, :], mask_m, 0.0)
    occ = jax.nn.sigmoid(-ek / THERMAL_ENERGY_KT) - jax.nn.sigmoid(-ep / THERMAL_ENERGY_KT)
    el = el_scr[...]
    for g in range(0, n_v, group):
        vs = range(g, min(g + group, n_v))
        acc = [None] * len(vs)
        for j in range(n_bands):
            u = u_scr[j]
            for x, v in enumerate(vs):
                term = t_scr[v * n_bands + j : v * n_bands + j + 1, :] * u
                acc[x] = term if acc[x] is None else acc[x] + term
        for x, v in enumerate(vs):
            diff = base - freq_ref[0, v]
            strength = acc[x] * acc[x] * jnp.exp(diff * diff * (-0.5 / (SIGMA * SIGMA))) * mask
            el = el + strength
            ph_scr[v] += strength * occ
    el_scr[...] = el

    @pl.when(m == pl.num_programs(0) - 1)
    def _():
        el_out[...] = el_scr[...]
        ph_out[...] = jnp.sum(jnp.sum(ph_scr[...], axis=1), axis=1, keepdims=True)


def linewidths(freq, a, eig, energies, limits, index, phase, n_bands, r):
    n_src, depth, cols = a.shape
    n_v = cols // n_bands
    k_loc = index.shape[1]
    total = n_src * depth
    whole = lambda *s: pl.BlockSpec(s, lambda m: (0,) * len(s))
    return pl.pallas_call(
        functools.partial(main_kernel, n_bands, n_v, r, 3),
        grid=(n_bands,),
        in_specs=[
            pl.BlockSpec(memory_space=pltpu.SMEM),
            whole(*a.shape),
            whole(*eig.shape),
            whole(*energies.shape),
            whole(*limits.shape),
            whole(*index.shape),
            whole(*phase.shape),
        ],
        out_specs=[whole(n_bands, k_loc), whole(n_v, 1)],
        out_shape=[
            jax.ShapeDtypeStruct((n_bands, k_loc), F32),
            jax.ShapeDtypeStruct((n_v, 1), F32),
        ],
        scratch_shapes=[
            pltpu.VMEM((cols, total), BF16),
            pltpu.VMEM((n_bands, n_bands, k_loc), F32),
            pltpu.VMEM((n_bands, n_bands, k_loc), F32),
            pltpu.VMEM((n_bands, k_loc), F32),
            pltpu.VMEM((n_bands, k_loc), F32),
            pltpu.VMEM((1, k_loc), F32),
            pltpu.VMEM((1, k_loc), F32),
            pltpu.VMEM((total, k_loc), BF16),
            pltpu.VMEM((cols, k_loc), F32),
            pltpu.VMEM((n_bands, k_loc), F32),
            pltpu.VMEM((n_v, n_bands, k_loc), F32),
        ],
        compiler_params=VMEM,
        name="linewidths",
    )(freq, a, eig, energies, limits, index, phase)


def on_device(coupling, rotation, freq, eigvec, energies, window, kq_index, kpoints, lattice):
    plane = ("ka", "row")
    everywhere = ("ka", "pb", "row")
    n_ka = lax.axis_size("ka")
    n_row = lax.axis_size("row")
    n_pb = lax.axis_size("pb")
    n_group = n_ka * n_row
    k_dev, n_bands = eigvec.shape[:2]
    q_dev, n_modes = rotation.shape[:2]
    assert q_dev == n_row
    total_k = k_dev * n_group
    total_q = q_dev * n_pb
    v_parts = math.gcd(n_modes, n_ka)
    k_parts = n_ka // v_parts
    v_count = n_modes // v_parts
    k_loc = total_k // k_parts
    ka_pos = lax.axis_index("ka")
    row_pos = lax.axis_index("row")
    pb_pos = lax.axis_index("pb")

    eig_all = lax.all_gather(eigvec.reshape(k_dev, n_bands * n_bands), plane, axis=0, tiled=True)
    level = jnp.concatenate([energies, window.astype(F32)[:, None]], axis=1)
    level_all = lax.all_gather(level, plane, axis=0, tiled=True)

    pad = -coupling.shape[1] % 8
    phase_lat = lattice
    if pad:
        coupling = jnp.pad(coupling, ((0, 0), (0, pad), (0, 0)))
    r = coupling.shape[1]
    rotated = rotate(coupling, rotation, n_bands, v_parts)
    if k_parts > 1:
        rotated = jnp.repeat(rotated, k_parts, axis=0)
    rotated = rotated.reshape((n_group,) + rotated.shape[2:])
    a = lax.all_to_all(rotated, plane, 0, 0, tiled=True)

    k_start = (ka_pos % k_parts) * k_loc
    kp = lax.dynamic_slice_in_dim(kpoints, k_start, k_loc, 0)
    phase = phase_table(phase_lat, kp)
    if pad:
        phase = jnp.pad(phase.reshape(n_group, r - pad, k_loc), ((0, 0), (0, pad), (0, 0)))
        phase = phase.reshape(n_group * r, k_loc)
    kq = lax.dynamic_slice(kq_index, (row_pos, k_start), (1, k_loc))
    index = jnp.concatenate([jnp.arange(k_loc, dtype=jnp.int32)[None] + k_start, kq], axis=0)
    v_start = (ka_pos // k_parts) * v_count
    freq_mine = lax.dynamic_slice(freq, (row_pos, v_start), (1, v_count))
    el, ph = linewidths(
        freq_mine, a, eig_all, level_all[:, :n_bands], level_all[:, n_bands:].T, index, phase,
        n_bands, r,
    )
    el = el * (1.0 / (total_q * n_modes * n_bands))
    ph = ph[:, 0] * (1.0 / (total_k * n_bands))
    if k_parts > 1:
        el = lax.dynamic_update_slice(jnp.zeros((n_bands, total_k), F32), el, (jnp.int32(0), k_start))
    per_row = 128 // k_dev
    fold = n_bands // per_row
    el = el.reshape(per_row, fold, n_group, k_dev).transpose(2, 1, 0, 3).reshape(n_group, fold, 128)
    ph_rows = 8 - fold % 8
    ph = jnp.pad(ph, (0, ph_rows * 128 - v_count)).reshape(1, ph_rows, 128)
    send = jnp.concatenate([el, jnp.broadcast_to(ph, (n_group, ph_rows, 128))], axis=1)
    send = send.reshape(n_ka, 1, n_row, fold + ph_rows, 128)
    send = jnp.broadcast_to(send, (n_ka, n_pb, n_row, fold + ph_rows, 128))
    send = send.reshape(n_group * n_pb, fold + ph_rows, 128)
    got = lax.all_to_all(send, everywhere, 0, 0, tiled=True)
    got = got.reshape(n_ka, n_pb, n_row, fold + ph_rows, 128)
    electron = jnp.sum(got[:, :, :, :fold], axis=(0, 1, 2))
    electron = electron.reshape(fold, per_row, k_dev).transpose(2, 1, 0).reshape(k_dev, n_bands)
    near = lax.dynamic_index_in_dim(got, pb_pos, 1, keepdims=False)[:, :, fold, :v_count]
    near = near.reshape(v_parts, k_parts, n_row, v_count).sum(axis=1)
    phonon = near.transpose(1, 0, 2).reshape(n_row, n_modes)
    return (electron, phonon)


def solution(mesh):
    return jax.shard_map(
        on_device,
        mesh=mesh,
        in_specs=(
            P("pb", ("ka", "row"), None),
            P("pb", None, None),
            P("pb", None),
            P(("ka", "row"), None, None),
            P(("ka", "row"), None),
            P(("ka", "row")),
            P("pb", None),
            P(),
            P(),
        ),
        out_specs=(P(("ka", "row"), None), P("pb", None)),
        check_vma=False,
    )
```

time: 253 us -> 104 us (0.41)
  matrix products: 83.4 us -> 0 us
  local copies, waits for them, and re-layouts: 48.6 us -> 7.26 us
  Pallas kernels: 0 us -> 41.1 us
  blocking collectives: 70.8 us -> 32.2 us
  waiting for transfers between devices: 25.2 us -> 8.23 us
  between operations: 14.8 us -> 0.75 us
  starting transfers between devices: 4.26 us -> 10.2 us
    dot_general x3 -> x0, matrix products: 83.4 us -> none  [the longest x1 59.8 us: block_terms(): jnp.einsum('imc,binc->bmnc', eig_kq, right, preferred_element_type=jnp.fl...]
    pallas_call x0 -> x2, Pallas kernels: none -> 41.1 us  [the longest x1 35 us: linewidths(): pl.pallas_call(functools.partial(main_kernel, n_bands, n_v, r, 3), grid=(...]
    reshape x1 -> x6, local copies, waits for them, and re-layouts: 29.6 us -> 1.6 us  [the longest x2 0.69 us: on_device(): electron.reshape(fold, per_row, k_dev).transpose(2, 1, 0)]
    psum x2 -> x0, blocking collectives: 24.2 us -> none  [the longest x1 19.3 us: on_device(): electron = lax.psum(elec_mine, 'pb')]
    unnamed x1 -> x0, blocking collectives: 13.5 us -> none
    unnamed x3 -> x0, waiting for transfers between devices: 9.64 us -> none
    convert_element_type x3 -> x0, local copies, waits for them, and re-layouts: 8.2 us -> none  [the longest x1 8 us: block_terms(): bloch = jnp.einsum('qrf,rk->fqk', coup_rows, phase_cols, preferred_elemen...]
    all_to_all x1 -> x2, waiting for transfers between devices: 15.6 us -> 8.23 us  [the longest x1 8.22 us: on_device(): got = lax.all_to_all(send, everywhere, 0, 0, tiled=True)]
  transfers between devices with their start and end apart: 3 -> 2, of which waited for: 2 -> 1; matrix products, arithmetic and copies ran while one was open for 5% -> 4% of each run, Pallas kernels for 0% -> 0%
where the time goes in v1:
time: 104 us; the launch traced here: 103 us
  Pallas kernels  41.1 us (40%)
  blocking collectives  32.2 us (31%)
  starting transfers between devices  10.2 us (10%)
  waiting for transfers between devices  8.23 us (8%)
  local copies, waits for them, and re-layouts  7.26 us (7%)
  other arithmetic  3.21 us (3%)
    pallas_call x1, Pallas kernels, linewidths(): pl.pallas_call(functools.partial(main_kernel, n_bands, n_v, r, 3), grid=(...  35 us
    all_gather x1, blocking collectives, on_device(): level_all = lax.all_gather(level, plane, axis=0, tiled=True)  22.7 us
    all_gather x1, blocking collectives, on_device(): lax.all_gather(eigvec.reshape(k_dev, n_bands * n_bands), plane, axis=0, t...  9.51 us
    all_to_all x1, waiting for transfers between devices, on_device(): got = lax.all_to_all(send, everywhere, 0, 0, tiled=True)  8.22 us
    pallas_call x1, Pallas kernels, rotate(): pl.pallas_call(functools.partial(rotate_kernel, n_modes, n_bands, v_parts...  6.07 us
    all_to_all x1, starting transfers between devices, on_device(): a = lax.all_to_all(rotated, plane, 0, 0, tiled=True)  5.32 us
    all_to_all x1, starting transfers between devices, on_device(): got = lax.all_to_all(send, everywhere, 0, 0, tiled=True)  4.89 us
    unnamed x18, local copies, waits for them, and re-layouts  2.65 us
  transfers between devices with their start and end apart: 2, of which 1 were waited for; matrix products, arithmetic and copies ran while one was open for 4% of the time, Pallas kernels for 0%

profile of v1, /device:TPU:0, one launch (start us, length us, event | category | flops | bytes accessed | tf_op | source)
XLA Modules:
  0.0 103.0 jit_solution(7583465149256199187)
XLA Ops:
  0.6 1.4 %copy.29.rot_ref = bf16[4,36,36]{2,1,0:T(8,128)(2,1)} copy(bf16[4,36,36]{2,0,1:T(4,128)(2,1)} %param.10) | data formatting | bytes 20736 | tf_op args[1]
  2.0 6.1 %rotate_modes.1 = bf16[2,4,192,432]{3,2,1,0:T(8,128)(2,1)} custom-call(bf16[4,8,20736]{2,1,0:T(8,128)(2,1)} %coup_ref.1, bf16[4,36,36]{2,1,0:T(8,128)(2,1)} %copy.29.rot_ref), custom_call_target="tpu_custom_call" | custom-call | tf_op jit(solution)/shard_map/rotate_modes/pallas_call | solution.py:67
  8.1 5.3 %all-to-all-start = ((bf16[8,192,432]{2,1,0:T(8,128)(2,1)}), bf16[8,192,432]{2,1,0:T(8,128)(2,1)S(1)}, u32[]{:S(2)}, u32[]{:S(2)}) async-start(bf16[8,192,432]{2,1,0:T(8,128)(2,1)} %bitcast.34), calls=%async_computation | async-start | bytes 3145728 | tf_op jit(solution)/shard_map/all_to_all | solution.py:233
  13.5 0.1 copy.37
  13.6 0.1 copy.32
  13.8 1.3 %dynamic_slice.12.freq_ref = f32[1,18]{1,0:T(1,128)} dynamic-slice(f32[4,36]{1,0:T(4,128)} %param.11, s32[]{:T(128)S(6)} %select_n.20, s32[]{:T(128)S(6)} %select_n.21), dynamic_slice_sizes={1,18} | dynamic-slice | bytes 148 | tf_op jit(solution)/shard_map/dynamic_slice | solution.py:244
  15.1 0.1 pad_maximum_fusion
  15.2 22.7 %all_gather.7 = f32[256,25]{1,0:T(8,128)S(1)} all-gather(f32[32,25]{1,0:T(8,128)S(1)} %pad_maximum_fusion), channel_id=1, replica_groups=mesh['ka'=2,'pb'=4,'row'=4] {'ka','row'}, dimensions={0}, use_global_device_ids=true | all-gather | bytes 28800 | tf_op jit(solution)/shard_map/all_gather | solution.py:222
  37.9 9.5 %all_gather.6.eig_ref = bf16[256,576]{1,0:T(8,128)(2,1)} all-gather(bf16[32,576]{1,0:T(8,128)(2,1)S(1)} %copy.37), channel_id=1, replica_groups=mesh['ka'=2,'pb'=4,'row'=4] {'ka','row'}, dimensions={0}, use_global_device_ids=true | all-gather | bytes 331776 | tf_op jit(solution)/shard_map/all_gather | solution.py:220
  47.5 0.6 pad_add_fusion.idx_ref
  48.0 0.8 slice_reduce_fusion.1
  48.8 0.9 cosine_convert_fusion.phase_ref
  49.8 1.1 %copy-done.1 = bf16[8,192,432]{2,1,0:T(8,128)(2,1)} copy-done((bf16[8,192,432]{2,1,0:T(8,128)(2,1)}, bf16[8,192,432]{2,1,0:T(8,128)(2,1)S(1)}, u32[]{:S(2)}) %copy-start.1) | copy-done | bytes 1327128
  50.9 35.0 %linewidths.1 = (f32[24,256]{1,0:T(8,128)}, f32[18,1]{1,0:T(8,128)}) custom-call(f32[1,18]{1,0:T(1,128)} %dynamic_slice.12.freq_ref, bf16[8,192,432]{2,1,0:T(8,128)(2,1)} %copy-done.1, bf16[256,576]{1,0:T(8,128)(2,1)} %all_gather.6.eig_ref, f32[256,24]{1,0:T(8,128)} %bitcast.35, f32[1,256]{1,0:T(1,128)} %bitcast.42, s32[2,256]{1,0:T(2,128)} %pad_add_fusion.idx_ref, ...), custom_call_target="tpu_custom_call" | custom-call | tf_op jit(solution)/shard_map/linewidths/pallas_call | solution.py:165
  85.9 0.8 multiply_reduce_fusion
  86.7 0.7 broadcast_multiply_fusion
  87.5 0.1 reshape.46
  87.6 0.1 concatenate.14
  87.8 0.7 broadcast_in_dim.22
  88.4 4.9 %all-to-all-start.1 = ((f32[32,8,128]{2,1,0:T(8,128)}), f32[32,8,128]{2,1,0:T(8,128)S(1)}, u32[]{:S(2)}, u32[]{:S(2)}) async-start(f32[32,8,128]{2,1,0:T(8,128)} %bitcast.12), calls=%async_computation.1 | async-start | bytes 262144 | tf_op jit(solution)/shard_map/all_to_all | solution.py:262
  93.3 8.2 %all-to-all-done.1 = f32[32,8,128]{2,1,0:T(8,128)S(1)} async-done(((f32[32,8,128]{2,1,0:T(8,128)}), f32[32,8,128]{2,1,0:T(8,128)S(1)}, u32[]{:S(2)}, u32[]{:S(2)}) %all-to-all-start.1) | async-done | bytes 131104 | tf_op jit(solution)/shard_map/all_to_all | solution.py:262
  101.6 0.1 reshape.49
  101.7 0.6 reshape.50
  102.3 0.7 reshape.51
  (33 shorter events, 0.3 us)
Async XLA Ops:
  0.6 46.8 %copy-start = (s32[4,256]{1,0:T(4,128)S(1)}, s32[4,256]{1,0:T(4,128)}, u32[]{:S(2)}) copy-start(s32[4,256]{1,0:T(4,128)} %param.15) | copy-start | bytes 12292
  8.1 5.4 %copy-start.3 = (bf16[32,24,24]{0,2,1:T(8,128)(2,1)S(1)}, bf16[32,24,24]{0,2,1:T(8,128)(2,1)}, u32[]{:S(2)}) copy-start(bf16[32,24,24]{0,2,1:T(8,128)(2,1)} %param.12) | copy-start | bytes 110596
  8.1 5.5 %copy-start.7 = (s32[32]{0:T(128)S(1)}, s32[32]{0:T(128)}, u32[]{:S(2)}) copy-start(s32[32]{0:T(128)} %param.14) | copy-start | bytes 388
  8.1 5.6 %copy-start.4 = (f32[32,24]{0,1:T(8,128)S(1)}, f32[32,24]{0,1:T(8,128)}, u32[]{:S(2)}) copy-start(f32[32,24]{0,1:T(8,128)} %param.13) | copy-start | bytes 9220
  8.1 5.7 %copy-start.6 = (s32[64,3]{0,1:T(4,128)S(1)}, s32[64,3]{0,1:T(4,128)}, u32[]{:S(2)}) copy-start(s32[64,3]{0,1:T(4,128)} %param.17) | copy-start | bytes 2308
  8.1 40.7 %copy-start.5 = (f32[256,3]{0,1:T(4,128)S(1)}, f32[256,3]{0,1:T(4,128)}, u32[]{:S(2)}) copy-start(f32[256,3]{0,1:T(4,128)} %param.16) | copy-start | bytes 9220
  8.1 41.6 %all-to-all-start = ((bf16[8,192,432]{2,1,0:T(8,128)(2,1)}), bf16[8,192,432]{2,1,0:T(8,128)(2,1)S(1)}, u32[]{:S(2)}, u32[]{:S(2)}) async-start(bf16[8,192,432]{2,1,0:T(8,128)(2,1)} %bitcast.34), calls=%async_computation | async-start | bytes 3145728 | tf_op jit(solution)/shard_map/all_to_all | solution.py:233
  37.9 11.8 %copy-start.2 = (f32[256,25]{1,0:T(8,128)}, f32[256,25]{1,0:T(8,128)S(1)}, u32[]{:S(2)}) copy-start(f32[256,25]{1,0:T(8,128)S(1)} %all_gather.7) | copy-start | bytes 76804
  49.8 1.2 %copy-start.1 = (bf16[8,192,432]{2,1,0:T(8,128)(2,1)}, bf16[8,192,432]{2,1,0:T(8,128)(2,1)S(1)}, u32[]{:S(2)}) copy-start(bf16[8,192,432]{2,1,0:T(8,128)(2,1)S(1)} %all-to-all-done.a_ref) | copy-start | bytes 3981316
  88.4 13.1 %all-to-all-start.1 = ((f32[32,8,128]{2,1,0:T(8,128)}), f32[32,8,128]{2,1,0:T(8,128)S(1)}, u32[]{:S(2)}, u32[]{:S(2)}) async-start(f32[32,8,128]{2,1,0:T(8,128)} %bitcast.12), calls=%async_computation.1 | async-start | bytes 262144 | tf_op jit(solution)/shard_map/all_to_all | solution.py:262

commit v2 on v1

v2 whole, which is shorter than its diff:
```python
import functools
import math

import jax
import jax.numpy as jnp
import numpy as np
from jax import lax
from jax.experimental import pallas as pl
from jax.experimental.pallas import tpu as pltpu
from jax.sharding import PartitionSpec as P

SIGMA = 0.1
THERMAL_ENERGY_KT = 0.2
VMEM = pltpu.CompilerParams(vmem_limit_bytes=56 * 1024 * 1024)
F32 = jnp.float32
BF16 = jnp.bfloat16


def phase_table(lattice, kpoint_rows):
    rvec = lattice.astype(jnp.float32)
    argument = (
        rvec[:, 0:1] * kpoint_rows[:, 0][None, :]
        + rvec[:, 1:2] * kpoint_rows[:, 1][None, :]
        + rvec[:, 2:3] * kpoint_rows[:, 2][None, :]
    )
    return jnp.cos(2.0 * math.pi * argument).astype(jnp.bfloat16)


def iota(shape, dim):
    return lax.broadcasted_iota(jnp.int32, shape, dim)


def rotate_kernel(n_modes, n_bands, v_parts, halves, coup_ref, rot_ref, out_ref):
    r = coup_ref.shape[1]
    pair = n_bands * n_bands
    rows = n_modes * r
    x = coup_ref[0].astype(F32)
    x = jnp.concatenate([x[:, c * pair : (c + 1) * pair] for c in range(n_modes)], axis=0).astype(BF16)
    rot = rot_ref[0]
    spread_v = (iota((rows, n_modes), 0) // r == iota((rows, n_modes), 1)).astype(BF16)
    spread_c = (iota((n_modes, rows), 1) // r == iota((n_modes, rows), 0)).astype(BF16)
    half = lax.dot_general(spread_v, rot, (((1,), (1,)), ((), ())), preferred_element_type=F32)
    full = jnp.dot(half.astype(BF16), spread_c, preferred_element_type=F32)
    same = iota((rows, rows), 0) % r == iota((rows, rows), 1) % r
    big = jnp.where(same, full, 0.0).astype(BF16)
    y = jnp.dot(big, x, preferred_element_type=F32)
    v_each = n_modes // v_parts // halves
    cols = v_each * n_bands
    for part in range(v_parts):
        pieces = []
        for h in range(halves):
            first = (part * halves + h) * v_each
            for i in range(n_bands):
                block = [
                    y[v * r : (v + 1) * r, i * n_bands : (i + 1) * n_bands]
                    for v in range(first, first + v_each)
                ]
                if cols % 128:
                    block.append(jnp.zeros((r, -cols % 128), F32))
                pieces.append(jnp.concatenate(block, axis=1))
        out_ref[part, 0] = jnp.concatenate(pieces, axis=0).T[:cols].astype(BF16)


def rotate(coupling, rotation, n_bands, v_parts, halves):
    q, r, width = coupling.shape
    n_modes = rotation.shape[1]
    rows = n_modes // v_parts // halves * n_bands
    cols = halves * n_bands * r
    return pl.pallas_call(
        functools.partial(rotate_kernel, n_modes, n_bands, v_parts, halves),
        grid=(q,),
        in_specs=[
            pl.BlockSpec((1, r, width), lambda a: (a, 0, 0)),
            pl.BlockSpec((1, n_modes, n_modes), lambda a: (a, 0, 0)),
        ],
        out_specs=pl.BlockSpec((v_parts, 1, rows, cols), lambda a: (0, a, 0, 0)),
        out_shape=jax.ShapeDtypeStruct((v_parts, q, rows, cols), BF16),
        compiler_params=VMEM,
        name="rotate_modes",
    )(coupling, rotation)


def prepare_kernel(
    n_bands, n_v,
    freq_ref, start_ref, kq_ref, points_ref, phase_ref,
    pv_out, bd_out, eo_out, so_out,
    eig_scr, en_scr, fl_scr,
):
    g = pl.program_id(0)
    per = 128 // n_bands
    k_all = points_ref.shape[0]
    k_loc = phase_ref.shape[1]
    n_r = phase_ref.shape[0]
    at_once = pv_out.shape[0]
    at_en = points_ref.shape[1] - 128
    n_vg = fl_scr.shape[1] // 128
    scale = 1.0 / (SIGMA * math.sqrt(2.0))
    lane = iota((1, 128), 1)
    roll = lambda x, shift: pltpu.roll(x, shift % 128, 1) if shift % 128 else x

    @pl.when(g == 0)
    def _():
        en = points_ref[:, at_en:].astype(F32)
        lim = en[:, 3 * n_bands : 3 * n_bands + 1]
        level = en + roll(en, -n_bands) + roll(en, -2 * n_bands)
        en_scr[...] = jnp.where(lane < n_bands, level, 0.0)
        keep = lane.astype(F32) < jnp.minimum(lim, float(n_bands))
        for i in range(n_bands):
            lo = i * n_bands
            tile = lo // 128 * 128
            block = roll(points_ref[:, tile : tile + 128].astype(F32), tile - lo)
            if lo + n_bands > tile + 128:
                more = roll(points_ref[:, tile + 128 : tile + 256].astype(F32), tile - lo)
                block = jnp.where(lane < tile + 128 - lo, block, more)
            eig_scr[pl.ds(i, k_all, stride=n_bands), :] = jnp.where(keep, block, 0.0)
        for vg in range(n_vg):
            row = jnp.zeros((1, 128), F32)
            for x in range(min(per, n_v - vg * per)):
                row = jnp.where(lane // n_bands == x, freq_ref[0, vg * per + x], row)
            fl_scr[0:1, vg * 128 : (vg + 1) * 128] = row

    for t in range(at_once):
        first = (g * at_once + t) * 2 * per
        c = iota((1, 256), 1)
        k_lane = first + c // 128 * per + c % 128 // n_bands
        k_lane = jnp.where((c % 128 < per * n_bands) & (k_lane < k_loc), k_lane, -1)
        spread = (iota((k_loc, 256), 0) == k_lane).astype(BF16)
        pv_out[t, :n_r, :] = jnp.dot(phase_ref[...], spread, preferred_element_type=F32).astype(BF16)
        far_rows = []
        v_tiles = []
        for kg in range(2):
            vl = None
            level = None
            diagonal = []
            for x in range(per):
                k = jnp.minimum(first + kg * per + x, k_loc - 1)
                near = k + start_ref[0]
                far = kq_ref[0, k]
                v = roll(eig_scr[pl.ds(pl.multiple_of(far * n_bands, 8), n_bands), :], n_bands * x)
                u = roll(eig_scr[pl.ds(pl.multiple_of(near * n_bands, 8), n_bands), :], n_bands * x)
                e = roll(en_scr[pl.ds(near, 1), :], n_bands * x)
                vl = v if vl is None else vl + v
                level = e if level is None else level + e
                diagonal.append(u)
                far_rows.append(en_scr[pl.ds(far, 1), :])
            v_tiles.append(vl)
            diagonal.append(jnp.zeros((128 - per * n_bands, 128), F32))
            bd_out[t, kg] = jnp.concatenate(diagonal, axis=0).T.astype(BF16)
            rows = slice(kg * 128, (kg + 1) * 128)
            occ = jax.nn.sigmoid(-level / THERMAL_ENERGY_KT)
            eo_out[t, rows, :128] = jnp.broadcast_to(level * scale, (128, 128)).T
            eo_out[t, rows, 128:] = jnp.broadcast_to(occ, (128, 128)).T
        pv_out[t, n_r:, :] = jnp.concatenate(v_tiles, axis=1).astype(BF16)
        far_rows.append(jnp.zeros((16 - 2 * per, 128), F32))
        far_e = jnp.concatenate(far_rows, axis=0)
        far_e = sum((roll(far_e, n_bands * x) for x in range(1, per)), far_e)
        so_out[t, :, n_vg * 128 :] = jax.nn.sigmoid(-far_e / THERMAL_ENERGY_KT)
        for vg in range(n_vg):
            sh = (far_e - fl_scr[0:1, vg * 128 : (vg + 1) * 128]) * scale
            so_out[t, :, vg * 128 : (vg + 1) * 128] = jnp.where(lane < per * n_bands, sh, 1e4)


def prepare(freq, start, kq, points, phase, n_bands, n_v, at_once=4):
    per = 128 // n_bands
    k_loc = phase.shape[1]
    tiles = -(-k_loc // (2 * per * at_once)) * at_once
    n_vg = -(-n_v // per)
    k_all = points.shape[0]
    n_pv = phase.shape[0] + n_bands
    whole = lambda x: pl.BlockSpec(x.shape, lambda g: (0,) * x.ndim)
    smem = pl.BlockSpec(memory_space=pltpu.SMEM)
    return pl.pallas_call(
        functools.partial(prepare_kernel, n_bands, n_v),
        grid=(tiles // at_once,),
        in_specs=[smem, smem, smem, whole(points), whole(phase)],
        out_specs=[
            pl.BlockSpec((at_once, n_pv, 256), lambda g: (g, 0, 0)),
            pl.BlockSpec((at_once, 2, 128, 128), lambda g: (g, 0, 0, 0)),
            pl.BlockSpec((at_once, 256, 256), lambda g: (g, 0, 0)),
            pl.BlockSpec((at_once, 16, (n_vg + 1) * 128), lambda g: (g, 0, 0)),
        ],
        out_shape=[
            jax.ShapeDtypeStruct((tiles, n_pv, 256), BF16),
            jax.ShapeDtypeStruct((tiles, 2, 128, 128), BF16),
            jax.ShapeDtypeStruct((tiles, 256, 256), F32),
            jax.ShapeDtypeStruct((tiles, 16, (n_vg + 1) * 128), F32),
        ],
        scratch_shapes=[
            pltpu.VMEM((k_all * n_bands, 128), F32),
            pltpu.VMEM((k_all, 128), F32),
            pltpu.VMEM((1, n_vg * 128), F32),
        ],
        compiler_params=VMEM,
        name="prepare",
    )(freq, start, kq, points, phase)


def lane_ranges(n_bands):
    per = 128 // n_bands
    lane = iota((n_bands, 128), 1)
    inside = []
    for d in range(2 * per - 1):
        lo = n_bands * d % 128
        hi = lo + n_bands
        inside.append(
            (lane >= lo) & (lane < hi) if hi <= 128 else (lane >= lo) | (lane < hi - 128)
        )
    return inside


def swap_blocks(t_ref, kg, n_bands, n_v):
    per = 128 // n_bands
    inside = lane_ranges(n_bands)
    tiles = []
    for first in range(0, n_v, per):
        count = min(per, n_v - first)
        rolled = []
        for x in range(count):
            v = first + x
            block = t_ref[v * n_bands : (v + 1) * n_bands, kg * 128 : (kg + 1) * 128]
            rolled.append(pltpu.roll(block, n_bands * x, 1) if x else block)
        column = []
        for k in range(per):
            mix = rolled[0] if count == per else jnp.where(inside[k], rolled[0], 0.0)
            for x in range(1, count):
                mix = jnp.where(inside[k + x], rolled[x], mix)
            column.append(pltpu.roll(mix, 128 - n_bands * k, 1) if k else mix)
        column.append(jnp.zeros((128 - per * n_bands, 128), F32))
        tiles.append(jnp.concatenate(column, axis=0).astype(BF16))
    return jnp.concatenate(tiles, axis=1)


def fill_products(w_ref, pv, n_bands, r):
    n_src = (pv.shape[0] - n_bands) // r
    depth = n_bands * r
    ph, vl = pv[: n_src * r].astype(F32), pv[n_src * r :].astype(F32)
    if r % 8 == 0:
        for i in range(0, n_bands, 2):
            v0 = vl[i : i + 1, :]
            v1 = vl[i + 1 : i + 2, :]
            for s in range(n_src):
                p = ph[s * r : (s + 1) * r, :]
                at = s * depth + i * r
                w_ref[at : at + 2 * r, :] = jnp.concatenate([p * v0, p * v1], axis=0).astype(BF16)
        return
    row = iota((depth, 1), 0)
    by_band = (row // r == iota((depth, n_bands), 1)).astype(BF16)
    v_rows = jnp.dot(by_band, vl.astype(BF16), preferred_element_type=F32)
    for s in range(n_src):
        by_src = (row % r + s * r == iota((depth, n_src * r), 1)).astype(BF16)
        p_rows = jnp.dot(by_src, ph.astype(BF16), preferred_element_type=F32)
        w_ref[s * depth : (s + 1) * depth, :] = (p_rows * v_rows).astype(BF16)


def group_sums(coupled, kg, eo_ref, so_ref, n_bands, ph):
    per = 128 // n_bands
    n_vg = len(ph)
    sums = []
    for k in range(per):
        here = slice(k * n_bands, (k + 1) * n_bands)
        lo = kg * 128 + k * n_bands
        kk = kg * per + k
        ek = eo_ref[0, lo : lo + n_bands, :128]
        occ = eo_ref[0, lo : lo + n_bands, 128:] - so_ref[0, kk : kk + 1, n_vg * 128 :]
        el = None
        for vg in range(n_vg):
            c = coupled[here, vg * 128 : (vg + 1) * 128]
            d = so_ref[0, kk : kk + 1, vg * 128 : (vg + 1) * 128] - ek
            strength = c * c * jnp.exp(-(d * d))
            el = strength if el is None else el + strength
            weighed = strength * occ
            ph[vg] = weighed if ph[vg] is None else ph[vg] + weighed
        sums.append(el)
    sums.append(jnp.zeros((128 - per * n_bands, 128), F32))
    return jnp.sum(jnp.concatenate(sums, axis=0).T, axis=0, keepdims=True)


def product_and_sums(a_ref, w_ref, t_new, t_old, bd_ref, eo_ref, so_ref, n_bands, n_v):
    per = 128 // n_bands
    n_vg = -(-n_v // per)
    cuts = [min(x * per, n_v) * n_bands for x in range(n_vg + 1)]
    parts = [slice(a, b) for a, b in zip(cuts, cuts[1:])]
    parts += [slice(0, 0)] * (4 - n_vg)

    def product(x):
        if parts[x].stop > parts[x].start:
            t_new[parts[x], :] = jnp.dot(a_ref[parts[x], :], w_ref[...], preferred_element_type=F32)

    ph = [None] * n_vg
    product(0)
    right = swap_blocks(t_old, 0, n_bands, n_v)
    product(1)
    c0 = jnp.dot(bd_ref[0, 0], right, preferred_element_type=F32)
    right = swap_blocks(t_old, 1, n_bands, n_v)
    product(2)
    el0 = group_sums(c0, 0, eo_ref, so_ref, n_bands, ph)
    c1 = jnp.dot(bd_ref[0, 1], right, preferred_element_type=F32)
    product(3)
    el1 = group_sums(c1, 1, eo_ref, so_ref, n_bands, ph)
    for x in range(4, n_vg):
        product(x)
    return [el0, el1], ph


def linewidth_kernel(
    n_bands, n_v, halves, r, el_scale, ph_scale,
    a_ref, pv_ref, bd0_ref, bd1_ref, eo0_ref, eo1_ref, so0_ref, so1_ref,
    el_out, ph_out,
    a_scr, w0_scr, w1_scr, t0_scr, t1_scr, ph_scr,
):
    g = pl.program_id(0)
    last = pl.num_programs(0) - 1
    n_src, rows, wide = a_ref.shape
    depth = wide // halves
    n_vg = ph_scr.shape[0]

    @pl.when(g == 0)
    def _():
        for s in range(n_src):
            block = a_ref[s]
            for h in range(halves):
                a_scr[h * rows : (h + 1) * rows, s * depth : (s + 1) * depth] = block[
                    :, h * depth : (h + 1) * depth
                ]
        t1_scr[...] = jnp.zeros_like(t1_scr)
        ph_scr[...] = jnp.zeros_like(ph_scr)

    fill_products(w0_scr, pv_ref[0], n_bands, r)
    el0, ph0 = product_and_sums(
        a_scr, w0_scr, t0_scr, t1_scr, bd0_ref, eo0_ref, so0_ref, n_bands, n_v
    )
    fill_products(w1_scr, pv_ref[1], n_bands, r)
    el1, ph1 = product_and_sums(
        a_scr, w1_scr, t1_scr, t0_scr, bd1_ref, eo1_ref, so1_ref, n_bands, n_v
    )
    el_out[g] = jnp.concatenate(el0 + el1, axis=0) * el_scale
    second = jnp.where(g < last, 1.0, 0.0)
    for vg in range(n_vg):
        ph_scr[vg] += ph0[vg] + ph1[vg] * second

    @pl.when(g == last)
    def _():
        fold = (iota((128, 128), 0) // n_bands == iota((128, 128), 1)).astype(F32)
        sums = jnp.sum(ph_scr[...], axis=1)
        ph_out[...] = (
            jnp.dot(sums, fold, precision=lax.Precision.HIGHEST, preferred_element_type=F32) * ph_scale
        )


def linewidths(a, prepared, k_loc, n_bands, n_v, halves, r, el_scale, ph_scale):
    pv, bd, eo, so = prepared
    steps = -(-k_loc // (128 // n_bands * 4))
    n_vg = so.shape[2] // 128 - 1
    total = (pv.shape[1] - n_bands) * n_bands
    tile0 = lambda g: jnp.maximum(2 * g - 1, 0)
    tile1 = lambda g: jnp.minimum(2 * g, 2 * steps - 1)
    pairs = [
        pl.BlockSpec((1,) + x.shape[1:], lambda g, f=f, n=x.ndim: (f(g),) + (0,) * (n - 1))
        for x in (bd, eo, so)
        for f in (tile0, tile1)
    ]
    el, ph = pl.pallas_call(
        functools.partial(linewidth_kernel, n_bands, n_v, halves, r, el_scale, ph_scale),
        grid=(steps + 1,),
        in_specs=[
            pl.BlockSpec(a.shape, lambda g: (0, 0, 0)),
            pl.BlockSpec((2,) + pv.shape[1:], lambda g: (jnp.minimum(g, steps - 1), 0, 0)),
        ]
        + pairs,
        out_specs=[
            pl.BlockSpec((steps + 1, 4, 128), lambda g: (0, 0, 0)),
            pl.BlockSpec((n_vg, 128), lambda g: (0, 0)),
        ],
        out_shape=[
            jax.ShapeDtypeStruct((steps + 1, 4, 128), F32),
            jax.ShapeDtypeStruct((n_vg, 128), F32),
        ],
        scratch_shapes=[
            pltpu.VMEM((n_v * n_bands, total), BF16),
            pltpu.VMEM((total, 256), BF16),
            pltpu.VMEM((total, 256), BF16),
            pltpu.VMEM((n_v * n_bands, 256), F32),
            pltpu.VMEM((n_v * n_bands, 256), F32),
            pltpu.VMEM((n_vg, n_bands, 128), F32),
        ],
        compiler_params=VMEM,
        name="linewidths",
    )(a, pv, bd, bd, eo, eo, so, so)
    return el.reshape(-1, 128)[2:], ph


def on_device(coupling, rotation, freq, eigvec, energies, window, kq_index, kpoints, lattice):
    plane = ("ka", "row")
    everywhere = ("ka", "pb", "row")
    n_ka = lax.axis_size("ka")
    n_row = lax.axis_size("row")
    n_pb = lax.axis_size("pb")
    n_group = n_ka * n_row
    k_dev, n_bands = eigvec.shape[:2]
    q_dev, n_modes = rotation.shape[:2]
    assert q_dev == n_row
    pair = n_bands * n_bands
    total_k = k_dev * n_group
    total_q = q_dev * n_pb
    v_parts = math.gcd(n_modes, n_ka)
    k_parts = n_ka // v_parts
    n_v = n_modes // v_parts
    halves = 2 if n_v % 2 == 0 else 1
    k_loc = total_k // k_parts
    ka_pos = lax.axis_index("ka")
    row_pos = lax.axis_index("row")
    pb_pos = lax.axis_index("pb")

    parts, rest = [], energies
    for _ in range(3):
        part = lax.reduce_precision(rest, 8, 7)
        parts.append(part.astype(BF16))
        rest = rest - part
    gap = -pair % 128
    mine = [eigvec.reshape(k_dev, pair), jnp.zeros((k_dev, gap), BF16)] + parts
    mine += [window.astype(BF16)[:, None], jnp.zeros((k_dev, 127 - 3 * n_bands), BF16)]
    mine = jnp.concatenate(mine, axis=1)
    points = lax.all_to_all(
        jnp.broadcast_to(mine[None], (n_group,) + mine.shape), plane, 0, 0, tiled=True
    ).reshape(total_k, mine.shape[1])

    pad = -coupling.shape[1] % 8
    if pad:
        coupling = jnp.pad(coupling, ((0, 0), (0, pad), (0, 0)))
    r, r_sent = coupling.shape[1] - pad, coupling.shape[1]
    rotated = rotate(coupling, rotation, n_bands, v_parts, halves)
    if k_parts > 1:
        rotated = jnp.repeat(rotated, k_parts, axis=0)
    rotated = rotated.reshape((n_group,) + rotated.shape[2:])
    a = lax.all_to_all(rotated, plane, 0, 0, tiled=True)
    if pad:
        a = a.reshape(a.shape[:2] + (halves * n_bands, r_sent))[..., :r]
        a = a.reshape(a.shape[:2] + (halves * n_bands * r,))

    k_start = (ka_pos % k_parts) * k_loc
    kp = lax.dynamic_slice_in_dim(kpoints, k_start, k_loc, 0)
    phase = phase_table(lattice, kp)
    kq = lax.dynamic_slice(kq_index, (row_pos, k_start), (1, k_loc))
    v_start = (ka_pos // k_parts) * n_v
    freq_mine = lax.dynamic_slice(freq, (row_pos, v_start), (1, n_v))
    prepared = prepare(
        freq_mine, k_start[None], kq, points, phase, n_bands, n_v
    )
    norm = 1.0 / (math.sqrt(2.0 * math.pi) * SIGMA)
    el, ph = linewidths(
        a, prepared, k_loc, n_bands, n_v, halves, r,
        norm / (total_q * n_modes * n_bands), norm / (total_k * n_bands),
    )
    per = 128 // n_bands
    el = el[:, : per * n_bands].reshape(-1, n_bands)[:k_loc].T
    ph = ph[:, :per].reshape(-1)[:n_v]
    if k_parts > 1:
        el = lax.dynamic_update_slice(jnp.zeros((n_bands, total_k), F32), el, (jnp.int32(0), k_start))
    per_row = 128 // k_dev
    fold = n_bands // per_row
    el = el.reshape(per_row, fold, n_group, k_dev).transpose(2, 1, 0, 3).reshape(n_group, fold, 128)
    ph_rows = 8 - fold % 8
    ph = jnp.pad(ph, (0, ph_rows * 128 - n_v)).reshape(1, ph_rows, 128)
    send = jnp.concatenate([el, jnp.broadcast_to(ph, (n_group, ph_rows, 128))], axis=1)
    send = send.reshape(n_ka, 1, n_row, fold + ph_rows, 128)
    send = jnp.broadcast_to(send, (n_ka, n_pb, n_row, fold + ph_rows, 128))
    send = send.reshape(n_group * n_pb, fold + ph_rows, 128)
    got = lax.all_to_all(send, everywhere, 0, 0, tiled=True)
    got = got.reshape(n_ka, n_pb, n_row, fold + ph_rows, 128)
    electron = jnp.sum(got[:, :, :, :fold], axis=(0, 1, 2))
    electron = electron.reshape(fold, per_row, k_dev).transpose(2, 1, 0).reshape(k_dev, n_bands)
    near = lax.dynamic_index_in_dim(got, pb_pos, 1, keepdims=False)[:, :, fold, :n_v]
    near = near.reshape(v_parts, k_parts, n_row, n_v).sum(axis=1)
    phonon = near.transpose(1, 0, 2).reshape(n_row, n_modes)
    return (electron, phonon)


def solution(mesh):
    return jax.shard_map(
        on_device,
        mesh=mesh,
        in_specs=(
            P("pb", ("ka", "row"), None),
            P("pb", None, None),
            P("pb", None),
            P(("ka", "row"), None, None),
            P(("ka", "row"), None),
            P(("ka", "row")),
            P("pb", None),
            P(),
            P(),
        ),
        out_specs=(P(("ka", "row"), None), P("pb", None)),
        check_vma=False,
    )
```

time: 104 us -> 80.7 us (0.78)
  blocking collectives: 32.2 us -> 0 us
  waiting for transfers between devices: 8.23 us -> 15.4 us
  local copies, waits for them, and re-layouts: 7.26 us -> 10.6 us
  Pallas kernels: 41.1 us -> 38.2 us
  starting transfers between devices: 10.2 us -> 12.7 us
    all_gather x2 -> x0, blocking collectives: 32.2 us -> none  [the longest x1 22.7 us: on_device(): level_all = lax.all_gather(level, plane, axis=0, tiled=True)]
    all_to_all x1, waiting for transfers between devices: 0.01 us -> 5.91 us  [on_device(): a = lax.all_to_all(rotated, plane, 0, 0, tiled=True)]
    all_to_all x0 -> x1, starting transfers between devices: none -> 5.17 us  [on_device(): lax.all_to_all(jnp.broadcast_to(mine[None], (n_group,) + mine.shape), pla...]
    pallas_call x1 -> x2, Pallas kernels: 35 us -> 31.8 us  [the longest x1 22.2 us: linewidths(): pl.pallas_call(functools.partial(linewidth_kernel, n_bands, n_v, halves,...]
    reshape x1 -> x3, local copies, waits for them, and re-layouts: 0.13 us -> 1.9 us  [the longest x1 1.04 us: on_device(): mine = [eigvec.reshape(k_dev, pair), jnp.zeros((k_dev, gap), BF16)] + parts]
    all_to_all x1, starting transfers between devices: 5.32 us -> 3.57 us  [on_device(): a = lax.all_to_all(rotated, plane, 0, 0, tiled=True)]
    mul x2 -> x0, other arithmetic: 1.56 us -> none  [the longest x1 0.82 us: on_device(): ph = ph[:, 0] * (1.0 / (total_k * n_bands))]
    all_to_all x0 -> x1, waiting for transfers between devices: none -> 1.23 us  [on_device(): lax.all_to_all(jnp.broadcast_to(mine[None], (n_group,) + mine.shape), pla...]
  transfers between devices with their start and end apart: 2 -> 3, of which waited for: 1 -> 3; matrix products, arithmetic and copies ran while one was open for 4% -> 4% of each run, Pallas kernels for 0% -> 20%
where the time goes in v2:
time: 80.7 us; the launch traced here: 80.1 us
  Pallas kernels  38.2 us (47%)
  waiting for transfers between devices  15.4 us (19%)
  starting transfers between devices  12.7 us (16%)
  local copies, waits for them, and re-layouts  10.6 us (13%)
  other arithmetic  2.38 us (3%)
    pallas_call x1, Pallas kernels, linewidths(): pl.pallas_call(functools.partial(linewidth_kernel, n_bands, n_v, halves,...  22.2 us
    pallas_call x1, Pallas kernels, prepare(): pl.pallas_call(functools.partial(prepare_kernel, n_bands, n_v), grid=(til...  9.59 us
    all_to_all x1, waiting for transfers between devices, on_device(): got = lax.all_to_all(send, everywhere, 0, 0, tiled=True)  8.22 us
    pallas_call x1, Pallas kernels, rotate(): pl.pallas_call(functools.partial(rotate_kernel, n_modes, n_bands, v_parts...  6.48 us
    all_to_all x1, waiting for transfers between devices, on_device(): a = lax.all_to_all(rotated, plane, 0, 0, tiled=True)  5.91 us
    all_to_all x1, starting transfers between devices, on_device(): lax.all_to_all(jnp.broadcast_to(mine[None], (n_group,) + mine.shape), pla...  5.17 us
    all_to_all x1, starting transfers between devices, on_device(): got = lax.all_to_all(send, everywhere, 0, 0, tiled=True)  3.99 us
    all_to_all x1, starting transfers between devices, on_device(): a = lax.all_to_all(rotated, plane, 0, 0, tiled=True)  3.57 us
  transfers between devices with their start and end apart: 3, of which 3 were waited for; matrix products, arithmetic and copies ran while one was open for 4% of the time, Pallas kernels for 20%

profile of v2, /device:TPU:0, one launch (start us, length us, event | category | flops | bytes accessed | tf_op | source)
XLA Modules:
  0.0 80.1 jit_solution(7146850403648952337)
XLA Ops:
  0.7 0.7 convert_bitcast_fusion
  1.4 0.7 fusion.1
  2.4 1.0 %copy.63 = bf16[32,576]{1,0:T(8,128)(2,1)S(1)} copy(bf16[32,576]{0,1:T(8,128)(2,1)} %bitcast.41) | data formatting | bytes 73728 | tf_op jit(solution)/shard_map/reshape | solution.py:420
  3.6 0.8 broadcast_in_dim.33
  4.3 5.2 %all-to-all-start.1 = ((bf16[8,32,768]{2,1,0:T(8,128)(2,1)}), bf16[8,32,768]{2,1,0:T(8,128)(2,1)S(1)}, u32[]{:S(2)}, u32[]{:S(2)}) async-start(bf16[8,32,768]{2,1,0:T(8,128)(2,1)} %broadcast_in_dim.33), calls=%async_computation.1 | async-start | bytes 786432 | tf_op jit(solution)/shard_map/all_to_all | solution.py:423
  9.5 0.6 copy.52.rot_ref
  10.1 6.5 %rotate_modes.1 = bf16[2,4,216,384]{3,2,1,0:T(8,128)(2,1)} custom-call(bf16[4,8,20736]{2,1,0:T(8,128)(2,1)} %coup_ref.1, bf16[4,36,36]{2,1,0:T(8,128)(2,1)} %copy.52.rot_ref), custom_call_target="tpu_custom_call" | custom-call | tf_op jit(solution)/shard_map/rotate_modes/pallas_call | solution.py:69
  16.6 1.2 %all-to-all-done.1 = bf16[8,32,768]{2,1,0:T(8,128)(2,1)S(1)} async-done(((bf16[8,32,768]{2,1,0:T(8,128)(2,1)}), bf16[8,32,768]{2,1,0:T(8,128)(2,1)S(1)}, u32[]{:S(2)}, u32[]{:S(2)}) %all-to-all-start.1) | async-done | bytes 393248 | tf_op jit(solution)/shard_map/all_to_all | solution.py:423
  17.9 0.8 copy-done.2
  18.6 3.6 %all-to-all-start = ((bf16[8,216,384]{2,1,0:T(8,128)(2,1)}), bf16[8,216,384]{2,1,0:T(8,128)(2,1)S(1)}, u32[]{:S(2)}, u32[]{:S(2)}) async-start(bf16[8,216,384]{2,1,0:T(8,128)(2,1)} %bitcast.36), calls=%async_computation | async-start | bytes 2654208 | tf_op jit(solution)/shard_map/all_to_all | solution.py:435
  22.2 1.3 %dynamic_slice.11.freq_ref = f32[1,18]{1,0:T(1,128)} dynamic-slice(f32[4,36]{1,0:T(4,128)} %param.11, s32[]{:T(128)S(6)} %select_n.20, s32[]{:T(128)S(6)} %select_n.21), dynamic_slice_sizes={1,18} | dynamic-slice | bytes 148 | tf_op jit(solution)/shard_map/dynamic_slice | solution.py:445
  23.5 0.6 constant_dynamic-slice_fusion.kq_ref
  24.1 0.9 %cosine_convert_fusion.phase_ref = bf16[64,256]{1,0:T(8,128)(2,1)} fusion(f32[256]{0:T(256)S(1)} %bitcast.46, f32[64]{0:T(128)S(1)} %get-tuple-element.21, f32[256]{0:T(256)S(1)} %bitcast.47, f32[64]{0:T(128)S(1)} %get-tuple-element.22, f32[256]{0:T(256)S(1)} %bitcast.45, f32[64]{0:T(128)S(1)} %get-tuple-element.20), kind=kLoop, calls=%fused_computation.2 | loop fusion | flops 114688 | bytes 36608 | tf_op jit(solution)/shard_map/convert_element_type | solution.py:26
  25.0 9.6 %prepare.1 = (bf16[28,88,256]{2,1,0:T(8,128)(2,1)}, bf16[28,2,128,128]{3,2,1,0:T(8,128)(2,1)}, f32[28,256,256]{2,1,0:T(8,128)}, f32[28,16,640]{2,1,0:T(8,128)}) custom-call(f32[1,18]{1,0:T(1,128)} %dynamic_slice.11.freq_ref, s32[1]{0:T(128)} %constant.52.clone.1.start_ref, s32[1,256]{1,0:T(1,128)} %constant_dynamic-slice_fusion.kq_ref, ...), custom_call_target="tpu_custom_call" | custom-call | tf_op jit(solution)/shard_map/prepare/pallas_call | solution.py:172
  34.6 5.9 %all-to-all-done.a_ref = bf16[8,216,384]{2,1,0:T(8,128)(2,1)S(1)} async-done(((bf16[8,216,384]{2,1,0:T(8,128)(2,1)}), bf16[8,216,384]{2,1,0:T(8,128)(2,1)S(1)}, u32[]{:S(2)}, u32[]{:S(2)}) %all-to-all-start) | async-done | bytes 1327136 | tf_op jit(solution)/shard_map/all_to_all | solution.py:435
  40.5 1.1 %copy-done.1 = bf16[8,216,384]{2,1,0:T(8,128)(2,1)} copy-done((bf16[8,216,384]{2,1,0:T(8,128)(2,1)}, bf16[8,216,384]{2,1,0:T(8,128)(2,1)S(1)}, u32[]{:S(2)}) %copy-start.1) | copy-done | bytes 1327128
  41.6 22.2 %linewidths.1 = (f32[14,4,128]{2,1,0:T(4,128)}, f32[4,128]{1,0:T(4,128)}) custom-call(bf16[8,216,384]{2,1,0:T(8,128)(2,1)} %copy-done.1, bf16[28,88,256]{2,1,0:T(8,128)(2,1)} %get-tuple-element.8.pv_ref, bf16[28,2,128,128]{3,2,1,0:T(8,128)(2,1)} %get-tuple-element.9.bd0_ref.bd1_ref, bf16[28,2,128,128]{3,2,1,0:T(8,128)(2,1)} %get-tuple-element.9.bd0_ref.bd1_ref, ...), custom_call_target="tpu_custom_call" | custom-call | tf_op jit(solution)/shard_map/linewidths/pallas_call | solution.py:362
  63.8 0.8 slice.50
  64.5 0.8 reshape.59
  65.8 0.7 broadcast_in_dim.37
  66.4 4.0 %all-to-all-start.2 = ((f32[32,8,128]{2,1,0:T(8,128)}), f32[32,8,128]{2,1,0:T(8,128)S(1)}, u32[]{:S(2)}, u32[]{:S(2)}) async-start(f32[32,8,128]{2,1,0:T(8,128)} %bitcast.15), calls=%async_computation.2 | async-start | bytes 262144 | tf_op jit(solution)/shard_map/all_to_all | solution.py:468
  70.5 8.2 %all-to-all-done.2 = f32[32,8,128]{2,1,0:T(8,128)S(1)} async-done(((f32[32,8,128]{2,1,0:T(8,128)}), f32[32,8,128]{2,1,0:T(8,128)S(1)}, u32[]{:S(2)}, u32[]{:S(2)}) %all-to-all-start.2) | async-done | bytes 131104 | tf_op jit(solution)/shard_map/all_to_all | solution.py:468
  78.7 0.7 reshape.64
  79.5 0.6 reshape.63
  (36 shorter events, 1.1 us)
Async XLA Ops:
  0.6 22.9 %copy-start = (s32[4,256]{1,0:T(4,128)S(1)}, s32[4,256]{1,0:T(4,128)}, u32[]{:S(2)}) copy-start(s32[4,256]{1,0:T(4,128)} %param.15) | copy-start | bytes 12292
  0.6 8.9 %copy-start.3 = (bf16[4,36,36]{2,0,1:T(4,128)(2,1)S(1)}, bf16[4,36,36]{2,0,1:T(4,128)(2,1)}, u32[]{:S(2)}) copy-start(bf16[4,36,36]{2,0,1:T(4,128)(2,1)} %param.10) | copy-start | bytes 31108
  4.3 13.5 %all-to-all-start.1 = ((bf16[8,32,768]{2,1,0:T(8,128)(2,1)}), bf16[8,32,768]{2,1,0:T(8,128)(2,1)S(1)}, u32[]{:S(2)}, u32[]{:S(2)}) async-start(bf16[8,32,768]{2,1,0:T(8,128)(2,1)} %broadcast_in_dim.33), calls=%async_computation.1 | async-start | bytes 786432 | tf_op jit(solution)/shard_map/all_to_all | solution.py:423
  17.9 0.8 copy-start.2
  17.9 4.4 %copy-start.5 = (s32[64,3]{0,1:T(4,128)S(1)}, s32[64,3]{0,1:T(4,128)}, u32[]{:S(2)}) copy-start(s32[64,3]{0,1:T(4,128)} %param.17) | copy-start | bytes 2308
  17.9 6.2 %copy-start.4 = (f32[256,3]{0,1:T(4,128)S(1)}, f32[256,3]{0,1:T(4,128)}, u32[]{:S(2)}) copy-start(f32[256,3]{0,1:T(4,128)} %param.16) | copy-start | bytes 9220
  18.6 21.9 %all-to-all-start = ((bf16[8,216,384]{2,1,0:T(8,128)(2,1)}), bf16[8,216,384]{2,1,0:T(8,128)(2,1)S(1)}, u32[]{:S(2)}, u32[]{:S(2)}) async-start(bf16[8,216,384]{2,1,0:T(8,128)(2,1)} %bitcast.36), calls=%async_computation | async-start | bytes 2654208 | tf_op jit(solution)/shard_map/all_to_all | solution.py:435
  40.5 1.1 %copy-start.1 = (bf16[8,216,384]{2,1,0:T(8,128)(2,1)}, bf16[8,216,384]{2,1,0:T(8,128)(2,1)S(1)}, u32[]{:S(2)}) copy-start(bf16[8,216,384]{2,1,0:T(8,128)(2,1)S(1)} %all-to-all-done.a_ref) | copy-start | bytes 3981316
  66.4 12.2 %all-to-all-start.2 = ((f32[32,8,128]{2,1,0:T(8,128)}), f32[32,8,128]{2,1,0:T(8,128)S(1)}, u32[]{:S(2)}, u32[]{:S(2)}) async-start(f32[32,8,128]{2,1,0:T(8,128)} %bitcast.15), calls=%async_computation.2 | async-start | bytes 262144 | tf_op jit(solution)/shard_map/all_to_all | solution.py:468

commit v3 on v2

v3 whole, which is shorter than its diff:
```python
import functools
import math

import jax
import jax.numpy as jnp
import numpy as np
from jax import lax
from jax.experimental import pallas as pl
from jax.experimental.pallas import tpu as pltpu
from jax.sharding import PartitionSpec as P

SIGMA = 0.1
THERMAL_ENERGY_KT = 0.2
VMEM = pltpu.CompilerParams(vmem_limit_bytes=40 * 1024 * 1024)
F32 = jnp.float32
BF16 = jnp.bfloat16
UNROLL = 3


def phase_table(lattice, kpoint_rows):
    rvec = lattice.astype(jnp.float32)
    argument = (
        rvec[:, 0:1] * kpoint_rows[:, 0][None, :]
        + rvec[:, 1:2] * kpoint_rows[:, 1][None, :]
        + rvec[:, 2:3] * kpoint_rows[:, 2][None, :]
    )
    return jnp.cos(2.0 * math.pi * argument).astype(jnp.bfloat16)


def iota(shape, dim):
    return lax.broadcasted_iota(jnp.int32, shape, dim)


def pack_kernel(eig_ref, en_ref, window_ref, out_ref):
    n_bands, _, k_dev = eig_ref.shape
    pair = n_bands * n_bands
    rows = [eig_ref[...].astype(F32).reshape(pair, k_dev), jnp.zeros((-pair % 128, k_dev), F32)]
    rest = en_ref[...]
    for _ in range(3):
        part = rest.astype(BF16).astype(F32)
        rows.append(part)
        rest = rest - part
    rows.append(window_ref[...].astype(F32))
    rows.append(jnp.zeros((127 - 3 * n_bands, k_dev), F32))
    packed = jnp.concatenate(rows, axis=0)
    packed = jnp.concatenate([packed, jnp.zeros((packed.shape[0], 128 - k_dev), F32)], axis=1)
    packed = packed.T[:k_dev].astype(BF16)
    for d in range(out_ref.shape[0]):
        out_ref[d] = packed


def pack(eigvec, energies, window, copies):
    k_dev, n_bands, _ = eigvec.shape
    wide = -(-n_bands * n_bands // 128) * 128 + 128
    args = (eigvec.transpose(1, 2, 0), energies.T, window.reshape(1, k_dev))
    return pl.pallas_call(
        pack_kernel,
        grid=(1,),
        in_specs=[pl.BlockSpec(x.shape, lambda g, n=x.ndim: (0,) * n) for x in args],
        out_specs=pl.BlockSpec((copies, k_dev, wide), lambda g: (0, 0, 0)),
        out_shape=jax.ShapeDtypeStruct((copies, k_dev, wide), BF16),
        compiler_params=VMEM,
        name="pack_points",
    )(*[pltpu.with_memory_space_constraint(x, pltpu.HBM) for x in args])


def finish_kernel(n_bands, n_v, k_parts, place_ref, got_ref, el_out, ph_out, scr):
    per = 128 // n_bands
    n_ka, n_pb, n_row, rows, _ = got_ref.shape
    lane = iota((1, 128), 1)
    total = None
    for ka in range(n_ka):
        for pb in range(n_pb):
            for row in range(n_row):
                part = got_ref[ka, pb, row]
                total = part if total is None else total + part
    for x in range(per):
        shifted = pltpu.roll(total, 128 - n_bands * x, 1) if x else total
        scr[pl.ds(x, rows, stride=per), :] = shifted
    k_dev = el_out.shape[1]
    mine = scr[pl.ds(place_ref[1], k_dev), :]
    mine = jnp.concatenate([mine, jnp.zeros((128 - k_dev, 128), F32)], axis=0)
    el_out[...] = mine.T[:n_bands, :k_dev]
    for row in range(n_row):
        line = jnp.zeros((1, 128), F32)
        for ka in range(n_ka):
            part = got_ref[ka, pl.ds(place_ref[0], 1), row][0]
            for first in range(0, n_v, per):
                to = ka // k_parts * n_v + first
                vg = first // per
                moved = pltpu.roll(part[vg : vg + 1], (to - per * n_bands) % 128, 1)
                count = min(per, n_v - first)
                line = line + jnp.where((lane >= to) & (lane < to + count), moved, 0.0)
        ph_out[row : row + 1, :] = line[:, : ph_out.shape[1]]


def finish(got, place, n_bands, n_v, k_parts, k_dev, n_modes):
    n_row, rows = got.shape[2:4]
    per = 128 // n_bands
    el, ph = pl.pallas_call(
        functools.partial(finish_kernel, n_bands, n_v, k_parts),
        in_specs=[pl.BlockSpec(memory_space=pltpu.SMEM), pl.BlockSpec(memory_space=pltpu.VMEM)],
        out_shape=[
            jax.ShapeDtypeStruct((n_bands, k_dev), F32),
            jax.ShapeDtypeStruct((n_row, n_modes), F32),
        ],
        scratch_shapes=[pltpu.VMEM((rows * per, 128), F32)],
        compiler_params=VMEM,
        name="finish",
    )(place, pltpu.with_memory_space_constraint(got, pltpu.VMEM))
    return el.T, ph


def rotate_kernel(n_modes, n_bands, v_parts, halves, coup_ref, rot_ref, out_ref):
    r = coup_ref.shape[1]
    pair = n_bands * n_bands
    rows = n_modes * r
    x = coup_ref[0].astype(F32)
    x = jnp.concatenate([x[:, c * pair : (c + 1) * pair] for c in range(n_modes)], axis=0).astype(BF16)
    rot = rot_ref[0]
    spread_v = (iota((rows, n_modes), 0) // r == iota((rows, n_modes), 1)).astype(BF16)
    spread_c = (iota((n_modes, rows), 1) // r == iota((n_modes, rows), 0)).astype(BF16)
    half = lax.dot_general(spread_v, rot, (((1,), (1,)), ((), ())), preferred_element_type=F32)
    full = jnp.dot(half.astype(BF16), spread_c, preferred_element_type=F32)
    same = iota((rows, rows), 0) % r == iota((rows, rows), 1) % r
    big = jnp.where(same, full, 0.0).astype(BF16)
    y = jnp.dot(big, x, preferred_element_type=F32)
    v_each = n_modes // v_parts // halves
    cols = v_each * n_bands
    for part in range(v_parts):
        pieces = []
        for h in range(halves):
            first = (part * halves + h) * v_each
            for i in range(n_bands):
                block = [
                    y[v * r : (v + 1) * r, i * n_bands : (i + 1) * n_bands]
                    for v in range(first, first + v_each)
                ]
                if cols % 128:
                    block.append(jnp.zeros((r, -cols % 128), F32))
                pieces.append(jnp.concatenate(block, axis=1))
        out_ref[part, 0] = jnp.concatenate(pieces, axis=0).T[:cols].astype(BF16)


def rotate(coupling, rotation, n_bands, v_parts, halves):
    q, r, width = coupling.shape
    n_modes = rotation.shape[1]
    rows = n_modes // v_parts // halves * n_bands
    cols = halves * n_bands * r
    return pl.pallas_call(
        functools.partial(rotate_kernel, n_modes, n_bands, v_parts, halves),
        grid=(q,),
        in_specs=[
            pl.BlockSpec((1, r, width), lambda a: (a, 0, 0)),
            pl.BlockSpec((1, n_modes, n_modes), lambda a: (a, 0, 0)),
        ],
        out_specs=pl.BlockSpec((v_parts, 1, rows, cols), lambda a: (0, a, 0, 0)),
        out_shape=jax.ShapeDtypeStruct((v_parts, q, rows, cols), BF16),
        compiler_params=VMEM,
        name="rotate_modes",
    )(coupling, rotation)


def prepare_kernel(
    n_bands, n_v, at_once,
    freq_ref, start_ref, kq_ref, points_ref, phase_ref,
    pv_out, bd_out, gauss_out, occ_out,
    eig_scr, en_scr, fl_scr,
):
    g = pl.program_id(0)
    per = 128 // n_bands
    k_all = points_ref.shape[0]
    k_loc = phase_ref.shape[1]
    n_r = phase_ref.shape[0]
    at_en = points_ref.shape[1] - 128
    n_vg = fl_scr.shape[1] // 128
    scale = 1.0 / (SIGMA * math.sqrt(2.0))
    lane = iota((1, 128), 1)
    roll = lambda x, shift: pltpu.roll(x, shift % 128, 1) if shift % 128 else x

    @pl.when(g == 0)
    def _():
        en = points_ref[:, at_en:].astype(F32)
        lim = en[:, 3 * n_bands : 3 * n_bands + 1]
        level = en + roll(en, -n_bands) + roll(en, -2 * n_bands)
        en_scr[...] = jnp.where(lane < n_bands, level, 0.0)
        keep = lane.astype(F32) < jnp.minimum(lim, float(n_bands))
        for i in range(n_bands):
            lo = i * n_bands
            tile = lo // 128 * 128
            block = roll(points_ref[:, tile : tile + 128].astype(F32), tile - lo)
            if lo + n_bands > tile + 128:
                more = roll(points_ref[:, tile + 128 : tile + 256].astype(F32), tile - lo)
                block = jnp.where(lane < tile + 128 - lo, block, more)
            eig_scr[pl.ds(i, k_all, stride=n_bands), :] = jnp.where(keep, block, 0.0)
        for vg in range(n_vg):
            row = jnp.zeros((1, 128), F32)
            for x in range(min(per, n_v - vg * per)):
                row = jnp.where(lane // n_bands == x, freq_ref[0, vg * per + x], row)
            fl_scr[0:1, vg * 128 : (vg + 1) * 128] = row

    for step in range(at_once):
        t = g * at_once + step
        first = t * 2 * per
        c = iota((1, 256), 1)
        k_lane = first + c // 128 * per + c % 128 // n_bands
        k_lane = jnp.where((c % 128 < per * n_bands) & (k_lane < k_loc), k_lane, -1)
        spread = (iota((k_loc, 256), 0) == k_lane).astype(BF16)
        pv_out[step, :n_r, :] = jnp.dot(phase_ref[...], spread, preferred_element_type=F32).astype(BF16)
        v_tiles = []
        for kg in range(2):
            vl = None
            level = None
            diagonal = []
            far_rows = []
            for x in range(per):
                k = jnp.minimum(first + kg * per + x, k_loc - 1)
                near = k + start_ref[0]
                far = kq_ref[0, k]
                v = roll(eig_scr[pl.ds(pl.multiple_of(far * n_bands, 8), n_bands), :], n_bands * x)
                u = roll(eig_scr[pl.ds(pl.multiple_of(near * n_bands, 8), n_bands), :], n_bands * x)
                e = roll(en_scr[pl.ds(near, 1), :], n_bands * x)
                vl = v if vl is None else vl + v
                level = e if level is None else level + e
                diagonal.append(u)
                far_rows.append(en_scr[pl.ds(far, 1), :])
            v_tiles.append(vl)
            diagonal.append(jnp.zeros((128 - per * n_bands, 128), F32))
            bd_out[step, kg] = jnp.concatenate(diagonal, axis=0).T.astype(BF16)
            occ = jax.nn.sigmoid(-level / THERMAL_ENERGY_KT)
            near_level = jnp.broadcast_to(level * scale, (128, 128)).T
            near_occ = jnp.broadcast_to(occ, (128, 128)).T
            far_e = jnp.concatenate(far_rows + [jnp.zeros((8 - per, 128), F32)], axis=0)
            far_e = sum((roll(far_e, n_bands * x) for x in range(1, per)), far_e)
            far_occ = jax.nn.sigmoid(-far_e / THERMAL_ENERGY_KT)
            for x in range(per):
                here = slice(x * n_bands, (x + 1) * n_bands)
                rows = slice(kg * 128 + x * n_bands, kg * 128 + (x + 1) * n_bands)
                occ_out[step, rows, :] = near_occ[here] - roll(far_occ[x : x + 1], n_bands * x)
                for vg in range(n_vg):
                    cols = slice(vg * 128, (vg + 1) * 128)
                    sh = (far_e[x : x + 1] - fl_scr[0:1, cols]) * scale
                    sh = roll(jnp.where(lane < per * n_bands, sh, 1e4), n_bands * x)
                    d = sh - near_level[here]
                    gauss_out[step, rows, cols] = jnp.exp(-(d * d)).astype(BF16)
        pv_out[step, n_r:, :] = jnp.concatenate(v_tiles, axis=1).astype(BF16)


def steps_of(k_loc, n_bands):
    tiles = -(-k_loc // (128 // n_bands * 2))
    return tiles, -(-(tiles + 1) // UNROLL)


def prepare(freq, start, kq, points, phase, n_bands, n_v):
    per = 128 // n_bands
    k_loc = phase.shape[1]
    at_once = UNROLL
    tiles = steps_of(k_loc, n_bands)[1] * at_once
    n_vg = -(-n_v // per)
    k_all = points.shape[0]
    n_pv = phase.shape[0] + n_bands
    whole = lambda x: pl.BlockSpec(x.shape, lambda g: (0,) * x.ndim)
    smem = pl.BlockSpec(memory_space=pltpu.SMEM)
    return pl.pallas_call(
        functools.partial(prepare_kernel, n_bands, n_v, at_once),
        grid=(tiles // at_once,),
        in_specs=[smem, smem, smem, pl.BlockSpec(memory_space=pltpu.VMEM), whole(phase)],
        out_specs=[
            pl.BlockSpec((at_once, n_pv, 256), lambda g: (g, 0, 0)),
            pl.BlockSpec((at_once, 2, 128, 128), lambda g: (g, 0, 0, 0)),
            pl.BlockSpec((at_once, 256, n_vg * 128), lambda g: (g, 0, 0)),
            pl.BlockSpec((at_once, 256, 128), lambda g: (g, 0, 0)),
        ],
        out_shape=[
            pltpu.HBM((tiles, n_pv, 256), BF16),
            pltpu.HBM((tiles, 2, 128, 128), BF16),
            pltpu.HBM((tiles, 256, n_vg * 128), BF16),
            pltpu.HBM((tiles, 256, 128), F32),
        ],
        scratch_shapes=[
            pltpu.VMEM((k_all * n_bands, 128), F32),
            pltpu.VMEM((k_all, 128), F32),
            pltpu.VMEM((1, n_vg * 128), F32),
        ],
        compiler_params=VMEM,
        name="prepare",
    )(freq, start, kq, points, phase)


def lane_ranges(n_bands):
    per = 128 // n_bands
    lane = iota((n_bands, 128), 1)
    inside = []
    for d in range(2 * per - 1):
        lo = n_bands * d % 128
        hi = lo + n_bands
        inside.append(
            (lane >= lo) & (lane < hi) if hi <= 128 else (lane >= lo) | (lane < hi - 128)
        )
    return inside


def swap_blocks(t_ref, kg, n_bands, n_v):
    per = 128 // n_bands
    inside = lane_ranges(n_bands)
    tiles = []
    for first in range(0, n_v, per):
        count = min(per, n_v - first)
        rolled = []
        for x in range(count):
            v = first + x
            block = t_ref[v * n_bands : (v + 1) * n_bands, kg * 128 : (kg + 1) * 128]
            rolled.append(pltpu.roll(block, n_bands * x, 1) if x else block)
        column = []
        for k in range(per):
            mix = rolled[0] if count == per else jnp.where(inside[k], rolled[0], 0.0)
            for x in range(1, count):
                mix = jnp.where(inside[k + x], rolled[x], mix)
            column.append(mix)
        column.append(jnp.zeros((128 - per * n_bands, 128), F32))
        tiles.append(jnp.concatenate(column, axis=0).astype(BF16))
    return jnp.concatenate(tiles, axis=1)


def fill_products(w_ref, pv, n_bands, r):
    n_src = (pv.shape[0] - n_bands) // r
    depth = n_bands * r
    ph, vl = pv[: n_src * r].astype(F32), pv[n_src * r :].astype(F32)
    if r % 8 == 0:
        for i in range(0, n_bands, 2):
            v0 = vl[i : i + 1, :]
            v1 = vl[i + 1 : i + 2, :]
            for s in range(n_src):
                p = ph[s * r : (s + 1) * r, :]
                at = s * depth + i * r
                w_ref[at : at + 2 * r, :] = jnp.concatenate([p * v0, p * v1], axis=0).astype(BF16)
        return
    row = iota((depth, 1), 0)
    by_band = (row // r == iota((depth, n_bands), 1)).astype(BF16)
    v_rows = jnp.dot(by_band, vl.astype(BF16), preferred_element_type=F32)
    for s in range(n_src):
        by_src = (row % r + s * r == iota((depth, n_src * r), 1)).astype(BF16)
        p_rows = jnp.dot(by_src, ph.astype(BF16), preferred_element_type=F32)
        w_ref[s * depth : (s + 1) * depth, :] = (p_rows * v_rows).astype(BF16)


def group_sums(coupled, kg, gauss_ref, occ_ref, n_bands, ph):
    per = 128 // n_bands
    n_vg = coupled.shape[1] // 128
    sums = []
    for k in range(per):
        here = slice(k * n_bands, (k + 1) * n_bands)
        rows = slice(kg * 128 + k * n_bands, kg * 128 + (k + 1) * n_bands)
        occ = occ_ref[0, rows, :]
        el = None
        for vg in range(n_vg):
            c = coupled[here, vg * 128 : (vg + 1) * 128]
            strength = c * c * gauss_ref[0, rows, vg * 128 : (vg + 1) * 128].astype(F32)
            el = strength if el is None else el + strength
            weighed = strength * occ
            weighed = sum(weighed[x : x + 8] for x in range(0, n_bands, 8))
            ph[k][vg] = weighed if ph[k][vg] is None else ph[k][vg] + weighed
        sums.append(el)
    sums.append(jnp.zeros((128 - per * n_bands, 128), F32))
    return jnp.sum(jnp.concatenate(sums, axis=0).T, axis=0, keepdims=True)


def product_and_sums(a_ref, w_ref, t_new, t_old, bd_ref, gauss_ref, occ_ref, ph_scr, scale, n_bands, n_v, fill):
    per = 128 // n_bands
    n_vg = -(-n_v // per)
    ph = [[None] * n_vg for _ in range(per)]
    t_new[...] = jnp.dot(a_ref[...], w_ref[...], preferred_element_type=F32)
    fill()
    right = swap_blocks(t_old, 0, n_bands, n_v)
    c0 = jnp.dot(bd_ref[0, 0], right, preferred_element_type=F32)
    right = swap_blocks(t_old, 1, n_bands, n_v)
    el0 = group_sums(c0, 0, gauss_ref, occ_ref, n_bands, ph)
    c1 = jnp.dot(bd_ref[0, 1], right, preferred_element_type=F32)
    el1 = group_sums(c1, 1, gauss_ref, occ_ref, n_bands, ph)
    for k in range(per):
        for vg in range(n_vg):
            add = ph[k][vg] if scale is None else ph[k][vg] * scale
            ph_scr[k, :, vg * 128 : (vg + 1) * 128] += add
    return [el0, el1]


def linewidth_kernel(n_bands, n_v, halves, r, tiles, k_dev, el_scale, ph_scale, a_ref, *refs):
    refs = list(refs)
    take = lambda n: [refs.pop(0) for _ in range(n)]
    unroll = UNROLL
    sources = take(4)
    (send_out,) = take(1)
    held, (sems,) = take(4), take(1)
    pv_ref, bd_ref, gauss_ref, occ_ref = held
    (a_scr,), w_scr, t_scr, (ph_scr,), (el_scr,) = take(1), take(unroll), take(unroll), take(1), take(1)
    g = pl.program_id(0)
    last = pl.num_programs(0) - 1
    steps = -(-(tiles + 1) // unroll)
    per = 128 // n_bands
    n_src, rows, wide = a_ref.shape
    depth = wide // halves
    n_vg = ph_scr.shape[2] // 128

    def copy(which, step):
        part = pl.ds(step * unroll, unroll)
        return pltpu.make_async_copy(sources[which].at[part], held[which].at[part], sems.at[which, step])

    @pl.when(g == 0)
    def _():
        for which in range(4):
            copy(which, 0).start()
        for step in range(1, steps):
            for which in range(4):
                copy(which, step).start()
        for s in range(n_src):
            block = a_ref[s]
            for h in range(halves):
                a_scr[h * rows : (h + 1) * rows, s * depth : (s + 1) * depth] = block[
                    :, h * depth : (h + 1) * depth
                ]
        t_scr[-1][...] = jnp.zeros_like(t_scr[-1])
        ph_scr[...] = jnp.zeros_like(ph_scr)
        copy(0, 0).wait()
        fill_products(w_scr[0], pv_ref[0], n_bands, r)

    @pl.when(g < last)
    def _():
        copy(0, g + 1).wait()

    for which in range(1, 4):
        copy(which, g).wait()

    def tile_of(ref, n):
        return ref.at[pl.ds(jnp.clip(unroll * g + n, 0, tiles - 1), 1)]

    el = []
    for x in range(unroll):
        beyond = (steps - 1) * unroll + x - 1 >= tiles
        scale = jnp.where(g < last, 1.0, 0.0) if beyond else None
        el += product_and_sums(
            a_scr, w_scr[x], t_scr[x], t_scr[x - 1], tile_of(bd_ref, x - 1), tile_of(gauss_ref, x - 1), tile_of(occ_ref, x - 1),
            ph_scr, scale, n_bands, n_v,
            lambda: fill_products(w_scr[(x + 1) % unroll], tile_of(pv_ref, x + 1)[0], n_bands, r),
        )
    el_scr[pl.ds(g * 8, 8), :] = jnp.concatenate(el + [jnp.zeros((8 - 2 * unroll, 128), F32)], axis=0)

    @pl.when(g == last)
    def _():
        fold = (iota((128, 128), 0) // n_bands == iota((128, 128), 1)).astype(F32)
        rows = []
        for vg in range(n_vg):
            row = jnp.zeros((8, 128), F32)
            for k in range(per):
                tile = ph_scr[k, :, vg * 128 : (vg + 1) * 128]
                row = row + (pltpu.roll(tile, 128 - n_bands * k, 1) if k else tile)
            rows.append(jnp.sum(row, axis=0, keepdims=True))
        sums = jnp.dot(
            jnp.concatenate(rows, axis=0), fold,
            precision=lax.Precision.HIGHEST, preferred_element_type=F32,
        )
        used = per * n_bands
        n_ka, n_pb, n_row, n_rows, _ = send_out.shape
        sums = pltpu.roll(sums * ph_scale, used, 1)
        sums = jnp.concatenate([sums, jnp.zeros((n_rows - n_vg, 128), F32)], axis=0)
        groups = [el_scr[g_ * 8 : g_ * 8 + 2 * unroll, :] for g_ in range(steps)]
        groups = jnp.concatenate(groups + [jnp.zeros((n_rows, 128), F32)], axis=0) * el_scale
        lane = iota((n_rows, 128), 1)
        for d in range(n_ka * n_row):
            lo = 2 + d * k_dev // per
            part = jnp.where(lane < used, groups[lo : lo + n_rows], sums)
            for pb in range(n_pb):
                send_out[d // n_row, pb, d % n_row] = part


def linewidths(a, prepared, k_loc, k_dev, n_row, n_pb, n_bands, n_v, halves, r, el_scale, ph_scale):
    pv, bd, gauss, occ = prepared
    per = 128 // n_bands
    unroll = UNROLL
    tiles, steps = steps_of(k_loc, n_bands)
    n_vg = gauss.shape[2] // 128
    total = (pv.shape[1] - n_bands) * n_bands

    a = pltpu.with_memory_space_constraint(a, pltpu.VMEM)
    tables = [pltpu.with_memory_space_constraint(x, pltpu.HBM) for x in (pv, bd, gauss, occ)]
    n_rows = -(-(-(-(per - 1 + k_dev) // per)) // 8) * 8
    n_ka = k_loc // k_dev // n_row
    return pl.pallas_call(
        functools.partial(
            linewidth_kernel, n_bands, n_v, halves, r, tiles, k_dev, el_scale, ph_scale
        ),
        grid=(steps,),
        in_specs=[pl.BlockSpec(memory_space=pltpu.VMEM)]
        + [pl.BlockSpec(memory_space=pltpu.HBM)] * len(tables),
        out_specs=pl.BlockSpec((n_ka, n_pb, n_row, n_rows, 128), lambda g: (0,) * 5),
        out_shape=jax.ShapeDtypeStruct((n_ka, n_pb, n_row, n_rows, 128), F32),
        scratch_shapes=[pltpu.VMEM(x.shape, x.dtype) for x in tables]
        + [pltpu.SemaphoreType.DMA((len(tables), steps))]
        + [pltpu.VMEM((n_v * n_bands, total), BF16)]
        + [pltpu.VMEM((total, 256), BF16)] * unroll
        + [pltpu.VMEM((n_v * n_bands, 256), F32)] * unroll
        + [pltpu.VMEM((per, 8, n_vg * 128), F32), pltpu.VMEM((steps * 8, 128), F32)],
        compiler_params=VMEM,
        name="linewidths",
    )(a, *tables)


def on_device(coupling, rotation, freq, eigvec, energies, window, kq_index, kpoints, lattice):
    plane = ("ka", "row")
    everywhere = ("ka", "pb", "row")
    n_ka = lax.axis_size("ka")
    n_row = lax.axis_size("row")
    n_pb = lax.axis_size("pb")
    n_group = n_ka * n_row
    k_dev, n_bands = eigvec.shape[:2]
    q_dev, n_modes = rotation.shape[:2]
    assert q_dev == n_row
    pair = n_bands * n_bands
    total_k = k_dev * n_group
    total_q = q_dev * n_pb
    v_parts = math.gcd(n_modes, n_ka)
    k_parts = n_ka // v_parts
    n_v = n_modes // v_parts
    halves = 2 if n_v % 2 == 0 else 1
    k_loc = total_k // k_parts
    ka_pos = lax.axis_index("ka")
    row_pos = lax.axis_index("row")
    pb_pos = lax.axis_index("pb")

    points = pack(eigvec, energies, window, n_group)
    points = lax.all_to_all(points, plane, 0, 0, tiled=True).reshape(total_k, -1)

    pad = -coupling.shape[1] % 8
    if pad:
        coupling = jnp.pad(coupling, ((0, 0), (0, pad), (0, 0)))
    r, r_sent = coupling.shape[1] - pad, coupling.shape[1]
    rotated = rotate(coupling, rotation, n_bands, v_parts, halves)
    if k_parts > 1:
        rotated = jnp.repeat(rotated, k_parts, axis=0)
    rotated = rotated.reshape((n_group,) + rotated.shape[2:])
    a = lax.all_to_all(rotated, plane, 0, 0, tiled=True)
    if pad:
        a = a.reshape(a.shape[:2] + (halves * n_bands, r_sent))[..., :r]
        a = a.reshape(a.shape[:2] + (halves * n_bands * r,))

    k_start = (ka_pos % k_parts) * k_loc
    kp = lax.dynamic_slice_in_dim(kpoints, k_start, k_loc, 0)
    phase = phase_table(lattice, kp)
    kq = lax.dynamic_slice(kq_index, (row_pos, k_start), (1, k_loc))
    v_start = (ka_pos // k_parts) * n_v
    freq_mine = lax.dynamic_slice(freq, (row_pos, v_start), (1, n_v))
    points = pltpu.with_memory_space_constraint(points, pltpu.VMEM)
    prepared = prepare(
        freq_mine, k_start[None], kq, points, phase, n_bands, n_v
    )
    norm = 1.0 / (math.sqrt(2.0 * math.pi) * SIGMA)
    send = linewidths(
        a, prepared, k_loc, k_dev, n_row, n_pb, n_bands, n_v, halves, r,
        norm / (total_q * n_modes * n_bands), norm / (total_k * n_bands),
    )
    if k_parts > 1:
        used = 128 // n_bands * n_bands
        rest = jnp.where(jnp.arange(128) < used, 0.0, send[:1])
        rest = jnp.broadcast_to(rest, (n_ka,) + send.shape[1:])
        send = lax.dynamic_update_slice_in_dim(rest, send, k_start // (k_dev * n_row), 0)
    got = lax.all_to_all(
        send.reshape((n_group * n_pb,) + send.shape[3:]), everywhere, 0, 0, tiled=True
    ).reshape(send.shape)
    n_local = k_loc // k_dev
    first = (ka_pos * n_row + row_pos) % n_local * k_dev % (128 // n_bands)
    place = jnp.stack([pb_pos, first]).astype(jnp.int32)
    electron, phonon = finish(got, place, n_bands, n_v, k_parts, k_dev, n_modes)
    return (electron, phonon)


def solution(mesh):
    return jax.shard_map(
        on_device,
        mesh=mesh,
        in_specs=(
            P("pb", ("ka", "row"), None),
            P("pb", None, None),
            P("pb", None),
            P(("ka", "row"), None, None),
            P(("ka", "row"), None),
            P(("ka", "row")),
            P("pb", None),
            P(),
            P(),
        ),
        out_specs=(P(("ka", "row"), None), P("pb", None)),
        check_vma=False,
    )
```

time: 80.7 us -> 69.6 us (0.86)
  local copies, waits for them, and re-layouts: 10.6 us -> 0.81 us
  Pallas kernels: 38.2 us -> 41.2 us
  waiting for transfers between devices: 15.4 us -> 13.1 us
  other arithmetic: 2.38 us -> 0.39 us
    pallas_call x1 -> x3, Pallas kernels: 9.59 us -> 18.2 us  [the longest x1 15 us: prepare(): pl.pallas_call(functools.partial(prepare_kernel, n_bands, n_v, at_once),...]
    pallas_call x1, Pallas kernels: 22.2 us -> 17.5 us  [linewidths(): pl.pallas_call(functools.partial(linewidth_kernel, n_bands, n_v, halves,...]
    all_to_all x1, waiting for transfers between devices: 5.91 us -> 2.21 us  [on_device(): a = lax.all_to_all(rotated, plane, 0, 0, tiled=True)]
    reshape x7 -> x0, local copies, waits for them, and re-layouts: 3.33 us -> none  [the longest x1 1.04 us: on_device(): mine = [eigvec.reshape(k_dev, pair), jnp.zeros((k_dev, gap), BF16)] + parts]
    unnamed x13 -> x11, local copies, waits for them, and re-layouts: 2.48 us -> 0.03 us
    broadcast_in_dim x8 -> x0, local copies, waits for them, and re-layouts: 1.56 us -> none  [the longest x1 0.77 us: on_device(): jnp.broadcast_to(mine[None], (n_group,) + mine.shape)]
    all_to_all x2, waiting for transfers between devices: 9.46 us -> 10.9 us  [the longest x1 8.12 us: on_device(): lax.all_to_all(send.reshape((n_group * n_pb,) + send.shape[3:]), everywhe...]
    pallas_call x1, Pallas kernels: 6.48 us -> 5.5 us  [rotate(): pl.pallas_call(functools.partial(rotate_kernel, n_modes, n_bands, v_parts...]
  transfers between devices with their start and end apart: 3 -> 3, of which waited for: 3 -> 3; matrix products, arithmetic and copies ran while one was open for 4% -> 2% of each run, Pallas kernels for 20% -> 30%
where the time goes in v3:
time: 69.6 us; the launch traced here: 69.2 us
  Pallas kernels  41.2 us (59%)
  waiting for transfers between devices  13.1 us (19%)
  starting transfers between devices  12.9 us (19%)
  local copies, waits for them, and re-layouts  0.81 us (1%)
  between operations  0.79 us (1%)
    pallas_call x1, Pallas kernels, linewidths(): pl.pallas_call(functools.partial(linewidth_kernel, n_bands, n_v, halves,...  17.5 us
    pallas_call x1, Pallas kernels, prepare(): pl.pallas_call(functools.partial(prepare_kernel, n_bands, n_v, at_once),...  15 us
    all_to_all x1, waiting for transfers between devices, on_device(): lax.all_to_all(send.reshape((n_group * n_pb,) + send.shape[3:]), everywhe...  8.12 us
    pallas_call x1, Pallas kernels, rotate(): pl.pallas_call(functools.partial(rotate_kernel, n_modes, n_bands, v_parts...  5.5 us
    all_to_all x1, starting transfers between devices, on_device(): lax.all_to_all(points, plane, 0, 0, tiled=True).reshape(total_k, -1)  5.17 us
    all_to_all x1, starting transfers between devices, on_device(): lax.all_to_all(send.reshape((n_group * n_pb,) + send.shape[3:]), everywhe...  4.06 us
    all_to_all x1, starting transfers between devices, on_device(): a = lax.all_to_all(rotated, plane, 0, 0, tiled=True)  3.7 us
    all_to_all x1, waiting for transfers between devices, on_device(): lax.all_to_all(points, plane, 0, 0, tiled=True).reshape(total_k, -1)  2.8 us
  transfers between devices with their start and end apart: 3, of which 3 were waited for; matrix products, arithmetic and copies ran while one was open for 2% of the time, Pallas kernels for 30%

profile of v3, /device:TPU:0, one launch (start us, length us, event | category | flops | bytes accessed | tf_op | source)
XLA Modules:
  0.0 69.2 jit_solution(8628762003444167831)
XLA Ops:
  0.6 0.0 copy-start
  0.6 0.0 copy-start.2
  0.7 0.0 copy-start.1
  0.7 1.9 %pack_points.1 = bf16[8,32,768]{2,1,0:T(8,128)(2,1)} custom-call(bf16[24,24,32]{2,1,0:T(8,128)(2,1)} %bitcast.21, f32[24,32]{1,0:T(8,128)} %bitcast.22, s32[1,32]{1,0:T(1,128)} %bitcast.26), custom_call_target="tpu_custom_call" | custom-call | tf_op jit(solution)/shard_map/pack_points/pallas_call | solution.py:56
  2.6 5.2 %all-to-all-start.1 = ((bf16[8,32,768]{2,1,0:T(8,128)(2,1)}), bf16[8,32,768]{2,1,0:T(8,128)(2,1)S(1)}, u32[]{:S(2)}, u32[]{:S(2)}) async-start(bf16[8,32,768]{2,1,0:T(8,128)(2,1)} %pack_points.1), calls=%async_computation.1 | async-start | bytes 786432 | tf_op jit(solution)/shard_map/all_to_all | solution.py:530
  7.7 0.0 copy-done.2
  7.8 0.0 copy-done.1
  7.8 5.5 %rotate_modes.1 = bf16[2,4,216,384]{3,2,1,0:T(8,128)(2,1)} custom-call(bf16[4,8,20736]{2,1,0:T(8,128)(2,1)S(1)} %copy-done.1, bf16[4,36,36]{2,1,0:T(8,128)(2,1)S(1)} %copy.11.rot_ref), custom_call_target="tpu_custom_call" | custom-call | tf_op jit(solution)/shard_map/rotate_modes/pallas_call | solution.py:150
  13.3 2.8 %all-to-all-done.1 = bf16[8,32,768]{2,1,0:T(8,128)(2,1)S(1)} async-done(((bf16[8,32,768]{2,1,0:T(8,128)(2,1)}), bf16[8,32,768]{2,1,0:T(8,128)(2,1)S(1)}, u32[]{:S(2)}, u32[]{:S(2)}) %all-to-all-start.1) | async-done | bytes 393248 | tf_op jit(solution)/shard_map/all_to_all | solution.py:530
  16.1 0.0 copy-start.4
  16.1 0.0 copy-start.3
  16.1 3.7 %all-to-all-start = ((bf16[8,216,384]{2,1,0:T(8,128)(2,1)}), bf16[8,216,384]{2,1,0:T(8,128)(2,1)S(1)}, u32[]{:S(2)}, u32[]{:S(2)}) async-start(bf16[8,216,384]{2,1,0:T(8,128)(2,1)} %bitcast.2), calls=%async_computation | async-start | bytes 2654208 | tf_op jit(solution)/shard_map/all_to_all | solution.py:540
  19.8 0.0 copy-done.4
  19.8 0.8 %dynamic_slice.7.freq_ref = f32[1,18]{1,0:T(1,128)S(1)} dynamic-slice(f32[4,36]{1,0:T(4,128)} %param.11, s32[]{:T(128)S(6)} %select_n.26, s32[]{:T(128)S(6)} %select_n.27), dynamic_slice_sizes={1,18} | dynamic-slice | bytes 148 | tf_op jit(solution)/shard_map/dynamic_slice | solution.py:550
  20.6 0.0 copy-done
  20.6 0.0 copy-done.3
  20.6 0.3 cosine_convert_fusion.phase_ref
  20.9 15.0 %prepare.1 = (bf16[27,88,256]{2,1,0:T(8,128)(2,1)}, bf16[27,2,128,128]{3,2,1,0:T(8,128)(2,1)}, bf16[27,256,512]{2,1,0:T(8,128)(2,1)}, f32[27,256,128]{2,1,0:T(8,128)}) custom-call(f32[1,18]{1,0:T(1,128)S(1)} %dynamic_slice.7.freq_ref, s32[1]{0:T(128)} %constant.64.clone.1.start_ref, s32[1,256]{1,0:T(1,128)S(1)} %constant_dynamic-slice_fusion.kq_ref, ...), custom_call_target="tpu_custom_call" | custom-call | tf_op jit(solution)/shard_map/prepare/pallas_call | solution.py:264
  35.9 2.2 %all-to-all-done.a_ref = bf16[8,216,384]{2,1,0:T(8,128)(2,1)S(1)} async-done(((bf16[8,216,384]{2,1,0:T(8,128)(2,1)}), bf16[8,216,384]{2,1,0:T(8,128)(2,1)S(1)}, u32[]{:S(2)}, u32[]{:S(2)}) %all-to-all-start) | async-done | bytes 1327136 | tf_op jit(solution)/shard_map/all_to_all | solution.py:540
  38.1 17.5 %linewidths.1 = f32[2,4,4,8,128]{4,3,2,1,0:T(8,128)} custom-call(bf16[8,216,384]{2,1,0:T(8,128)(2,1)S(1)} %all-to-all-done.a_ref, bf16[27,88,256]{2,1,0:T(8,128)(2,1)} %get-tuple-element.8.refs_0_, bf16[27,2,128,128]{3,2,1,0:T(8,128)(2,1)} %get-tuple-element.9.refs_1_, bf16[27,256,512]{2,1,0:T(8,128)(2,1)} %get-tuple-element.10.refs_2_, ...), custom_call_target="tpu_custom_call" | custom-call | tf_op jit(solution)/shard_map/linewidths/pallas_call | solution.py:487
  55.6 4.1 %all-to-all-start.2 = ((f32[32,8,128]{2,1,0:T(8,128)}), f32[32,8,128]{2,1,0:T(8,128)S(1)}, u32[]{:S(2)}, u32[]{:S(2)}) async-start(f32[32,8,128]{2,1,0:T(8,128)} %bitcast.13), calls=%async_computation.2 | async-start | bytes 262144 | tf_op jit(solution)/shard_map/all_to_all | solution.py:565
  59.7 0.1 pad_add_fusion.place_ref
  59.8 8.1 %all-to-all-done.2 = f32[32,8,128]{2,1,0:T(8,128)S(1)} async-done(((f32[32,8,128]{2,1,0:T(8,128)}), f32[32,8,128]{2,1,0:T(8,128)S(1)}, u32[]{:S(2)}, u32[]{:S(2)}) %all-to-all-start.2) | async-done | bytes 131104 | tf_op jit(solution)/shard_map/all_to_all | solution.py:565
  67.9 1.3 %finish.1 = (f32[24,32]{1,0:T(8,128)}, f32[4,36]{1,0:T(4,128)}) custom-call(s32[2]{0:T(128)S(1)} %pad_add_fusion.place_ref, f32[2,4,4,8,128]{4,3,2,1,0:T(8,128)S(1)} %bitcast.20), custom_call_target="tpu_custom_call" | custom-call | tf_op jit(solution)/shard_map/finish/pallas_call | solution.py:100
  (5 shorter events, 0.0 us)
Async XLA Ops:
  0.6 19.9 %copy-start = (s32[4,256]{1,0:T(4,128)S(1)}, s32[4,256]{1,0:T(4,128)}, u32[]{:S(2)}) copy-start(s32[4,256]{1,0:T(4,128)} %param.15) | copy-start | bytes 12292
  0.6 7.1 %copy-start.2 = (bf16[4,36,36]{2,0,1:T(4,128)(2,1)S(1)}, bf16[4,36,36]{2,0,1:T(4,128)(2,1)}, u32[]{:S(2)}) copy-start(bf16[4,36,36]{2,0,1:T(4,128)(2,1)} %param.10) | copy-start | bytes 31108
  0.7 7.1 %copy-start.1 = (bf16[4,8,20736]{2,1,0:T(8,128)(2,1)S(1)}, bf16[4,8,20736]{2,1,0:T(8,128)(2,1)}, u32[]{:S(2)}) copy-start(bf16[4,8,20736]{2,1,0:T(8,128)(2,1)} %coup_ref.1) | copy-start | bytes 3981316
  2.6 13.5 %all-to-all-start.1 = ((bf16[8,32,768]{2,1,0:T(8,128)(2,1)}), bf16[8,32,768]{2,1,0:T(8,128)(2,1)S(1)}, u32[]{:S(2)}, u32[]{:S(2)}) async-start(bf16[8,32,768]{2,1,0:T(8,128)(2,1)} %pack_points.1), calls=%async_computation.1 | async-start | bytes 786432 | tf_op jit(solution)/shard_map/all_to_all | solution.py:530
  16.1 3.7 %copy-start.4 = (s32[64,3]{0,1:T(4,128)S(1)}, s32[64,3]{0,1:T(4,128)}, u32[]{:S(2)}) copy-start(s32[64,3]{0,1:T(4,128)} %param.17) | copy-start | bytes 2308
  16.1 4.5 %copy-start.3 = (f32[256,3]{0,1:T(4,128)S(1)}, f32[256,3]{0,1:T(4,128)}, u32[]{:S(2)}) copy-start(f32[256,3]{0,1:T(4,128)} %param.16) | copy-start | bytes 9220
  16.1 22.0 %all-to-all-start = ((bf16[8,216,384]{2,1,0:T(8,128)(2,1)}), bf16[8,216,384]{2,1,0:T(8,128)(2,1)S(1)}, u32[]{:S(2)}, u32[]{:S(2)}) async-start(bf16[8,216,384]{2,1,0:T(8,128)(2,1)} %bitcast.2), calls=%async_computation | async-start | bytes 2654208 | tf_op jit(solution)/shard_map/all_to_all | solution.py:540
  55.6 12.3 %all-to-all-start.2 = ((f32[32,8,128]{2,1,0:T(8,128)}), f32[32,8,128]{2,1,0:T(8,128)S(1)}, u32[]{:S(2)}, u32[]{:S(2)}) async-start(f32[32,8,128]{2,1,0:T(8,128)} %bitcast.13), calls=%async_computation.2 | async-start | bytes 262144 | tf_op jit(solution)/shard_map/all_to_all | solution.py:565

commit v4 on v3

v4 whole, which is shorter than its diff:
```python
import functools
import math

import jax
import jax.numpy as jnp
import numpy as np
from jax import lax
from jax.experimental import pallas as pl
from jax.experimental.pallas import tpu as pltpu
from jax.sharding import PartitionSpec as P

SIGMA = 0.1
THERMAL_ENERGY_KT = 0.2
VMEM = pltpu.CompilerParams(vmem_limit_bytes=40 * 1024 * 1024)
F32 = jnp.float32
BF16 = jnp.bfloat16
UNROLL = 3
K_PER = 4


def phase_rows(lattice, kpoint_rows):
    rvec = lattice.astype(jnp.float32)
    argument = (
        rvec[:, 0][None, :] * kpoint_rows[:, 0:1]
        + rvec[:, 1][None, :] * kpoint_rows[:, 1:2]
        + rvec[:, 2][None, :] * kpoint_rows[:, 2:3]
    )
    return jnp.cos(2.0 * math.pi * argument).astype(jnp.bfloat16)


def iota(shape, dim):
    return lax.broadcasted_iota(jnp.int32, shape, dim)


def pack_kernel(eig_ref, en_ref, window_ref, out_ref):
    n_bands, _, k_dev = eig_ref.shape
    rest = en_ref[...]
    high = rest.astype(BF16).astype(F32)
    rows = [eig_ref[...].astype(F32).reshape(n_bands * n_bands, k_dev), high, rest - high]
    rows.append(window_ref[...].astype(F32))
    rows.append(jnp.zeros((out_ref.shape[2] - n_bands * (n_bands + 2) - 1, k_dev), F32))
    packed = jnp.concatenate(rows, axis=0)
    packed = jnp.concatenate([packed, jnp.zeros((packed.shape[0], 128 - k_dev), F32)], axis=1)
    packed = packed.T[:k_dev].astype(BF16)
    for d in range(out_ref.shape[0]):
        out_ref[d] = packed


def pack(eigvec, energies, window, copies):
    k_dev, n_bands, _ = eigvec.shape
    wide = -(-(n_bands * (n_bands + 2) + 1) // 128) * 128
    args = (eigvec.transpose(1, 2, 0), energies.T, window.reshape(1, k_dev))
    return pl.pallas_call(
        pack_kernel,
        grid=(1,),
        in_specs=[pl.BlockSpec(x.shape, lambda g, n=x.ndim: (0,) * n) for x in args],
        out_specs=pl.BlockSpec(memory_space=pltpu.VMEM),
        out_shape=pltpu.VMEM((copies, k_dev, wide), BF16),
        compiler_params=VMEM,
        name="pack_points",
    )(*[pltpu.with_memory_space_constraint(x, pltpu.HBM) for x in args])


def finish_kernel(n_bands, n_v, k_parts, place_ref, got_ref, el_out, ph_out, scr):
    n_ka, n_pb, n_row, rows, _ = got_ref.shape
    lane = iota((1, 128), 1)
    total = None
    for ka in range(n_ka):
        for pb in range(n_pb):
            for row in range(n_row):
                part = got_ref[ka, pb, row]
                total = part if total is None else total + part
    for x in range(K_PER):
        scr[pl.ds(x, rows, stride=K_PER), :] = pltpu.roll(total, 128 - n_bands * x, 1) if x else total
    k_dev = el_out.shape[1]
    mine = jnp.concatenate([scr[...], jnp.zeros((128 - k_dev, 128), F32)], axis=0)
    el_out[...] = mine.T[:n_bands, :k_dev]
    for row in range(n_row):
        line = jnp.zeros((1, 128), F32)
        for ka in range(n_ka):
            part = got_ref[ka, pl.ds(place_ref[0], 1), row][0]
            to = ka // k_parts * n_v
            moved = pltpu.roll(part[0:1], (to - K_PER * n_bands) % 128, 1)
            line = line + jnp.where((lane >= to) & (lane < to + n_v), moved, 0.0)
        ph_out[row : row + 1, :] = line[:, : ph_out.shape[1]]


def finish(got, place, n_bands, n_v, k_parts, k_dev, n_modes):
    n_row, rows = got.shape[2:4]
    el, ph = pl.pallas_call(
        functools.partial(finish_kernel, n_bands, n_v, k_parts),
        in_specs=[pl.BlockSpec(memory_space=pltpu.SMEM), pl.BlockSpec(memory_space=pltpu.VMEM)],
        out_shape=[
            jax.ShapeDtypeStruct((n_bands, k_dev), F32),
            jax.ShapeDtypeStruct((n_row, n_modes), F32),
        ],
        scratch_shapes=[pltpu.VMEM((rows * K_PER, 128), F32)],
        compiler_params=VMEM,
        name="finish",
    )(place, pltpu.with_memory_space_constraint(got, pltpu.VMEM))
    return el.T, ph


def rotate_kernel(n_modes, n_bands, v_parts, coup_ref, rot_ref, out_ref):
    r = coup_ref.shape[1]
    pair = n_bands * n_bands
    rows = n_modes * r
    x = coup_ref[0].astype(F32)
    x = jnp.concatenate([x[:, c * pair : (c + 1) * pair] for c in range(n_modes)], axis=0).astype(BF16)
    rot = rot_ref[...].astype(F32)
    rot = jnp.sum(jnp.where(iota(rot.shape, 1) == pl.program_id(0), rot, 0.0), axis=1).astype(BF16)
    spread_v = (iota((rows, n_modes), 0) // r == iota((rows, n_modes), 1)).astype(BF16)
    spread_c = (iota((n_modes, rows), 1) // r == iota((n_modes, rows), 0)).astype(BF16)
    half = lax.dot_general(spread_v, rot, (((1,), (1,)), ((), ())), preferred_element_type=F32)
    full = jnp.dot(half.astype(BF16), spread_c, preferred_element_type=F32)
    same = iota((rows, rows), 0) % r == iota((rows, rows), 1) % r
    big = jnp.where(same, full, 0.0).astype(BF16)
    y = jnp.dot(big, x, preferred_element_type=F32)
    n_v = n_modes // v_parts
    half_i = n_bands // 2
    wide = out_ref.shape[3]
    for part in range(v_parts):
        pieces = []
        for i in range(half_i):
            block = [
                y[v * r : (v + 1) * r, x * n_bands : (x + 1) * n_bands]
                for x in (i, i + half_i)
                for v in range(part * n_v, (part + 1) * n_v)
            ]
            if wide > 2 * n_v * n_bands:
                block.append(jnp.zeros((r, wide - 2 * n_v * n_bands), F32))
            pieces.append(jnp.concatenate(block, axis=1))
        out_ref[part, 0] = jnp.concatenate(pieces, axis=0).astype(BF16)


def rotate(coupling, rotation, n_bands, v_parts):
    q, r, width = coupling.shape
    n_modes = rotation.shape[1]
    rows = n_bands // 2 * r
    cols = -(-(2 * n_modes // v_parts * n_bands) // 128) * 128
    return pl.pallas_call(
        functools.partial(rotate_kernel, n_modes, n_bands, v_parts),
        grid=(q,),
        in_specs=[
            pl.BlockSpec((1, r, width), lambda a: (a, 0, 0)),
            pl.BlockSpec((n_modes, q, n_modes), lambda a: (0, 0, 0)),
        ],
        out_specs=pl.BlockSpec((v_parts, 1, rows, cols), lambda a: (0, a, 0, 0)),
        out_shape=jax.ShapeDtypeStruct((v_parts, q, rows, cols), BF16),
        compiler_params=VMEM,
        name="rotate_modes",
    )(
        pltpu.with_memory_space_constraint(coupling, pltpu.HBM),
        pltpu.with_memory_space_constraint(rotation.transpose(1, 0, 2), pltpu.HBM),
    )


def steps_of(k_loc):
    tiles = k_loc // (2 * K_PER)
    return tiles, -(-(tiles + 1) // UNROLL)


def prepare_kernel(
    n_bands, n_v, k_loc,
    freq_ref, start_ref, kq_ref, points_ref,
    wt_out, bd_out, gauss_out, occ_out,
    eig_scr, en_scr, keep_scr,
):
    g = pl.program_id(0)
    used = K_PER * n_bands
    k_all = points_ref.shape[0]
    at_en = points_ref.shape[1] - 128
    slots = 2 * K_PER
    scale = 1.0 / (SIGMA * math.sqrt(2.0))
    lane = iota((1, 128), 1)
    roll = lambda x, shift: pltpu.roll(x, shift % 128, 1) if shift % 128 else x

    @pl.when(g == 0)
    def _():
        en = roll(points_ref[:, at_en:].astype(F32), -(n_bands * n_bands % 128))
        lim = en[:, 2 * n_bands : 2 * n_bands + 1]
        en_scr[...] = jnp.where(lane < n_bands, en + roll(en, -n_bands), 0.0)
        keep = lane.astype(F32) < jnp.minimum(lim, float(n_bands))
        for i in range(n_bands):
            lo = i * n_bands
            tile = lo // 128 * 128
            block = roll(points_ref[:, tile : tile + 128].astype(F32), tile - lo)
            if lo + n_bands > tile + 128:
                more = roll(points_ref[:, tile + 128 : tile + 256].astype(F32), tile - lo)
                block = jnp.where(lane < tile + 128 - lo, block, more)
            eig_scr[pl.ds(i, k_all, stride=n_bands), :] = jnp.where(keep, block, 0.0)
        shape = (slots * n_bands, slots * n_bands)
        keep_scr[...] = (iota(shape, 0) // n_bands == iota(shape, 1) % slots).astype(BF16)

    by_band = (iota((n_bands, slots * n_bands), 0) == iota((n_bands, slots * n_bands), 1) // slots).astype(BF16)
    for step in range(UNROLL):
        t = g * UNROLL + step
        first = jnp.minimum(t * slots, k_loc - slots)
        v_tiles = []
        blocks = []
        for kg in range(2):
            vl = None
            level = None
            diagonal = []
            far_rows = []
            for x in range(K_PER):
                k = first + kg * K_PER + x
                near = k + start_ref[0]
                far = kq_ref[0, k]
                v = roll(eig_scr[pl.ds(pl.multiple_of(far * n_bands, 8), n_bands), :], n_bands * x)
                u = roll(eig_scr[pl.ds(pl.multiple_of(near * n_bands, 8), n_bands), :], n_bands * x)
                e = roll(en_scr[pl.ds(near, 1), :], n_bands * x)
                vl = v if vl is None else vl + v
                level = e if level is None else level + e
                diagonal.append(u)
                far_rows.append(jnp.broadcast_to(en_scr[pl.ds(far, 1), :], (n_bands, 128)))
            v_tiles.append(vl)
            blocks.append(jnp.concatenate(diagonal + [jnp.zeros((128 - used, 128), F32)], axis=0))
            cols = slice(kg * 128, (kg + 1) * 128)
            far_e = jnp.concatenate(far_rows + [jnp.zeros((128 - used, 128), F32)], axis=0).T[:n_bands]
            occ_out[step, :, cols] = jax.nn.sigmoid(-level / THERMAL_ENERGY_KT) - jax.nn.sigmoid(
                -far_e / THERMAL_ENERGY_KT
            )
            base = (far_e - level) * scale
            for v in range(0, n_v, 2):
                both = []
                for x in range(v, min(v + 2, n_v)):
                    d = base - freq_ref[0, x] * scale
                    both.append(jnp.exp(-(d * d)))
                rows = slice(v * n_bands, (v + len(both)) * n_bands)
                gauss_out[step, rows, cols] = jnp.concatenate(both, axis=0).astype(BF16)
        zero = jnp.zeros((128, 128), F32)
        bd_out[step, :128, :] = jnp.concatenate([blocks[0], zero], axis=1).astype(BF16)
        bd_out[step, 128:, :] = jnp.concatenate([zero, blocks[1]], axis=1).astype(BF16)
        vl = jnp.concatenate(v_tiles, axis=1).astype(BF16)
        wt = lax.dot_general(vl, by_band, (((0,), (0,)), ((), ())), preferred_element_type=F32)
        wt = jnp.concatenate([wt[:used], wt[128 : 128 + used]], axis=0)
        wt_out[step] = wt.astype(BF16) * keep_scr[...]


def prepare(freq, start, kq, points, n_bands, n_v):
    k_loc = kq.shape[1]
    steps = steps_of(k_loc)[1]
    tiles = steps * UNROLL
    k_all = points.shape[0]
    wide = 2 * K_PER * n_bands
    smem = pl.BlockSpec(memory_space=pltpu.SMEM)
    shapes = ((wide, wide), (256, 256), (n_v * n_bands, 256), (n_bands, 256))
    types = (BF16, BF16, BF16, F32)
    return pl.pallas_call(
        functools.partial(prepare_kernel, n_bands, n_v, k_loc),
        grid=(steps,),
        in_specs=[smem, smem, smem, pl.BlockSpec(memory_space=pltpu.VMEM)],
        out_specs=[pl.BlockSpec((UNROLL,) + x, lambda g: (g, 0, 0)) for x in shapes],
        out_shape=[pltpu.HBM((tiles,) + x, t) for x, t in zip(shapes, types)],
        scratch_shapes=[
            pltpu.VMEM((k_all * n_bands, 128), F32),
            pltpu.VMEM((k_all, 128), F32),
            pltpu.VMEM((wide, wide), BF16),
        ],
        compiler_params=VMEM,
        name="prepare",
    )(freq, start, kq, points)


def swap_blocks(t_ref, n_bands, n_v):
    v_per = 128 // n_bands
    lane = iota((n_bands, 128), 1)
    inside = []
    for d in range(v_per + K_PER - 1):
        lo = n_bands * d % 128
        hi = lo + n_bands
        inside.append(
            (lane >= lo) & (lane < hi) if hi <= 128 else (lane >= lo) | (lane < hi - 128)
        )
    halves = []
    for kg in range(2):
        column = []
        for first in range(0, n_v, v_per):
            vg = first // v_per
            rolled = []
            for k in range(K_PER):
                row = (kg * K_PER + k) * n_bands
                block = t_ref[row : row + n_bands, vg * 128 : (vg + 1) * 128]
                rolled.append(pltpu.roll(block, n_bands * k, 1) if k else block)
            for v in range(min(v_per, n_v - first)):
                mix = rolled[0]
                for k in range(1, K_PER):
                    mix = jnp.where(inside[v + k], rolled[k], mix)
                column.append(pltpu.roll(mix, 128 - n_bands * v, 1) if v else mix)
        halves.append(jnp.concatenate(column, axis=0).astype(BF16))
    return jnp.concatenate(halves, axis=1)


def tile_step(wt_ref, b_ref, t_new, t_old, bd_ref, gauss_ref, occ_ref, ph_scr, scale, n_bands, n_v):
    t_new[...] = jnp.dot(wt_ref[0], b_ref[0], preferred_element_type=F32)
    left = swap_blocks(t_old, n_bands, n_v)
    coupled = jnp.dot(left, bd_ref[0], preferred_element_type=F32)
    occ = occ_ref[0]
    el = None
    for v in range(0, n_v, 2):
        count = min(2, n_v - v)
        gauss = gauss_ref[0, v * n_bands : (v + count) * n_bands, :].astype(F32)
        for x in range(count):
            c = coupled[(v + x) * n_bands : (v + x + 1) * n_bands]
            strength = c * c * gauss[x * n_bands : (x + 1) * n_bands]
            el = strength if el is None else el + strength
            weighed = strength * occ
            weighed = sum(weighed[z : z + 8] for z in range(0, n_bands, 8))
            weighed = weighed[:, :128] + weighed[:, 128:]
            ph_scr[v + x] += weighed if scale is None else weighed * scale
    el = jnp.sum(el, axis=0, keepdims=True)
    return [el[:, :128], el[:, 128:]]


def linewidth_kernel(n_bands, n_v, r, tiles, k_dev, el_scale, ph_scale, a_ref, phase_ref, *refs):
    refs = list(refs)
    take = lambda n: [refs.pop(0) for _ in range(n)]
    unroll = UNROLL
    sources = take(4)
    (send_out,) = take(1)
    held, (sems,) = take(4), take(1)
    wt_ref, bd_ref, gauss_ref, occ_ref = held
    (a_scr, b_scr, ph_scr, el_scr), t_scr = take(4), take(unroll)
    g = pl.program_id(0)
    last = pl.num_programs(0) - 1
    steps = -(-(tiles + 1) // unroll)
    n_src = a_ref.shape[0]
    half_i = n_bands // 2
    v_per = 128 // n_bands
    cols = n_v * n_bands
    slots = 2 * K_PER

    def copy(which, step):
        part = pl.ds(step * unroll, unroll)
        return pltpu.make_async_copy(sources[which].at[part], held[which].at[part], sems.at[which, step])

    @pl.when(g == 0)
    def _():
        for step in range(steps):
            for which in range(4):
                copy(which, step).start()
        lane = iota((1, 128), 1)
        for s in range(0, n_src, 2):
            for h in range(2):
                for vg in range(-(-n_v // v_per)):
                    lo = h * cols + vg * v_per * n_bands
                    tile, off = lo // 128 * 128, lo % 128
                    both = []
                    for x in (s, s + 1):
                        block = a_ref[x, :, tile : tile + 128].astype(F32)
                        if off:
                            block = pltpu.roll(block, 128 - off, 1)
                            if tile + 128 < a_ref.shape[2]:
                                more = a_ref[x, :, tile + 128 : tile + 256].astype(F32)
                                block = jnp.where(lane < 128 - off, block, pltpu.roll(more, 128 - off, 1))
                        both.append(block)
                    for i in range(half_i):
                        here = slice(i * r, (i + 1) * r)
                        a_scr[h * half_i + i, s * r : (s + 2) * r, vg * 128 : (vg + 1) * 128] = (
                            jnp.concatenate([both[0][here], both[1][here]], axis=0).astype(BF16)
                        )
        for i in range(0, n_bands, 2):
            b0 = jnp.dot(phase_ref[...], a_scr[i], preferred_element_type=F32)
            b1 = jnp.dot(phase_ref[...], a_scr[i + 1], preferred_element_type=F32)
            for t in range(tiles):
                here = slice(t * slots, (t + 1) * slots)
                b_scr[t, i * slots : (i + 2) * slots, :] = jnp.concatenate(
                    [b0[here], b1[here]], axis=0
                ).astype(BF16)
        t_scr[-1][...] = jnp.zeros_like(t_scr[-1])
        ph_scr[...] = jnp.zeros_like(ph_scr)

    for which in range(4):
        copy(which, g).wait()

    def tile_of(ref, n):
        return ref.at[pl.ds(jnp.clip(unroll * g + n, 0, tiles - 1), 1)]

    el = []
    for x in range(unroll):
        beyond = (steps - 1) * unroll + x - 1 >= tiles
        scale = jnp.where(g < last, 1.0, 0.0) if beyond else None
        el += tile_step(
            tile_of(wt_ref, x), tile_of(b_scr, x), t_scr[x], t_scr[x - 1], tile_of(bd_ref, x - 1),
            tile_of(gauss_ref, x - 1), tile_of(occ_ref, x - 1), ph_scr, scale, n_bands, n_v,
        )
    el_scr[pl.ds(g * 8, 8), :] = jnp.concatenate(el + [jnp.zeros((8 - 2 * unroll, 128), F32)], axis=0)

    @pl.when(g == last)
    def _():
        used = K_PER * n_bands
        n_ka, n_pb, n_row, n_rows, _ = send_out.shape
        sums = jnp.sum(ph_scr[...], axis=1)
        sums = jnp.concatenate([sums, jnp.zeros((128 - n_v, 128), F32)], axis=0).T
        sums = pltpu.roll(jnp.sum(sums, axis=0, keepdims=True) * ph_scale, used, 1)
        groups = [el_scr[x * 8 : x * 8 + 2 * unroll, :] for x in range(steps)]
        groups = jnp.concatenate(groups, axis=0) * el_scale
        lane = iota((n_rows, 128), 1)
        for d in range(n_ka * n_row):
            lo = 2 + d * n_rows
            part = jnp.where(lane < used, groups[lo : lo + n_rows], sums)
            for pb in range(n_pb):
                send_out[d // n_row, pb, d % n_row] = part


def linewidths(a, phase, prepared, k_loc, k_dev, n_row, n_pb, n_bands, n_v, r, el_scale, ph_scale):
    wt, bd, gauss, occ = prepared
    tiles, steps = steps_of(k_loc)
    lanes = -(-n_v // (128 // n_bands)) * 128
    wide = 2 * K_PER * n_bands
    depth = a.shape[0] * r
    a = pltpu.with_memory_space_constraint(a, pltpu.VMEM)
    tables = [pltpu.with_memory_space_constraint(x, pltpu.HBM) for x in (wt, bd, gauss, occ)]
    n_rows = k_dev // K_PER
    n_ka = k_loc // k_dev // n_row
    return pl.pallas_call(
        functools.partial(linewidth_kernel, n_bands, n_v, r, tiles, k_dev, el_scale, ph_scale),
        grid=(steps,),
        in_specs=[pl.BlockSpec(memory_space=pltpu.VMEM)] * 2
        + [pl.BlockSpec(memory_space=pltpu.HBM)] * len(tables),
        out_specs=pl.BlockSpec((n_ka, n_pb, n_row, n_rows, 128), lambda g: (0,) * 5),
        out_shape=jax.ShapeDtypeStruct((n_ka, n_pb, n_row, n_rows, 128), F32),
        scratch_shapes=[pltpu.VMEM(x.shape, x.dtype) for x in tables]
        + [pltpu.SemaphoreType.DMA((len(tables), steps))]
        + [
            pltpu.VMEM((n_bands, depth, lanes), BF16),
            pltpu.VMEM((tiles, wide, lanes), BF16),
            pltpu.VMEM((n_v, 8, 128), F32),
            pltpu.VMEM((steps * 8, 128), F32),
        ]
        + [pltpu.VMEM((wide, lanes), F32)] * UNROLL,
        compiler_params=VMEM,
        name="linewidths",
    )(a, phase, *tables)


def on_device(coupling, rotation, freq, eigvec, energies, window, kq_index, kpoints, lattice):
    plane = ("ka", "row")
    everywhere = ("ka", "pb", "row")
    n_ka = lax.axis_size("ka")
    n_row = lax.axis_size("row")
    n_pb = lax.axis_size("pb")
    n_group = n_ka * n_row
    k_dev, n_bands = eigvec.shape[:2]
    q_dev, n_modes = rotation.shape[:2]
    assert q_dev == n_row
    pair = n_bands * n_bands
    total_k = k_dev * n_group
    total_q = q_dev * n_pb
    v_parts = math.gcd(n_modes, n_ka)
    k_parts = n_ka // v_parts
    n_v = n_modes // v_parts
    k_loc = total_k // k_parts
    ka_pos = lax.axis_index("ka")
    row_pos = lax.axis_index("row")
    pb_pos = lax.axis_index("pb")

    points = pack(eigvec, energies, window, n_group)
    points = lax.all_to_all(points, plane, 0, 0, tiled=True).reshape(total_k, -1)

    pad = -coupling.shape[1] % 8
    if pad:
        coupling = jnp.pad(coupling, ((0, 0), (0, pad), (0, 0)))
    r = coupling.shape[1]
    rotated = rotate(coupling, rotation, n_bands, v_parts)
    if k_parts > 1:
        rotated = jnp.repeat(rotated, k_parts, axis=0)
    rotated = rotated.reshape((n_group,) + rotated.shape[2:])
    a = lax.all_to_all(rotated, plane, 0, 0, tiled=True)
    k_start = (ka_pos % k_parts) * k_loc
    kp = lax.dynamic_slice_in_dim(kpoints, k_start, k_loc, 0)
    phase = phase_rows(lattice, kp)
    if pad:
        phase = jnp.pad(phase.reshape(k_loc, n_group, r - pad), ((0, 0), (0, 0), (0, pad)))
        phase = phase.reshape(k_loc, n_group * r)
    kq = lax.dynamic_slice(kq_index, (row_pos, k_start), (1, k_loc))
    v_start = (ka_pos // k_parts) * n_v
    freq_mine = lax.dynamic_slice(freq, (row_pos, v_start), (1, n_v))
    points = pltpu.with_memory_space_constraint(points, pltpu.VMEM)
    prepared = prepare(freq_mine, k_start[None], kq, points, n_bands, n_v)
    norm = 1.0 / (math.sqrt(2.0 * math.pi) * SIGMA)
    send = linewidths(
        a, phase, prepared, k_loc, k_dev, n_row, n_pb, n_bands, n_v, r,
        norm / (total_q * n_modes * n_bands), norm / (total_k * n_bands),
    )
    if k_parts > 1:
        used = K_PER * n_bands
        rest = jnp.where(jnp.arange(128) < used, 0.0, send[:1])
        rest = jnp.broadcast_to(rest, (n_ka,) + send.shape[1:])
        send = lax.dynamic_update_slice_in_dim(rest, send, k_start // (k_dev * n_row), 0)
    got = lax.all_to_all(
        send.reshape((n_group * n_pb,) + send.shape[3:]), everywhere, 0, 0, tiled=True
    ).reshape(send.shape)
    place = pb_pos[None].astype(jnp.int32)
    electron, phonon = finish(got, place, n_bands, n_v, k_parts, k_dev, n_modes)
    return (electron, phonon)


def solution(mesh):
    return jax.shard_map(
        on_device,
        mesh=mesh,
        in_specs=(
            P("pb", ("ka", "row"), None),
            P("pb", None, None),
            P("pb", None),
            P(("ka", "row"), None, None),
            P(("ka", "row"), None),
            P(("ka", "row")),
            P("pb", None),
            P(),
            P(),
        ),
        out_specs=(P(("ka", "row"), None), P("pb", None)),
        check_vma=False,
    )
```

time: 69.6 us -> 64.8 us (0.931)
  Pallas kernels: 41.2 us -> 35.1 us
  waiting for transfers between devices: 13.1 us -> 14.4 us
    pallas_call x2, Pallas kernels: 32.4 us -> 26.3 us  [the longest x1 13.7 us: linewidths(): pl.pallas_call(functools.partial(linewidth_kernel, n_bands, n_v, r, tiles...]
    all_to_all x1, waiting for transfers between devices: 2.21 us -> 4.82 us  [on_device(): a = lax.all_to_all(rotated, plane, 0, 0, tiled=True)]
    all_to_all x1, waiting for transfers between devices: 2.8 us -> 1.4 us  [on_device(): lax.all_to_all(points, plane, 0, 0, tiled=True).reshape(total_k, -1)]
    pallas_call x1, Pallas kernels: 5.5 us -> 6.24 us  [rotate(): pl.pallas_call(functools.partial(rotate_kernel, n_modes, n_bands, v_parts...]
  transfers between devices with their start and end apart: 3 -> 3, of which waited for: 3 -> 3; matrix products, arithmetic and copies ran while one was open for 2% -> 2% of each run, Pallas kernels for 30% -> 29%
where the time goes in v4:
time: 64.8 us; the launch traced here: 64.4 us
  Pallas kernels  35.1 us (54%)
  waiting for transfers between devices  14.4 us (22%)
  starting transfers between devices  12.7 us (20%)
  local copies, waits for them, and re-layouts  0.8 us (1%)
  between operations  0.73 us (1%)
    pallas_call x1, Pallas kernels, linewidths(): pl.pallas_call(functools.partial(linewidth_kernel, n_bands, n_v, r, tiles...  13.7 us
    pallas_call x1, Pallas kernels, prepare(): pl.pallas_call(functools.partial(prepare_kernel, n_bands, n_v, k_loc), gr...  12.7 us
    all_to_all x1, waiting for transfers between devices, on_device(): lax.all_to_all(send.reshape((n_group * n_pb,) + send.shape[3:]), everywhe...  8.22 us
    pallas_call x1, Pallas kernels, rotate(): pl.pallas_call(functools.partial(rotate_kernel, n_modes, n_bands, v_parts...  6.24 us
    all_to_all x1, starting transfers between devices, on_device(): lax.all_to_all(points, plane, 0, 0, tiled=True).reshape(total_k, -1)  5.17 us
    all_to_all x1, waiting for transfers between devices, on_device(): a = lax.all_to_all(rotated, plane, 0, 0, tiled=True)  4.82 us
    all_to_all x1, starting transfers between devices, on_device(): lax.all_to_all(send.reshape((n_group * n_pb,) + send.shape[3:]), everywhe...  4 us
    all_to_all x1, starting transfers between devices, on_device(): a = lax.all_to_all(rotated, plane, 0, 0, tiled=True)  3.57 us
  transfers between devices with their start and end apart: 3, of which 3 were waited for; matrix products, arithmetic and copies ran while one was open for 2% of the time, Pallas kernels for 29%

profile of v4, /device:TPU:0, one launch (start us, length us, event | category | flops | bytes accessed | tf_op | source)
XLA Modules:
  0.0 64.4 jit_solution(14269078287689485361)
XLA Ops:
  0.6 0.0 copy-start
  0.6 0.0 copy-start.2
  0.7 0.0 copy-start.1
  0.7 1.8 %pack_points.1 = bf16[8,32,640]{2,1,0:T(8,128)(2,1)} custom-call(bf16[24,24,32]{2,1,0:T(8,128)(2,1)} %bitcast.21, f32[24,32]{1,0:T(8,128)} %bitcast.23, s32[1,32]{1,0:T(1,128)} %bitcast.27), custom_call_target="tpu_custom_call" | custom-call | tf_op jit(solution)/shard_map/pack_points/pallas_call | solution.py:53
  2.4 5.2 %all-to-all-start.1 = ((bf16[8,32,640]{2,1,0:T(8,128)(2,1)}), bf16[8,32,640]{2,1,0:T(8,128)(2,1)S(1)}, u32[]{:S(2)}, u32[]{:S(2)}) async-start(bf16[8,32,640]{2,1,0:T(8,128)(2,1)} %pack_points.1), calls=%async_computation.1 | async-start | bytes 655360 | tf_op jit(solution)/shard_map/all_to_all | solution.py:460
  7.6 6.2 %rotate_modes.1 = bf16[2,4,96,896]{3,2,1,0:T(8,128)(2,1)} custom-call(bf16[4,8,20736]{2,1,0:T(8,128)(2,1)} %coup_ref.1, bf16[36,4,36]{2,1,0:T(4,128)(2,1)} %bitcast.22), custom_call_target="tpu_custom_call" | custom-call | tf_op jit(solution)/shard_map/rotate_modes/pallas_call | solution.py:141
  13.8 1.4 %all-to-all-done.1 = bf16[8,32,640]{2,1,0:T(8,128)(2,1)S(1)} async-done(((bf16[8,32,640]{2,1,0:T(8,128)(2,1)}), bf16[8,32,640]{2,1,0:T(8,128)(2,1)S(1)}, u32[]{:S(2)}, u32[]{:S(2)}) %all-to-all-start.1) | async-done | bytes 327712 | tf_op jit(solution)/shard_map/all_to_all | solution.py:460
  15.2 3.6 %all-to-all-start = ((bf16[8,96,896]{2,1,0:T(8,128)(2,1)}), bf16[8,96,896]{2,1,0:T(8,128)(2,1)S(1)}, u32[]{:S(2)}, u32[]{:S(2)}) async-start(bf16[8,96,896]{2,1,0:T(8,128)(2,1)} %bitcast.2), calls=%async_computation | async-start | bytes 2752512 | tf_op jit(solution)/shard_map/all_to_all | solution.py:470
  18.8 0.0 copy-done.2
  18.8 0.8 %dynamic_slice.7.freq_ref = f32[1,18]{1,0:T(1,128)S(1)} dynamic-slice(f32[4,36]{1,0:T(4,128)} %param.11, s32[]{:T(128)S(6)} %select_n.16, s32[]{:T(128)S(6)} %select_n.17), dynamic_slice_sizes={1,18} | dynamic-slice | bytes 148 | tf_op jit(solution)/shard_map/dynamic_slice | solution.py:479
  19.6 0.0 copy-done
  19.6 0.0 copy-done.1
  19.7 0.5 cosine_convert_fusion.phase_ref
  20.2 12.7 %prepare.1 = (bf16[33,192,192]{2,1,0:T(8,128)(2,1)}, bf16[33,256,256]{2,1,0:T(8,128)(2,1)}, bf16[33,432,256]{2,1,0:T(8,128)(2,1)}, f32[33,24,256]{2,1,0:T(8,128)}) custom-call(f32[1,18]{1,0:T(1,128)S(1)} %dynamic_slice.7.freq_ref, s32[1]{0:T(128)} %constant.46.clone.1.start_ref, s32[1,256]{1,0:T(1,128)S(1)} %constant_dynamic-slice_fusion.kq_ref, ...), custom_call_target="tpu_custom_call" | custom-call | tf_op jit(solution)/shard_map/prepare/pallas_call | solution.py:250
  32.8 4.8 %all-to-all-done.a_ref = bf16[8,96,896]{2,1,0:T(8,128)(2,1)S(1)} async-done(((bf16[8,96,896]{2,1,0:T(8,128)(2,1)}), bf16[8,96,896]{2,1,0:T(8,128)(2,1)S(1)}, u32[]{:S(2)}, u32[]{:S(2)}) %all-to-all-start) | async-done | bytes 1376288 | tf_op jit(solution)/shard_map/all_to_all | solution.py:470
  37.7 13.7 %linewidths.1 = f32[2,4,4,8,128]{4,3,2,1,0:T(8,128)} custom-call(bf16[8,96,896]{2,1,0:T(8,128)(2,1)S(1)} %all-to-all-done.a_ref, bf16[256,64]{1,0:T(8,128)(2,1)S(1)} %cosine_convert_fusion.phase_ref, bf16[33,192,192]{2,1,0:T(8,128)(2,1)} %get-tuple-element.8.refs_0_, bf16[33,256,256]{2,1,0:T(8,128)(2,1)} %get-tuple-element.9.refs_1_, ...), custom_call_target="tpu_custom_call" | custom-call | tf_op jit(solution)/shard_map/linewidths/pallas_call | solution.py:417
  51.3 4.0 %all-to-all-start.2 = ((f32[32,8,128]{2,1,0:T(8,128)}), f32[32,8,128]{2,1,0:T(8,128)S(1)}, u32[]{:S(2)}, u32[]{:S(2)}) async-start(f32[32,8,128]{2,1,0:T(8,128)} %bitcast.13), calls=%async_computation.2 | async-start | bytes 262144 | tf_op jit(solution)/shard_map/all_to_all | solution.py:492
  55.4 8.2 %all-to-all-done.2 = f32[32,8,128]{2,1,0:T(8,128)S(1)} async-done(((f32[32,8,128]{2,1,0:T(8,128)}), f32[32,8,128]{2,1,0:T(8,128)S(1)}, u32[]{:S(2)}, u32[]{:S(2)}) %all-to-all-start.2) | async-done | bytes 131104 | tf_op jit(solution)/shard_map/all_to_all | solution.py:492
  63.6 0.8 %finish.1 = (f32[24,32]{1,0:T(8,128)}, f32[4,36]{1,0:T(4,128)}) custom-call(s32[1]{0:T(128)} %bitcast.place_ref, f32[2,4,4,8,128]{4,3,2,1,0:T(8,128)S(1)} %bitcast.20), custom_call_target="tpu_custom_call" | custom-call | tf_op jit(solution)/shard_map/finish/pallas_call | solution.py:90
  (4 shorter events, 0.0 us)
Async XLA Ops:
  0.6 19.0 %copy-start = (s32[4,256]{1,0:T(4,128)S(1)}, s32[4,256]{1,0:T(4,128)}, u32[]{:S(2)}) copy-start(s32[4,256]{1,0:T(4,128)} %param.15) | copy-start | bytes 12292
  0.6 18.2 %copy-start.2 = (s32[64,3]{0,1:T(4,128)S(1)}, s32[64,3]{0,1:T(4,128)}, u32[]{:S(2)}) copy-start(s32[64,3]{0,1:T(4,128)} %param.17) | copy-start | bytes 2308
  0.7 19.0 %copy-start.1 = (f32[256,3]{0,1:T(4,128)S(1)}, f32[256,3]{0,1:T(4,128)}, u32[]{:S(2)}) copy-start(f32[256,3]{0,1:T(4,128)} %param.16) | copy-start | bytes 9220
  2.4 12.8 %all-to-all-start.1 = ((bf16[8,32,640]{2,1,0:T(8,128)(2,1)}), bf16[8,32,640]{2,1,0:T(8,128)(2,1)S(1)}, u32[]{:S(2)}, u32[]{:S(2)}) async-start(bf16[8,32,640]{2,1,0:T(8,128)(2,1)} %pack_points.1), calls=%async_computation.1 | async-start | bytes 655360 | tf_op jit(solution)/shard_map/all_to_all | solution.py:460
  15.2 22.4 %all-to-all-start = ((bf16[8,96,896]{2,1,0:T(8,128)(2,1)}), bf16[8,96,896]{2,1,0:T(8,128)(2,1)S(1)}, u32[]{:S(2)}, u32[]{:S(2)}) async-start(bf16[8,96,896]{2,1,0:T(8,128)(2,1)} %bitcast.2), calls=%async_computation | async-start | bytes 2752512 | tf_op jit(solution)/shard_map/all_to_all | solution.py:470
  51.3 12.2 %all-to-all-start.2 = ((f32[32,8,128]{2,1,0:T(8,128)}), f32[32,8,128]{2,1,0:T(8,128)S(1)}, u32[]{:S(2)}, u32[]{:S(2)}) async-start(f32[32,8,128]{2,1,0:T(8,128)} %bitcast.13), calls=%async_computation.2 | async-start | bytes 262144 | tf_op jit(solution)/shard_map/all_to_all | solution.py:492

commit v5 on v4

--- a/solution.py
+++ b/solution.py
@@ -14,7 +14,8 @@
 VMEM = pltpu.CompilerParams(vmem_limit_bytes=40 * 1024 * 1024)
 F32 = jnp.float32
 BF16 = jnp.bfloat16
-UNROLL = 3
+UNROLL = 11
+PREPARED = 3
 K_PER = 4
 
 
@@ -193,8 +194,8 @@
         keep_scr[...] = (iota(shape, 0) // n_bands == iota(shape, 1) % slots).astype(BF16)
 
     by_band = (iota((n_bands, slots * n_bands), 0) == iota((n_bands, slots * n_bands), 1) // slots).astype(BF16)
-    for step in range(UNROLL):
-        t = g * UNROLL + step
+    for step in range(PREPARED):
+        t = g * PREPARED + step
         first = jnp.minimum(t * slots, k_loc - slots)
         v_tiles = []
         blocks = []
@@ -229,9 +230,10 @@
                     both.append(jnp.exp(-(d * d)))
                 rows = slice(v * n_bands, (v + len(both)) * n_bands)
                 gauss_out[step, rows, cols] = jnp.concatenate(both, axis=0).astype(BF16)
-        zero = jnp.zeros((128, 128), F32)
-        bd_out[step, :128, :] = jnp.concatenate([blocks[0], zero], axis=1).astype(BF16)
-        bd_out[step, 128:, :] = jnp.concatenate([zero, blocks[1]], axis=1).astype(BF16)
+        for kg in range(2):
+            bd_out[step, kg] = blocks[kg].astype(BF16)
+            turned = jnp.concatenate([blocks[kg][120:], blocks[kg][:120]], axis=0)
+            bd_out[step, 2 + kg] = turned.astype(BF16)
         vl = jnp.concatenate(v_tiles, axis=1).astype(BF16)
         wt = lax.dot_general(vl, by_band, (((0,), (0,)), ((), ())), preferred_element_type=F32)
         wt = jnp.concatenate([wt[:used], wt[128 : 128 + used]], axis=0)
@@ -240,18 +242,22 @@
 
 def prepare(freq, start, kq, points, n_bands, n_v):
     k_loc = kq.shape[1]
-    steps = steps_of(k_loc)[1]
-    tiles = steps * UNROLL
+    tiles, steps = steps_of(k_loc)
+    tiles = max(tiles, steps * UNROLL)
+    steps = -(-tiles // PREPARED)
+    tiles = steps * PREPARED
     k_all = points.shape[0]
     wide = 2 * K_PER * n_bands
     smem = pl.BlockSpec(memory_space=pltpu.SMEM)
-    shapes = ((wide, wide), (256, 256), (n_v * n_bands, 256), (n_bands, 256))
+    shapes = ((wide, wide), (4, 128, 128), (n_v * n_bands, 256), (n_bands, 256))
     types = (BF16, BF16, BF16, F32)
     return pl.pallas_call(
         functools.partial(prepare_kernel, n_bands, n_v, k_loc),
         grid=(steps,),
         in_specs=[smem, smem, smem, pl.BlockSpec(memory_space=pltpu.VMEM)],
-        out_specs=[pl.BlockSpec((UNROLL,) + x, lambda g: (g, 0, 0)) for x in shapes],
+        out_specs=[
+            pl.BlockSpec((PREPARED,) + x, lambda g, n=len(x): (g,) + (0,) * n) for x in shapes
+        ],
         out_shape=[pltpu.HBM((tiles,) + x, t) for x, t in zip(shapes, types)],
         scratch_shapes=[
             pltpu.VMEM((k_all * n_bands, 128), F32),
@@ -265,17 +271,11 @@
 
 def swap_blocks(t_ref, n_bands, n_v):
     v_per = 128 // n_bands
-    lane = iota((n_bands, 128), 1)
-    inside = []
-    for d in range(v_per + K_PER - 1):
-        lo = n_bands * d % 128
-        hi = lo + n_bands
-        inside.append(
-            (lane >= lo) & (lane < hi) if hi <= 128 else (lane >= lo) | (lane < hi - 128)
-        )
-    halves = []
+    lane = iota((8, 128), 1)
+    low = [n_bands * d % 128 for d in range(v_per + K_PER - 1)]
+    from_low = [lane >= x for x in low]
+    halves = [[[] for _ in range(v_per)] for _ in range(2)]
     for kg in range(2):
-        column = []
         for first in range(0, n_v, v_per):
             vg = first // v_per
             rolled = []
@@ -283,26 +283,57 @@
                 row = (kg * K_PER + k) * n_bands
                 block = t_ref[row : row + n_bands, vg * 128 : (vg + 1) * 128]
                 rolled.append(pltpu.roll(block, n_bands * k, 1) if k else block)
-            for v in range(min(v_per, n_v - first)):
-                mix = rolled[0]
-                for k in range(1, K_PER):
-                    mix = jnp.where(inside[v + k], rolled[k], mix)
-                column.append(pltpu.roll(mix, 128 - n_bands * v, 1) if v else mix)
-        halves.append(jnp.concatenate(column, axis=0).astype(BF16))
-    return jnp.concatenate(halves, axis=1)
+            for x in range(min(v_per, n_v - first)):
+                order = sorted(range(K_PER), key=lambda k: low[x + k])
+                if low[x + order[-1]] + n_bands > 128:
+                    order.insert(0, order[-1])
+                for z in range(0, n_bands, 8):
+                    mix = rolled[order[0]][z : z + 8]
+                    for k in order[1:]:
+                        mix = jnp.where(from_low[x + k], rolled[k][z : z + 8], mix)
+                    halves[kg][x].append(mix)
+    return [
+        jnp.concatenate([jnp.concatenate(h[x], axis=0).astype(BF16) for h in halves], axis=1)
+        for x in range(min(v_per, n_v))
+    ]
+
+
+def turned_blocks(bd_ref, x, n_bands):
+    shift = n_bands * x % 128
+    which = shift % 16 // 8
+    shift -= 8 * which
+    halves = []
+    for kg in range(2):
+        if shift:
+            halves.append(
+                jnp.concatenate(
+                    [bd_ref[0, 2 * which + kg, 128 - shift :, :], bd_ref[0, 2 * which + kg, : 128 - shift, :]],
+                    axis=0,
+                )
+            )
+        else:
+            halves.append(bd_ref[0, 2 * which + kg])
+    zero = jnp.zeros((128, 128), BF16)
+    return jnp.concatenate(
+        [jnp.concatenate([halves[0], zero], axis=1), jnp.concatenate([zero, halves[1]], axis=1)], axis=0
+    )
 
 
 def tile_step(wt_ref, b_ref, t_new, t_old, bd_ref, gauss_ref, occ_ref, ph_scr, scale, n_bands, n_v):
     t_new[...] = jnp.dot(wt_ref[0], b_ref[0], preferred_element_type=F32)
-    left = swap_blocks(t_old, n_bands, n_v)
-    coupled = jnp.dot(left, bd_ref[0], preferred_element_type=F32)
+    v_per = 128 // n_bands
+    coupled = [
+        jnp.dot(left, turned_blocks(bd_ref, x, n_bands), preferred_element_type=F32)
+        for x, left in enumerate(swap_blocks(t_old, n_bands, n_v))
+    ]
     occ = occ_ref[0]
     el = None
     for v in range(0, n_v, 2):
         count = min(2, n_v - v)
         gauss = gauss_ref[0, v * n_bands : (v + count) * n_bands, :].astype(F32)
         for x in range(count):
-            c = coupled[(v + x) * n_bands : (v + x + 1) * n_bands]
+            at = (v + x) // v_per * n_bands
+            c = coupled[(v + x) % v_per][at : at + n_bands]
             strength = c * c * gauss[x * n_bands : (x + 1) * n_bands]
             el = strength if el is None else el + strength
             weighed = strength * occ
@@ -385,7 +416,8 @@
             tile_of(wt_ref, x), tile_of(b_scr, x), t_scr[x], t_scr[x - 1], tile_of(bd_ref, x - 1),
             tile_of(gauss_ref, x - 1), tile_of(occ_ref, x - 1), ph_scr, scale, n_bands, n_v,
         )
-    el_scr[pl.ds(g * 8, 8), :] = jnp.concatenate(el + [jnp.zeros((8 - 2 * unroll, 128), F32)], axis=0)
+    stride = el_scr.shape[0] // steps
+    el_scr[pl.ds(g * stride, 2 * unroll), :] = jnp.concatenate(el, axis=0)
 
     @pl.when(g == last)
     def _():
@@ -394,7 +426,7 @@
         sums = jnp.sum(ph_scr[...], axis=1)
         sums = jnp.concatenate([sums, jnp.zeros((128 - n_v, 128), F32)], axis=0).T
         sums = pltpu.roll(jnp.sum(sums, axis=0, keepdims=True) * ph_scale, used, 1)
-        groups = [el_scr[x * 8 : x * 8 + 2 * unroll, :] for x in range(steps)]
+        groups = [el_scr[x * stride : x * stride + 2 * unroll, :] for x in range(steps)]
         groups = jnp.concatenate(groups, axis=0) * el_scale
         lane = iota((n_rows, 128), 1)
         for d in range(n_ka * n_row):
@@ -427,7 +459,7 @@
             pltpu.VMEM((n_bands, depth, lanes), BF16),
             pltpu.VMEM((tiles, wide, lanes), BF16),
             pltpu.VMEM((n_v, 8, 128), F32),
-            pltpu.VMEM((steps * 8, 128), F32),
+            pltpu.VMEM((steps * -(-2 * UNROLL // 8) * 8, 128), F32),
         ]
         + [pltpu.VMEM((wide, lanes), F32)] * UNROLL,
         compiler_params=VMEM,

time: 64.8 us -> 62 us (0.957)
  Pallas kernels: 35.1 us -> 31.9 us
    pallas_call x1, Pallas kernels: 13.7 us -> 10.9 us  [linewidths(): pl.pallas_call(functools.partial(linewidth_kernel, n_bands, n_v, r, tiles...]
  transfers between devices with their start and end apart: 3 -> 3, of which waited for: 3 -> 3; matrix products, arithmetic and copies ran while one was open for 2% -> 2% of each run, Pallas kernels for 29% -> 30%
where the time goes in v5:
time: 62 us; the launch traced here: 61.6 us
  Pallas kernels  31.9 us (51%)
  waiting for transfers between devices  14.9 us (24%)
  starting transfers between devices  12.7 us (20%)
  local copies, waits for them, and re-layouts  0.8 us (1%)
  between operations  0.73 us (1%)
    pallas_call x1, Pallas kernels, prepare(): pl.pallas_call(functools.partial(prepare_kernel, n_bands, n_v, k_loc), gr...  12.2 us
    pallas_call x1, Pallas kernels, linewidths(): pl.pallas_call(functools.partial(linewidth_kernel, n_bands, n_v, r, tiles...  10.9 us
    all_to_all x1, waiting for transfers between devices, on_device(): lax.all_to_all(send.reshape((n_group * n_pb,) + send.shape[3:]), everywhe...  8.22 us
    pallas_call x1, Pallas kernels, rotate(): pl.pallas_call(functools.partial(rotate_kernel, n_modes, n_bands, v_parts...  6.24 us
    all_to_all x1, waiting for transfers between devices, on_device(): a = lax.all_to_all(rotated, plane, 0, 0, tiled=True)  5.32 us
    all_to_all x1, starting transfers between devices, on_device(): lax.all_to_all(points, plane, 0, 0, tiled=True).reshape(total_k, -1)  5.17 us
    all_to_all x1, starting transfers between devices, on_device(): lax.all_to_all(send.reshape((n_group * n_pb,) + send.shape[3:]), everywhe...  4 us
    all_to_all x1, starting transfers between devices, on_device(): a = lax.all_to_all(rotated, plane, 0, 0, tiled=True)  3.57 us
  transfers between devices with their start and end apart: 3, of which 3 were waited for; matrix products, arithmetic and copies ran while one was open for 2% of the time, Pallas kernels for 30%

profile of v5, /device:TPU:0, one launch (start us, length us, event | category | flops | bytes accessed | tf_op | source)
XLA Modules:
  0.0 61.6 jit_solution(4760732417633347795)
XLA Ops:
  0.6 0.0 copy-start
  0.6 0.0 copy-start.2
  0.7 0.0 copy-start.1
  0.7 1.8 %pack_points.1 = bf16[8,32,640]{2,1,0:T(8,128)(2,1)} custom-call(bf16[24,24,32]{2,1,0:T(8,128)(2,1)} %bitcast.21, f32[24,32]{1,0:T(8,128)} %bitcast.23, s32[1,32]{1,0:T(1,128)} %bitcast.27), custom_call_target="tpu_custom_call" | custom-call | tf_op jit(solution)/shard_map/pack_points/pallas_call | solution.py:54
  2.4 5.2 %all-to-all-start.1 = ((bf16[8,32,640]{2,1,0:T(8,128)(2,1)}), bf16[8,32,640]{2,1,0:T(8,128)(2,1)S(1)}, u32[]{:S(2)}, u32[]{:S(2)}) async-start(bf16[8,32,640]{2,1,0:T(8,128)(2,1)} %pack_points.1), calls=%async_computation.1 | async-start | bytes 655360 | tf_op jit(solution)/shard_map/all_to_all | solution.py:492
  7.6 6.2 %rotate_modes.1 = bf16[2,4,96,896]{3,2,1,0:T(8,128)(2,1)} custom-call(bf16[4,8,20736]{2,1,0:T(8,128)(2,1)} %coup_ref.1, bf16[36,4,36]{2,1,0:T(4,128)(2,1)} %bitcast.22), custom_call_target="tpu_custom_call" | custom-call | tf_op jit(solution)/shard_map/rotate_modes/pallas_call | solution.py:142
  13.8 1.4 %all-to-all-done.1 = bf16[8,32,640]{2,1,0:T(8,128)(2,1)S(1)} async-done(((bf16[8,32,640]{2,1,0:T(8,128)(2,1)}), bf16[8,32,640]{2,1,0:T(8,128)(2,1)S(1)}, u32[]{:S(2)}, u32[]{:S(2)}) %all-to-all-start.1) | async-done | bytes 327712 | tf_op jit(solution)/shard_map/all_to_all | solution.py:492
  15.2 3.6 %all-to-all-start = ((bf16[8,96,896]{2,1,0:T(8,128)(2,1)}), bf16[8,96,896]{2,1,0:T(8,128)(2,1)S(1)}, u32[]{:S(2)}, u32[]{:S(2)}) async-start(bf16[8,96,896]{2,1,0:T(8,128)(2,1)} %bitcast.2), calls=%async_computation | async-start | bytes 2752512 | tf_op jit(solution)/shard_map/all_to_all | solution.py:502
  18.8 0.0 copy-done.2
  18.8 0.8 %dynamic_slice.7.freq_ref = f32[1,18]{1,0:T(1,128)S(1)} dynamic-slice(f32[4,36]{1,0:T(4,128)} %param.11, s32[]{:T(128)S(6)} %select_n.16, s32[]{:T(128)S(6)} %select_n.17), dynamic_slice_sizes={1,18} | dynamic-slice | bytes 148 | tf_op jit(solution)/shard_map/dynamic_slice | solution.py:511
  19.6 0.0 copy-done
  19.6 0.0 copy-done.1
  19.7 0.5 cosine_convert_fusion.phase_ref
  20.2 12.2 %prepare.1 = (bf16[33,192,192]{2,1,0:T(8,128)(2,1)}, bf16[33,4,128,128]{3,2,1,0:T(8,128)(2,1)}, bf16[33,432,256]{2,1,0:T(8,128)(2,1)}, f32[33,24,256]{2,1,0:T(8,128)}) custom-call(f32[1,18]{1,0:T(1,128)S(1)} %dynamic_slice.7.freq_ref, s32[1]{0:T(128)} %constant.46.clone.1.start_ref, s32[1,256]{1,0:T(1,128)S(1)} %constant_dynamic-slice_fusion.kq_ref, ...), custom_call_target="tpu_custom_call" | custom-call | tf_op jit(solution)/shard_map/prepare/pallas_call | solution.py:254
  32.4 5.3 %all-to-all-done.a_ref = bf16[8,96,896]{2,1,0:T(8,128)(2,1)S(1)} async-done(((bf16[8,96,896]{2,1,0:T(8,128)(2,1)}), bf16[8,96,896]{2,1,0:T(8,128)(2,1)S(1)}, u32[]{:S(2)}, u32[]{:S(2)}) %all-to-all-start) | async-done | bytes 1376288 | tf_op jit(solution)/shard_map/all_to_all | solution.py:502
  37.7 10.9 %linewidths.1 = f32[2,4,4,8,128]{4,3,2,1,0:T(8,128)} custom-call(bf16[8,96,896]{2,1,0:T(8,128)(2,1)S(1)} %all-to-all-done.a_ref, bf16[256,64]{1,0:T(8,128)(2,1)S(1)} %cosine_convert_fusion.phase_ref, bf16[33,192,192]{2,1,0:T(8,128)(2,1)} %get-tuple-element.8.refs_0_, bf16[33,4,128,128]{3,2,1,0:T(8,128)(2,1)} %get-tuple-element.9.refs_1_, ...), custom_call_target="tpu_custom_call" | custom-call | tf_op jit(solution)/shard_map/linewidths/pallas_call | solution.py:449
  48.6 4.0 %all-to-all-start.2 = ((f32[32,8,128]{2,1,0:T(8,128)}), f32[32,8,128]{2,1,0:T(8,128)S(1)}, u32[]{:S(2)}, u32[]{:S(2)}) async-start(f32[32,8,128]{2,1,0:T(8,128)} %bitcast.13), calls=%async_computation.2 | async-start | bytes 262144 | tf_op jit(solution)/shard_map/all_to_all | solution.py:524
  52.6 8.2 %all-to-all-done.2 = f32[32,8,128]{2,1,0:T(8,128)S(1)} async-done(((f32[32,8,128]{2,1,0:T(8,128)}), f32[32,8,128]{2,1,0:T(8,128)S(1)}, u32[]{:S(2)}, u32[]{:S(2)}) %all-to-all-start.2) | async-done | bytes 131104 | tf_op jit(solution)/shard_map/all_to_all | solution.py:524
  60.8 0.8 %finish.1 = (f32[24,32]{1,0:T(8,128)}, f32[4,36]{1,0:T(4,128)}) custom-call(s32[1]{0:T(128)} %bitcast.place_ref, f32[2,4,4,8,128]{4,3,2,1,0:T(8,128)S(1)} %bitcast.20), custom_call_target="tpu_custom_call" | custom-call | tf_op jit(solution)/shard_map/finish/pallas_call | solution.py:91
  (4 shorter events, 0.0 us)
Async XLA Ops:
  0.6 19.0 %copy-start = (s32[4,256]{1,0:T(4,128)S(1)}, s32[4,256]{1,0:T(4,128)}, u32[]{:S(2)}) copy-start(s32[4,256]{1,0:T(4,128)} %param.15) | copy-start | bytes 12292
  0.6 18.2 %copy-start.2 = (s32[64,3]{0,1:T(4,128)S(1)}, s32[64,3]{0,1:T(4,128)}, u32[]{:S(2)}) copy-start(s32[64,3]{0,1:T(4,128)} %param.17) | copy-start | bytes 2308
  0.7 19.0 %copy-start.1 = (f32[256,3]{0,1:T(4,128)S(1)}, f32[256,3]{0,1:T(4,128)}, u32[]{:S(2)}) copy-start(f32[256,3]{0,1:T(4,128)} %param.16) | copy-start | bytes 9220
  2.4 12.8 %all-to-all-start.1 = ((bf16[8,32,640]{2,1,0:T(8,128)(2,1)}), bf16[8,32,640]{2,1,0:T(8,128)(2,1)S(1)}, u32[]{:S(2)}, u32[]{:S(2)}) async-start(bf16[8,32,640]{2,1,0:T(8,128)(2,1)} %pack_points.1), calls=%async_computation.1 | async-start | bytes 655360 | tf_op jit(solution)/shard_map/all_to_all | solution.py:492
  15.2 22.4 %all-to-all-start = ((bf16[8,96,896]{2,1,0:T(8,128)(2,1)}), bf16[8,96,896]{2,1,0:T(8,128)(2,1)S(1)}, u32[]{:S(2)}, u32[]{:S(2)}) async-start(bf16[8,96,896]{2,1,0:T(8,128)(2,1)} %bitcast.2), calls=%async_computation | async-start | bytes 2752512 | tf_op jit(solution)/shard_map/all_to_all | solution.py:502
  48.6 12.2 %all-to-all-start.2 = ((f32[32,8,128]{2,1,0:T(8,128)}), f32[32,8,128]{2,1,0:T(8,128)S(1)}, u32[]{:S(2)}, u32[]{:S(2)}) async-start(f32[32,8,128]{2,1,0:T(8,128)} %bitcast.13), calls=%async_computation.2 | async-start | bytes 262144 | tf_op jit(solution)/shard_map/all_to_all | solution.py:524

commit v6 on v5

--- a/solution.py
+++ b/solution.py
@@ -43,8 +43,9 @@
     packed = jnp.concatenate(rows, axis=0)
     packed = jnp.concatenate([packed, jnp.zeros((packed.shape[0], 128 - k_dev), F32)], axis=1)
     packed = packed.T[:k_dev].astype(BF16)
+    half = k_dev // 2
     for d in range(out_ref.shape[0]):
-        out_ref[d] = packed
+        out_ref[d] = packed[d % 2 * half : (d % 2 + 1) * half]
 
 
 def pack(eigvec, energies, window, copies):
@@ -56,7 +57,7 @@
         grid=(1,),
         in_specs=[pl.BlockSpec(x.shape, lambda g, n=x.ndim: (0,) * n) for x in args],
         out_specs=pl.BlockSpec(memory_space=pltpu.VMEM),
-        out_shape=pltpu.VMEM((copies, k_dev, wide), BF16),
+        out_shape=pltpu.VMEM((copies, k_dev // 2, wide), BF16),
         compiler_params=VMEM,
         name="pack_points",
     )(*[pltpu.with_memory_space_constraint(x, pltpu.HBM) for x in args])
@@ -489,7 +490,11 @@
     pb_pos = lax.axis_index("pb")
 
     points = pack(eigvec, energies, window, n_group)
-    points = lax.all_to_all(points, plane, 0, 0, tiled=True).reshape(total_k, -1)
+    mine = lax.all_to_all(points, plane, 0, 0, tiled=True)
+    other = lax.ppermute(mine, "row", [(i, i ^ 1) for i in range(n_row)])
+    odd = row_pos % 2 == 1
+    points = jnp.concatenate([jnp.where(odd, other, mine), jnp.where(odd, mine, other)], axis=1)
+    points = points.reshape(total_k, -1)
 
     pad = -coupling.shape[1] % 8
     if pad:

time: 62 us -> 61.3 us (0.989)
  waiting for transfers between devices: 14.9 us -> 13.1 us
  starting transfers between devices: 12.7 us -> 13.9 us
    all_to_all x1, waiting for transfers between devices: 1.4 us -> 0.01 us  [on_device(): mine = lax.all_to_all(points, plane, 0, 0, tiled=True)]
    all_to_all x1, starting transfers between devices: 3.57 us -> 4.19 us  [on_device(): a = lax.all_to_all(rotated, plane, 0, 0, tiled=True)]
  transfers between devices with their start and end apart: 3 -> 4, of which waited for: 3 -> 2; matrix products, arithmetic and copies ran while one was open for 2% -> 2% of each run, Pallas kernels for 30% -> 30%
where the time goes in v6:
time: 61.3 us; the launch traced here: 60.8 us
  Pallas kernels  31.7 us (52%)
  starting transfers between devices  13.9 us (23%)
  waiting for transfers between devices  13.1 us (21%)
  local copies, waits for them, and re-layouts  0.79 us (1%)
  between operations  0.76 us (1%)
    pallas_call x1, Pallas kernels, prepare(): pl.pallas_call(functools.partial(prepare_kernel, n_bands, n_v, k_loc), gr...  12 us
    pallas_call x1, Pallas kernels, linewidths(): pl.pallas_call(functools.partial(linewidth_kernel, n_bands, n_v, r, tiles...  10.9 us
    all_to_all x1, waiting for transfers between devices, on_device(): lax.all_to_all(send.reshape((n_group * n_pb,) + send.shape[3:]), everywhe...  8.22 us
    pallas_call x1, Pallas kernels, rotate(): pl.pallas_call(functools.partial(rotate_kernel, n_modes, n_bands, v_parts...  6.21 us
    all_to_all x1, starting transfers between devices, on_device(): mine = lax.all_to_all(points, plane, 0, 0, tiled=True)  5.17 us
    all_to_all x1, waiting for transfers between devices, on_device(): a = lax.all_to_all(rotated, plane, 0, 0, tiled=True)  4.85 us
    all_to_all x1, starting transfers between devices, on_device(): a = lax.all_to_all(rotated, plane, 0, 0, tiled=True)  4.19 us
    all_to_all x1, starting transfers between devices, on_device(): lax.all_to_all(send.reshape((n_group * n_pb,) + send.shape[3:]), everywhe...  4.01 us
  transfers between devices with their start and end apart: 4, of which 2 were waited for; matrix products, arithmetic and copies ran while one was open for 2% of the time, Pallas kernels for 30%

profile of v6, /device:TPU:0, one launch (start us, length us, event | category | flops | bytes accessed | tf_op | source)
XLA Modules:
  0.0 60.8 jit_solution(5597777358916623602)
XLA Ops:
  0.6 0.0 copy-start
  0.6 0.0 copy-start.2
  0.7 0.0 copy-start.1
  0.7 1.7 %pack_points.1 = bf16[8,16,640]{2,1,0:T(8,128)(2,1)} custom-call(bf16[24,24,32]{2,1,0:T(8,128)(2,1)} %bitcast.21, f32[24,32]{1,0:T(8,128)} %bitcast.23, s32[1,32]{1,0:T(1,128)} %bitcast.27), custom_call_target="tpu_custom_call" | custom-call | tf_op jit(solution)/shard_map/pack_points/pallas_call | solution.py:55
  2.4 5.2 %all-to-all-start.1 = ((bf16[8,16,640]{2,1,0:T(8,128)(2,1)}), bf16[8,16,640]{2,1,0:T(8,128)(2,1)S(1)}, u32[]{:S(2)}, u32[]{:S(2)}) async-start(bf16[8,16,640]{2,1,0:T(8,128)(2,1)} %pack_points.1), calls=%async_computation.1 | async-start | bytes 327680 | tf_op jit(solution)/shard_map/all_to_all | solution.py:493
  7.6 6.2 %rotate_modes.1 = bf16[2,4,96,896]{3,2,1,0:T(8,128)(2,1)} custom-call(bf16[4,8,20736]{2,1,0:T(8,128)(2,1)} %coup_ref.1, bf16[36,4,36]{2,1,0:T(4,128)(2,1)} %bitcast.22), custom_call_target="tpu_custom_call" | custom-call | tf_op jit(solution)/shard_map/rotate_modes/pallas_call | solution.py:143
  13.8 0.0 all-to-all-done.1
  13.8 4.2 %all-to-all-start = ((bf16[8,96,896]{2,1,0:T(8,128)(2,1)}), bf16[8,96,896]{2,1,0:T(8,128)(2,1)S(1)}, u32[]{:S(2)}, u32[]{:S(2)}) async-start(bf16[8,96,896]{2,1,0:T(8,128)(2,1)} %bitcast.2), calls=%async_computation | async-start | bytes 2752512 | tf_op jit(solution)/shard_map/all_to_all | solution.py:507
  18.0 0.0 copy-done.2
  18.0 0.0 copy-done.1
  18.0 0.6 collective-permute-start
  18.6 0.5 cosine_convert_fusion.phase_ref
  19.1 0.8 %dynamic_slice.7.freq_ref = f32[1,18]{1,0:T(1,128)S(1)} dynamic-slice(f32[4,36]{1,0:T(4,128)} %param.11, s32[]{:T(128)S(6)} %select_n.32, s32[]{:T(128)S(6)} %select_n.33), dynamic_slice_sizes={1,18} | dynamic-slice | bytes 148 | tf_op jit(solution)/shard_map/dynamic_slice | solution.py:516
  19.9 0.0 copy-done
  19.9 0.0 collective-permute-done
  20.0 12.0 %prepare.1 = (bf16[33,192,192]{2,1,0:T(8,128)(2,1)}, bf16[33,4,128,128]{3,2,1,0:T(8,128)(2,1)}, bf16[33,432,256]{2,1,0:T(8,128)(2,1)}, f32[33,24,256]{2,1,0:T(8,128)}) custom-call(f32[1,18]{1,0:T(1,128)S(1)} %dynamic_slice.7.freq_ref, s32[1]{0:T(128)} %constant.54.clone.1.start_ref, s32[1,256]{1,0:T(1,128)S(1)} %constant_dynamic-slice_fusion.kq_ref, ...), custom_call_target="tpu_custom_call" | custom-call | tf_op jit(solution)/shard_map/prepare/pallas_call | solution.py:255
  32.0 4.9 %all-to-all-done.a_ref = bf16[8,96,896]{2,1,0:T(8,128)(2,1)S(1)} async-done(((bf16[8,96,896]{2,1,0:T(8,128)(2,1)}), bf16[8,96,896]{2,1,0:T(8,128)(2,1)S(1)}, u32[]{:S(2)}, u32[]{:S(2)}) %all-to-all-start) | async-done | bytes 1376288 | tf_op jit(solution)/shard_map/all_to_all | solution.py:507
  36.9 10.9 %linewidths.1 = f32[2,4,4,8,128]{4,3,2,1,0:T(8,128)} custom-call(bf16[8,96,896]{2,1,0:T(8,128)(2,1)S(1)} %all-to-all-done.a_ref, bf16[256,64]{1,0:T(8,128)(2,1)S(1)} %cosine_convert_fusion.phase_ref, bf16[33,192,192]{2,1,0:T(8,128)(2,1)} %get-tuple-element.8.refs_0_, bf16[33,4,128,128]{3,2,1,0:T(8,128)(2,1)} %get-tuple-element.9.refs_1_, ...), custom_call_target="tpu_custom_call" | custom-call | tf_op jit(solution)/shard_map/linewidths/pallas_call | solution.py:450
  47.8 4.0 %all-to-all-start.2 = ((f32[32,8,128]{2,1,0:T(8,128)}), f32[32,8,128]{2,1,0:T(8,128)S(1)}, u32[]{:S(2)}, u32[]{:S(2)}) async-start(f32[32,8,128]{2,1,0:T(8,128)} %bitcast.13), calls=%async_computation.2 | async-start | bytes 262144 | tf_op jit(solution)/shard_map/all_to_all | solution.py:529
  51.8 8.2 %all-to-all-done.2 = f32[32,8,128]{2,1,0:T(8,128)S(1)} async-done(((f32[32,8,128]{2,1,0:T(8,128)}), f32[32,8,128]{2,1,0:T(8,128)S(1)}, u32[]{:S(2)}, u32[]{:S(2)}) %all-to-all-start.2) | async-done | bytes 131104 | tf_op jit(solution)/shard_map/all_to_all | solution.py:529
  60.1 0.8 %finish.1 = (f32[24,32]{1,0:T(8,128)}, f32[4,36]{1,0:T(4,128)}) custom-call(s32[1]{0:T(128)} %bitcast.place_ref, f32[2,4,4,8,128]{4,3,2,1,0:T(8,128)S(1)} %bitcast.20), custom_call_target="tpu_custom_call" | custom-call | tf_op jit(solution)/shard_map/finish/pallas_call | solution.py:92
  (6 shorter events, 0.1 us)
Async XLA Ops:
  0.6 19.3 %copy-start = (s32[4,256]{1,0:T(4,128)S(1)}, s32[4,256]{1,0:T(4,128)}, u32[]{:S(2)}) copy-start(s32[4,256]{1,0:T(4,128)} %param.15) | copy-start | bytes 12292
  0.6 17.3 %copy-start.2 = (s32[64,3]{0,1:T(4,128)S(1)}, s32[64,3]{0,1:T(4,128)}, u32[]{:S(2)}) copy-start(s32[64,3]{0,1:T(4,128)} %param.17) | copy-start | bytes 2308
  0.7 17.3 %copy-start.1 = (f32[256,3]{0,1:T(4,128)S(1)}, f32[256,3]{0,1:T(4,128)}, u32[]{:S(2)}) copy-start(f32[256,3]{0,1:T(4,128)} %param.16) | copy-start | bytes 9220
  2.4 11.4 %all-to-all-start.1 = ((bf16[8,16,640]{2,1,0:T(8,128)(2,1)}), bf16[8,16,640]{2,1,0:T(8,128)(2,1)S(1)}, u32[]{:S(2)}, u32[]{:S(2)}) async-start(bf16[8,16,640]{2,1,0:T(8,128)(2,1)} %pack_points.1), calls=%async_computation.1 | async-start | bytes 327680 | tf_op jit(solution)/shard_map/all_to_all | solution.py:493
  13.8 23.1 %all-to-all-start = ((bf16[8,96,896]{2,1,0:T(8,128)(2,1)}), bf16[8,96,896]{2,1,0:T(8,128)(2,1)S(1)}, u32[]{:S(2)}, u32[]{:S(2)}) async-start(bf16[8,96,896]{2,1,0:T(8,128)(2,1)} %bitcast.2), calls=%async_computation | async-start | bytes 2752512 | tf_op jit(solution)/shard_map/all_to_all | solution.py:507
  18.0 1.9 %collective-permute-start = (bf16[8,16,640]{2,1,0:T(8,128)(2,1)S(1)}, bf16[8,16,640]{2,1,0:T(8,128)(2,1)S(1)}, u32[]{:S(2)}, u32[]{:S(2)}) collective-permute-start(bf16[8,16,640]{2,1,0:T(8,128)(2,1)S(1)} %all-to-all-done.1), channel_id=1, source_target_pairs={{0,1},{1,0},{2,3},{3,2},{4,5},{5,4},{6,7},{7,6},{8,9},{9,8},{10,11... | collective-permute-start | bytes 491528 | tf_op jit(solution)/shard_map/ppermute | solution.py:494
  47.8 12.2 %all-to-all-start.2 = ((f32[32,8,128]{2,1,0:T(8,128)}), f32[32,8,128]{2,1,0:T(8,128)S(1)}, u32[]{:S(2)}, u32[]{:S(2)}) async-start(f32[32,8,128]{2,1,0:T(8,128)} %bitcast.13), calls=%async_computation.2 | async-start | bytes 262144 | tf_op jit(solution)/shard_map/all_to_all | solution.py:529

commit v7 on v6

--- a/solution.py
+++ b/solution.py
@@ -17,6 +17,7 @@
 UNROLL = 11
 PREPARED = 3
 K_PER = 4
+I_ROWS = 2
 
 
 def phase_rows(lattice, kpoint_rows):
@@ -119,18 +120,18 @@
     big = jnp.where(same, full, 0.0).astype(BF16)
     y = jnp.dot(big, x, preferred_element_type=F32)
     n_v = n_modes // v_parts
-    half_i = n_bands // 2
     wide = out_ref.shape[3]
+    sent = n_bands // I_ROWS * n_v * n_bands
     for part in range(v_parts):
         pieces = []
-        for i in range(half_i):
+        for i in range(I_ROWS):
             block = [
                 y[v * r : (v + 1) * r, x * n_bands : (x + 1) * n_bands]
-                for x in (i, i + half_i)
+                for x in range(i, n_bands, I_ROWS)
                 for v in range(part * n_v, (part + 1) * n_v)
             ]
-            if wide > 2 * n_v * n_bands:
-                block.append(jnp.zeros((r, wide - 2 * n_v * n_bands), F32))
+            if wide > sent:
+                block.append(jnp.zeros((r, wide - sent), F32))
             pieces.append(jnp.concatenate(block, axis=1))
         out_ref[part, 0] = jnp.concatenate(pieces, axis=0).astype(BF16)
 
@@ -138,8 +139,8 @@
 def rotate(coupling, rotation, n_bands, v_parts):
     q, r, width = coupling.shape
     n_modes = rotation.shape[1]
-    rows = n_bands // 2 * r
-    cols = -(-(2 * n_modes // v_parts * n_bands) // 128) * 128
+    rows = I_ROWS * r
+    cols = -(-(n_bands // I_ROWS * (n_modes // v_parts) * n_bands) // 128) * 128
     return pl.pallas_call(
         functools.partial(rotate_kernel, n_modes, n_bands, v_parts),
         grid=(q,),
@@ -358,7 +359,6 @@
     last = pl.num_programs(0) - 1
     steps = -(-(tiles + 1) // unroll)
     n_src = a_ref.shape[0]
-    half_i = n_bands // 2
     v_per = 128 // n_bands
     cols = n_v * n_bands
     slots = 2 * K_PER
@@ -369,12 +369,11 @@
 
     @pl.when(g == 0)
     def _():
-        for step in range(steps):
-            for which in range(4):
-                copy(which, step).start()
+        for which in range(4):
+            copy(which, 0).start()
         lane = iota((1, 128), 1)
         for s in range(0, n_src, 2):
-            for h in range(2):
+            for h in range(n_bands // I_ROWS):
                 for vg in range(-(-n_v // v_per)):
                     lo = h * cols + vg * v_per * n_bands
                     tile, off = lo // 128 * 128, lo % 128
@@ -387,9 +386,9 @@
                                 more = a_ref[x, :, tile + 128 : tile + 256].astype(F32)
                                 block = jnp.where(lane < 128 - off, block, pltpu.roll(more, 128 - off, 1))
                         both.append(block)
-                    for i in range(half_i):
+                    for i in range(I_ROWS):
                         here = slice(i * r, (i + 1) * r)
-                        a_scr[h * half_i + i, s * r : (s + 2) * r, vg * 128 : (vg + 1) * 128] = (
+                        a_scr[h * I_ROWS + i, s * r : (s + 2) * r, vg * 128 : (vg + 1) * 128] = (
                             jnp.concatenate([both[0][here], both[1][here]], axis=0).astype(BF16)
                         )
         for i in range(0, n_bands, 2):
@@ -405,6 +404,11 @@
 
     for which in range(4):
         copy(which, g).wait()
+
+    @pl.when(g < last)
+    def _():
+        for which in range(4):
+            copy(which, g + 1).start()
 
     def tile_of(ref, n):
         return ref.at[pl.ds(jnp.clip(unroll * g + n, 0, tiles - 1), 1)]

time: 61.3 us -> 61 us (level)
    pallas_call x1, Pallas kernels: 10.9 us -> 11.9 us  [linewidths(): pl.pallas_call(functools.partial(linewidth_kernel, n_bands, n_v, r, tiles...]
    pallas_call x1, Pallas kernels: 6.21 us -> 5.32 us  [rotate(): pl.pallas_call(functools.partial(rotate_kernel, n_modes, n_bands, v_parts...]
  transfers between devices with their start and end apart: 4 -> 4, of which waited for: 2 -> 3; matrix products, arithmetic and copies ran while one was open for 2% -> 2% of each run, Pallas kernels for 30% -> 29%
where the time goes in v7:
time: 61 us; the launch traced here: 60.6 us
  Pallas kernels  31.8 us (52%)
  starting transfers between devices  13.4 us (22%)
  waiting for transfers between devices  13.3 us (22%)
  local copies, waits for them, and re-layouts  0.79 us (1%)
  between operations  0.76 us (1%)
    pallas_call x1, Pallas kernels, prepare(): pl.pallas_call(functools.partial(prepare_kernel, n_bands, n_v, k_loc), gr...  12.1 us
    pallas_call x1, Pallas kernels, linewidths(): pl.pallas_call(functools.partial(linewidth_kernel, n_bands, n_v, r, tiles...  11.9 us
    all_to_all x1, waiting for transfers between devices, on_device(): lax.all_to_all(send.reshape((n_group * n_pb,) + send.shape[3:]), everywhe...  8.22 us
    pallas_call x1, Pallas kernels, rotate(): pl.pallas_call(functools.partial(rotate_kernel, n_modes, n_bands, v_parts...  5.32 us
    all_to_all x1, starting transfers between devices, on_device(): mine = lax.all_to_all(points, plane, 0, 0, tiled=True)  5.17 us
    all_to_all x1, waiting for transfers between devices, on_device(): a = lax.all_to_all(rotated, plane, 0, 0, tiled=True)  4.47 us
    all_to_all x1, starting transfers between devices, on_device(): lax.all_to_all(send.reshape((n_group * n_pb,) + send.shape[3:]), everywhe...  4 us
    all_to_all x1, starting transfers between devices, on_device(): a = lax.all_to_all(rotated, plane, 0, 0, tiled=True)  3.63 us
  transfers between devices with their start and end apart: 4, of which 3 were waited for; matrix products, arithmetic and copies ran while one was open for 2% of the time, Pallas kernels for 29%

profile of v7, /device:TPU:0, one launch (start us, length us, event | category | flops | bytes accessed | tf_op | source)
XLA Modules:
  0.0 60.6 jit_solution(2758479115865226482)
XLA Ops:
  0.6 0.0 copy-start
  0.6 0.0 copy-start.2
  0.7 0.0 copy-start.1
  0.7 1.7 %pack_points.1 = bf16[8,16,640]{2,1,0:T(8,128)(2,1)} custom-call(bf16[24,24,32]{2,1,0:T(8,128)(2,1)} %bitcast.21, f32[24,32]{1,0:T(8,128)} %bitcast.23, s32[1,32]{1,0:T(1,128)} %bitcast.27), custom_call_target="tpu_custom_call" | custom-call | tf_op jit(solution)/shard_map/pack_points/pallas_call | solution.py:56
  2.4 5.2 %all-to-all-start.1 = ((bf16[8,16,640]{2,1,0:T(8,128)(2,1)}), bf16[8,16,640]{2,1,0:T(8,128)(2,1)S(1)}, u32[]{:S(2)}, u32[]{:S(2)}) async-start(bf16[8,16,640]{2,1,0:T(8,128)(2,1)} %pack_points.1), calls=%async_computation.1 | async-start | bytes 327680 | tf_op jit(solution)/shard_map/all_to_all | solution.py:497
  7.6 5.3 %rotate_modes.1 = bf16[2,4,16,5248]{3,2,1,0:T(8,128)(2,1)} custom-call(bf16[4,8,20736]{2,1,0:T(8,128)(2,1)} %coup_ref.1, bf16[36,4,36]{2,1,0:T(4,128)(2,1)} %bitcast.22), custom_call_target="tpu_custom_call" | custom-call | tf_op jit(solution)/shard_map/rotate_modes/pallas_call | solution.py:144
  12.9 0.6 all-to-all-done.1
  13.4 3.6 %all-to-all-start = ((bf16[8,16,5248]{2,1,0:T(8,128)(2,1)}), bf16[8,16,5248]{2,1,0:T(8,128)(2,1)S(1)}, u32[]{:S(2)}, u32[]{:S(2)}) async-start(bf16[8,16,5248]{2,1,0:T(8,128)(2,1)} %bitcast.2), calls=%async_computation | async-start | bytes 2686976 | tf_op jit(solution)/shard_map/all_to_all | solution.py:511
  17.1 0.0 copy-done.2
  17.1 0.0 copy-done.1
  17.1 0.6 collective-permute-start
  17.7 0.5 cosine_convert_fusion.phase_ref
  18.2 0.8 %dynamic_slice.7.freq_ref = f32[1,18]{1,0:T(1,128)S(1)} dynamic-slice(f32[4,36]{1,0:T(4,128)} %param.11, s32[]{:T(128)S(6)} %select_n.32, s32[]{:T(128)S(6)} %select_n.33), dynamic_slice_sizes={1,18} | dynamic-slice | bytes 148 | tf_op jit(solution)/shard_map/dynamic_slice | solution.py:520
  19.0 0.0 copy-done
  19.0 0.0 collective-permute-done
  19.1 12.1 %prepare.1 = (bf16[33,192,192]{2,1,0:T(8,128)(2,1)}, bf16[33,4,128,128]{3,2,1,0:T(8,128)(2,1)}, bf16[33,432,256]{2,1,0:T(8,128)(2,1)}, f32[33,24,256]{2,1,0:T(8,128)}) custom-call(f32[1,18]{1,0:T(1,128)S(1)} %dynamic_slice.7.freq_ref, s32[1]{0:T(128)} %constant.54.clone.1.start_ref, s32[1,256]{1,0:T(1,128)S(1)} %constant_dynamic-slice_fusion.kq_ref, ...), custom_call_target="tpu_custom_call" | custom-call | tf_op jit(solution)/shard_map/prepare/pallas_call | solution.py:256
  31.2 4.5 %all-to-all-done.a_ref = bf16[8,16,5248]{2,1,0:T(8,128)(2,1)S(1)} async-done(((bf16[8,16,5248]{2,1,0:T(8,128)(2,1)}), bf16[8,16,5248]{2,1,0:T(8,128)(2,1)S(1)}, u32[]{:S(2)}, u32[]{:S(2)}) %all-to-all-start) | async-done | bytes 1343520 | tf_op jit(solution)/shard_map/all_to_all | solution.py:511
  35.6 11.9 %linewidths.1 = f32[2,4,4,8,128]{4,3,2,1,0:T(8,128)} custom-call(bf16[8,16,5248]{2,1,0:T(8,128)(2,1)S(1)} %all-to-all-done.a_ref, bf16[256,64]{1,0:T(8,128)(2,1)S(1)} %cosine_convert_fusion.phase_ref, bf16[33,192,192]{2,1,0:T(8,128)(2,1)} %get-tuple-element.8.refs_0_, bf16[33,4,128,128]{3,2,1,0:T(8,128)(2,1)} %get-tuple-element.9.refs_1_, ...), custom_call_target="tpu_custom_call" | custom-call | tf_op jit(solution)/shard_map/linewidths/pallas_call | solution.py:454
  47.5 4.0 %all-to-all-start.2 = ((f32[32,8,128]{2,1,0:T(8,128)}), f32[32,8,128]{2,1,0:T(8,128)S(1)}, u32[]{:S(2)}, u32[]{:S(2)}) async-start(f32[32,8,128]{2,1,0:T(8,128)} %bitcast.13), calls=%async_computation.2 | async-start | bytes 262144 | tf_op jit(solution)/shard_map/all_to_all | solution.py:533
  51.6 8.2 %all-to-all-done.2 = f32[32,8,128]{2,1,0:T(8,128)S(1)} async-done(((f32[32,8,128]{2,1,0:T(8,128)}), f32[32,8,128]{2,1,0:T(8,128)S(1)}, u32[]{:S(2)}, u32[]{:S(2)}) %all-to-all-start.2) | async-done | bytes 131104 | tf_op jit(solution)/shard_map/all_to_all | solution.py:533
  59.8 0.8 %finish.1 = (f32[24,32]{1,0:T(8,128)}, f32[4,36]{1,0:T(4,128)}) custom-call(s32[1]{0:T(128)} %bitcast.place_ref, f32[2,4,4,8,128]{4,3,2,1,0:T(8,128)S(1)} %bitcast.20), custom_call_target="tpu_custom_call" | custom-call | tf_op jit(solution)/shard_map/finish/pallas_call | solution.py:93
  (6 shorter events, 0.1 us)
Async XLA Ops:
  0.6 18.4 %copy-start = (s32[4,256]{1,0:T(4,128)S(1)}, s32[4,256]{1,0:T(4,128)}, u32[]{:S(2)}) copy-start(s32[4,256]{1,0:T(4,128)} %param.15) | copy-start | bytes 12292
  0.6 16.4 %copy-start.2 = (s32[64,3]{0,1:T(4,128)S(1)}, s32[64,3]{0,1:T(4,128)}, u32[]{:S(2)}) copy-start(s32[64,3]{0,1:T(4,128)} %param.17) | copy-start | bytes 2308
  0.7 16.4 %copy-start.1 = (f32[256,3]{0,1:T(4,128)S(1)}, f32[256,3]{0,1:T(4,128)}, u32[]{:S(2)}) copy-start(f32[256,3]{0,1:T(4,128)} %param.16) | copy-start | bytes 9220
  2.4 11.1 %all-to-all-start.1 = ((bf16[8,16,640]{2,1,0:T(8,128)(2,1)}), bf16[8,16,640]{2,1,0:T(8,128)(2,1)S(1)}, u32[]{:S(2)}, u32[]{:S(2)}) async-start(bf16[8,16,640]{2,1,0:T(8,128)(2,1)} %pack_points.1), calls=%async_computation.1 | async-start | bytes 327680 | tf_op jit(solution)/shard_map/all_to_all | solution.py:497
  13.4 22.2 %all-to-all-start = ((bf16[8,16,5248]{2,1,0:T(8,128)(2,1)}), bf16[8,16,5248]{2,1,0:T(8,128)(2,1)S(1)}, u32[]{:S(2)}, u32[]{:S(2)}) async-start(bf16[8,16,5248]{2,1,0:T(8,128)(2,1)} %bitcast.2), calls=%async_computation | async-start | bytes 2686976 | tf_op jit(solution)/shard_map/all_to_all | solution.py:511
  17.1 1.9 %collective-permute-start = (bf16[8,16,640]{2,1,0:T(8,128)(2,1)S(1)}, bf16[8,16,640]{2,1,0:T(8,128)(2,1)S(1)}, u32[]{:S(2)}, u32[]{:S(2)}) collective-permute-start(bf16[8,16,640]{2,1,0:T(8,128)(2,1)S(1)} %all-to-all-done.1), channel_id=1, source_target_pairs={{0,1},{1,0},{2,3},{3,2},{4,5},{5,4},{6,7},{7,6},{8,9},{9,8},{10,11... | collective-permute-start | bytes 491528 | tf_op jit(solution)/shard_map/ppermute | solution.py:498
  47.5 12.2 %all-to-all-start.2 = ((f32[32,8,128]{2,1,0:T(8,128)}), f32[32,8,128]{2,1,0:T(8,128)S(1)}, u32[]{:S(2)}, u32[]{:S(2)}) async-start(f32[32,8,128]{2,1,0:T(8,128)} %bitcast.13), calls=%async_computation.2 | async-start | bytes 262144 | tf_op jit(solution)/shard_map/all_to_all | solution.py:533
